TPU v7x, 256 devices: a whole 4x4x8 slice. The times are simulated.
256 devices in a mesh: seq: 64 (over y_lo, x, z), head: 4 (over y_hi, core).
Axes of the slice: x: 4, y: 4 (y_hi: 2, y_lo: 2; y = y_hi * 2 + y_lo), z: 8, core: 2. Of those that a mesh axis runs over, the one named last changes fastest.
Arguments:
- query_rows: bfloat16 [32768, 2560], P('seq', 'head'), may hold values from -8 to 8
- key_rows: bfloat16 [32768, 2560], P('seq', 'head'), may hold values from -8 to 8
- value_rows: bfloat16 [32768, 2560], P('seq', 'head'), may hold values from -3 to 3
- out_weight: bfloat16 [2560, 2560], P('head'), may hold values from -0.125 to 0.125
- cotangent: bfloat16 [32768, 2560], P('seq', 'head'), may hold values from -6 to 6
- offsets: int32 [2, 32], P(None, 'head'), may hold values from 0 to 63, as said below
Outputs:
- attended: bfloat16 [32768, 2560], P('seq', 'head')
- grad_query: bfloat16 [32768, 2560], P('seq', 'head')
- grad_key: bfloat16 [32768, 2560], P('seq', 'head')
- grad_value: bfloat16 [32768, 2560], P('seq', 'head')
Inputs may be any that keep to these rules, and one draw needn't show every extreme that they name: `offsets`: row 0 holds each head's offset at the middle level, below 4; row 1 the offset at the sequence-wide level, below 64.
All inputs are finite; a program needn't handle non-finite values.
Results may differ from a plain program's by a relative error of at most 0.025.
Values may be sent and summed in bfloat16 or wider, within the bound.
No kernel may reach another device: no remote copies, remote signals or barrier semaphores. Data moves between devices by JAX's collectives and lax.ppermute only.
A program may use at most 128 MiB of HBM per device.

v0:
```python
import math

import jax
import jax.numpy as jnp
from jax import lax
from jax.sharding import PartitionSpec as P

NEAR_RATE = 4


def passed_along(block, axis, distance):
    devices = range(lax.axis_size(axis))
    route = [(i - distance, i) for i in devices if i - distance in devices]
    return lax.ppermute(block, axis, route)


def choose_rows(matrix, dilation, pick_mask):
    row_count, head_count, head_width = matrix.shape
    grid_view = matrix.reshape(row_count // dilation, dilation, head_count, head_width)
    return jnp.einsum(
        "arhd,rh->ahd",
        grid_view,
        pick_mask.astype(matrix.dtype),
        preferred_element_type=jnp.float32,
    ).astype(matrix.dtype)


def choose_stats(stats, dilation, pick_mask):
    grid_view = stats.reshape(stats.shape[0] // dilation, dilation, stats.shape[1])
    return jnp.sum(jnp.where(pick_mask[None], grid_view, 0.0), axis=1)


def spread_rows(level_out, dilation, pick_mask):
    widened = jnp.where(pick_mask[None, :, :, None], level_out[:, None], 0.0)
    return widened.reshape(level_out.shape[0] * dilation, level_out.shape[1], level_out.shape[2])


def spread_stats(stats, dilation, pick_mask, filler):
    widened = jnp.where(pick_mask[None], stats[:, None], filler)
    return widened.reshape(stats.shape[0] * dilation, stats.shape[1])


def level_scores(queries, keys, allowed, score_scale):
    raw_scores = (
        jnp.einsum("ahd,bhd->hab", queries, keys, preferred_element_type=jnp.float32) * score_scale
    )
    return jnp.where(allowed[None], raw_scores, -jnp.inf)


def row_lognorm(scores):
    row_max = jnp.max(scores, axis=2, keepdims=True)
    exp_total = jnp.sum(jnp.exp(scores - row_max), axis=2)
    return (row_max[..., 0] + jnp.log(exp_total)).T


def level_probs(scores, log_rows):
    weights = jnp.exp(scores - log_rows.T[:, :, None])
    return (weights, weights.astype(jnp.bfloat16))


def level_grads(queries, keys, values, grads_out, weights, rounded, deltas, score_scale):
    grad_weights = jnp.einsum("ahd,bhd->hab", grads_out, values, preferred_element_type=jnp.float32)
    grad_scores = (weights * (grad_weights - deltas.T[:, :, None]) * score_scale).astype(
        jnp.bfloat16
    )
    query_grad = jnp.einsum("hab,bhd->ahd", grad_scores, keys, preferred_element_type=jnp.float32)
    key_grad = jnp.einsum("hab,ahd->bhd", grad_scores, queries, preferred_element_type=jnp.float32)
    value_grad = jnp.einsum("hab,ahd->bhd", rounded, grads_out, preferred_element_type=jnp.float32)
    return (query_grad, key_grad, value_grad)


def on_device(query_rows, key_rows, value_rows, out_weight, cotangent, offsets):
    tokens = query_rows.shape[0]
    head_count = offsets.shape[1]
    row_width = query_rows.shape[1]
    head_width = row_width // head_count
    score_scale = 1.0 / math.sqrt(head_width)
    far_rate = lax.axis_size("seq")
    near_rate = NEAR_RATE
    seq_index = lax.axis_index("seq")
    group_pos = seq_index % near_rate
    near_count = tokens // near_rate
    far_count = tokens // far_rate
    near_mask = jnp.arange(near_rate)[:, None] == offsets[0][None, :]
    far_mask = jnp.arange(far_rate)[:, None] == offsets[1][None, :]

    def split_heads(matrix):
        return matrix.reshape(matrix.shape[0], head_count, head_width)

    queries = split_heads(query_rows)
    keys = split_heads(key_rows)
    values = split_heads(value_rows)
    near_queries = choose_rows(queries, near_rate, near_mask)
    near_own_keys = choose_rows(keys, near_rate, near_mask).reshape(near_count, row_width)
    near_own_values = choose_rows(values, near_rate, near_mask).reshape(near_count, row_width)
    far_queries = choose_rows(queries, far_rate, far_mask)
    far_own_keys = choose_rows(keys, far_rate, far_mask)
    far_own_values = choose_rows(values, far_rate, far_mask)
    key_slots = []
    value_slots = []
    for distance in range(near_rate - 1, 0, -1):
        moved_keys, moved_values = passed_along((near_own_keys, near_own_values), "seq", distance)
        key_slots.append(moved_keys)
        value_slots.append(moved_values)
    key_slots.append(near_own_keys)
    value_slots.append(near_own_values)
    near_keys = split_heads(jnp.concatenate(key_slots, axis=0))
    near_values = split_heads(jnp.concatenate(value_slots, axis=0))
    far_keys, far_values = (
        lax.all_gather(far_own_keys.reshape(far_count, row_width), "seq", axis=0, tiled=True),
        lax.all_gather(far_own_values.reshape(far_count, row_width), "seq", axis=0, tiled=True),
    )
    far_keys = split_heads(far_keys)
    far_values = split_heads(far_values)
    local_allowed = jnp.arange(tokens)[:, None] >= jnp.arange(tokens)[None, :]
    slot_index = (group_pos - (near_rate - 1)) * near_count + jnp.arange(near_rate * near_count)
    near_index = group_pos * near_count + jnp.arange(near_count)
    near_allowed = (slot_index[None, :] <= near_index[:, None]) & (slot_index[None, :] >= 0)
    far_index = seq_index * far_count + jnp.arange(far_count)
    far_allowed = jnp.arange(tokens)[None, :] <= far_index[:, None]
    local_scores = level_scores(queries, keys, local_allowed, score_scale)
    near_scores = level_scores(near_queries, near_keys, near_allowed, score_scale)
    far_scores = level_scores(far_queries, far_keys, far_allowed, score_scale)
    log_total = jnp.logaddexp(
        row_lognorm(local_scores),
        spread_stats(row_lognorm(near_scores), near_rate, near_mask, -jnp.inf),
    )
    log_total = jnp.logaddexp(
        log_total, spread_stats(row_lognorm(far_scores), far_rate, far_mask, -jnp.inf)
    )
    near_log = choose_stats(log_total, near_rate, near_mask)
    far_log = choose_stats(log_total, far_rate, far_mask)
    local_weights, local_rounded = level_probs(local_scores, log_total)
    near_weights, near_rounded = level_probs(near_scores, near_log)
    far_weights, far_rounded = level_probs(far_scores, far_log)
    local_out = jnp.einsum(
        "hab,bhd->ahd", local_rounded, values, preferred_element_type=jnp.float32
    )
    near_out = jnp.einsum(
        "hab,bhd->ahd", near_rounded, near_values, preferred_element_type=jnp.float32
    )
    far_out = jnp.einsum(
        "hab,bhd->ahd", far_rounded, far_values, preferred_element_type=jnp.float32
    )
    attended_sum = (
        local_out
        + spread_rows(near_out, near_rate, near_mask)
        + spread_rows(far_out, far_rate, far_mask)
    )
    attended = attended_sum.astype(jnp.bfloat16).reshape(tokens, row_width)
    grad_sum = lax.dot_general(
        lax.all_gather(cotangent, "head", axis=1, tiled=True),
        out_weight,
        (((1,), (1,)), ((), ())),
        preferred_element_type=jnp.float32,
    )
    grads_out = split_heads(grad_sum.astype(jnp.bfloat16))
    deltas = jnp.sum(
        grads_out.astype(jnp.float32) * split_heads(attended).astype(jnp.float32), axis=2
    )
    near_grads_out = choose_rows(grads_out, near_rate, near_mask)
    far_grads_out = choose_rows(grads_out, far_rate, far_mask)
    near_deltas = choose_stats(deltas, near_rate, near_mask)
    far_deltas = choose_stats(deltas, far_rate, far_mask)
    local_dquery, local_dkey, local_dvalue = level_grads(
        queries, keys, values, grads_out, local_weights, local_rounded, deltas, score_scale
    )
    near_dquery, near_dkey, near_dvalue = level_grads(
        near_queries,
        near_keys,
        near_values,
        near_grads_out,
        near_weights,
        near_rounded,
        near_deltas,
        score_scale,
    )
    far_dquery, far_dkey, far_dvalue = level_grads(
        far_queries,
        far_keys,
        far_values,
        far_grads_out,
        far_weights,
        far_rounded,
        far_deltas,
        score_scale,
    )
    key_parts = near_dkey.reshape(near_rate, near_count, row_width)
    value_parts = near_dvalue.reshape(near_rate, near_count, row_width)
    near_key_total = key_parts[near_rate - 1]
    near_value_total = value_parts[near_rate - 1]
    for distance in range(1, near_rate):
        came_keys, came_values = passed_along(
            (key_parts[near_rate - 1 - distance], value_parts[near_rate - 1 - distance]),
            "seq",
            -distance,
        )
        near_key_total = near_key_total + came_keys
        near_value_total = near_value_total + came_values
    far_key_total, far_value_total = (
        lax.psum_scatter(
            far_dkey.reshape(tokens, row_width), "seq", scatter_dimension=0, tiled=True
        ),
        lax.psum_scatter(
            far_dvalue.reshape(tokens, row_width), "seq", scatter_dimension=0, tiled=True
        ),
    )
    query_total = (
        local_dquery
        + spread_rows(near_dquery, near_rate, near_mask)
        + spread_rows(far_dquery, far_rate, far_mask)
    )
    key_total = (
        local_dkey
        + spread_rows(split_heads(near_key_total), near_rate, near_mask)
        + spread_rows(split_heads(far_key_total), far_rate, far_mask)
    )
    value_total = (
        local_dvalue
        + spread_rows(split_heads(near_value_total), near_rate, near_mask)
        + spread_rows(split_heads(far_value_total), far_rate, far_mask)
    )
    grad_query = query_total.astype(jnp.bfloat16).reshape(tokens, row_width)
    grad_key = key_total.astype(jnp.bfloat16).reshape(tokens, row_width)
    grad_value = value_total.astype(jnp.bfloat16).reshape(tokens, row_width)
    return (attended, grad_query, grad_key, grad_value)


def solution(mesh):
    return jax.shard_map(
        on_device,
        mesh=mesh,
        in_specs=(
            P("seq", "head"),
            P("seq", "head"),
            P("seq", "head"),
            P("head", None),
            P("seq", "head"),
            P(None, "head"),
        ),
        out_specs=(P("seq", "head"), P("seq", "head"), P("seq", "head"), P("seq", "head")),
        check_vma=False,
    )
```

profile of v0, /device:TPU:8, one launch (start us, length us, event | category | flops | bytes accessed | tf_op | source)
XLA Modules:
  0.0 1116.1 jit_solution(2572958287425633693)
XLA Ops:
  9.5 3.0 reshape_reshape.27
  14.1 171.4 %all_gather.9 = bf16[512,640]{1,0:T(8,128)(2,1)} all-gather(bf16[8,640]{1,0:T(8,128)(2,1)S(1)} %reshape.329), channel_id=1, replica_groups=mesh['seq'=64,'head'=4] {'seq'}, dimensions={0}, use_global_device_ids=true | all-gather | bytes 665600 | tf_op jit(solution)/shard_map/all_gather | solution.py:110
  185.5 3.0 reshape_reshape.25
  188.5 2.9 reshape_reshape.24
  191.4 3.0 reshape_reshape.26
  194.4 2.2 copy.58
  196.5 2.2 copy.59
  198.7 2.9 reshape_reshape.28
  201.7 3.0 reshape_reshape.29
  204.6 2.2 copy.65
  217.1 165.8 %all_gather.10 = bf16[512,640]{1,0:T(8,128)(2,1)} all-gather(bf16[8,640]{1,0:T(8,128)(2,1)S(1)} %reshape.334), channel_id=1, replica_groups=mesh['seq'=64,'head'=4] {'seq'}, dimensions={0}, use_global_device_ids=true | all-gather | bytes 665600 | tf_op jit(solution)/shard_map/all_gather | solution.py:111
  382.9 2.2 copy.72
  387.9 2.8 fusion.1
  390.7 3.2 copy-done.2
  395.7 4.8 convolution_convert_fusion
  400.5 2.3 reshape_reshape.30
  402.8 4.4 multiply_reduce_fusion
  412.3 2.4 collective-permute-start.2
  422.5 6.0 collective-permute-start.5
  434.8 5.0 collective-permute-start.10
  439.7 7.0 collective-permute-start.11
  446.8 3.5 collective-permute-start.9
  459.4 7.9 multiply_reduce_fusion.4
  475.8 3.4 collective-permute-start.6
  479.2 7.1 collective-permute-start.7
  486.4 6.7 multiply_convert_fusion
  499.6 5.8 collective-permute-start.8
  505.4 3.8 fusion.14
  514.8 3.1 collective-permute-done.8
  521.2 566.3 %all-reduce.5.cloned.1.call-done = (f32[512,640]{0,1:T(8,128)}, f32[512,640]{0,1:T(8,128)}) async-done(((f32[512,640]{0,1:T(8,128)}, f32[512,640]{0,1:T(8,128)}), (f32[512,640]{0,1:T(8,128)}, f32[512,640]{0,1:T(8,128)})) %all-reduce.5.cloned.1.call-update) | async-done | bytes 2621456
  1091.3 6.6 fusion.12
  1101.4 5.5 fusion.11
  (196 shorter events, 79.1 us)
Async XLA Ops:
  7.2 388.5 %copy-start = (bf16[640,2560]{1,0:T(8,128)(2,1)S(1)}, bf16[640,2560]{1,0:T(8,128)(2,1)}, u32[]{:S(2)}) copy-start(bf16[640,2560]{1,0:T(8,128)(2,1)} %param.9) | copy-start | bytes 9830404
  7.2 388.5 %all-gather.2.cloned.1.call-start = ((), (), s32[]{:S(2)}) async-start(), calls=%async_computation | async-start | bytes 3276800 | tf_op jit(solution)/shard_map/all_gather | solution.py:152
  7.9 1079.6 %all-reduce.5.cloned.1.call-start = ((), (), s32[]{:S(2)}) async-start(), calls=%async_computation.1 | async-start | bytes 5242880
  402.8 16.8 %copy-start.8 = (bf16[512,640]{1,0:T(8,128)(2,1)S(1)}, bf16[512,640]{1,0:T(8,128)(2,1)}, u32[]{:S(2)}) copy-start(bf16[512,640]{1,0:T(8,128)(2,1)} %convolution_convert_fusion) | copy-start | bytes 1966084
  408.4 21.5 %copy-start.22 = (bf16[8,128,80]{1,2,0:T(8,128)(2,1)}, bf16[8,128,80]{1,2,0:T(8,128)(2,1)S(1)}, u32[]{:S(2)}) copy-start(bf16[8,128,80]{1,2,0:T(8,128)(2,1)S(1)} %copy.109) | copy-start | bytes 491524
  408.4 14.1 %collective-permute-start = (bf16[128,640]{0,1:T(8,128)(2,1)S(1)}, bf16[128,640]{0,1:T(8,128)(2,1)S(1)}, u32[]{:S(2)}, u32[]{:S(2)}) collective-permute-start(bf16[128,640]{0,1:T(8,128)(2,1)S(1)} %bitcast.280), channel_id=1, source_target_pairs={{0,12},{4,16},{8,20},{12,24},{16,28},{20,32},{24,36},{28,40},{32,4... | collective-permute-start | bytes 491528 | tf_op jit(solution)/shard_map/ppermute | solution.py:14
  410.3 18.2 %collective-permute-start.1 = (bf16[128,640]{0,1:T(8,128)(2,1)S(1)}, bf16[128,640]{0,1:T(8,128)(2,1)S(1)}, u32[]{:S(2)}, u32[]{:S(2)}) collective-permute-start(bf16[128,640]{0,1:T(8,128)(2,1)S(1)} %bitcast.281), channel_id=1, source_target_pairs={{0,8},{4,12},{8,16},{12,20},{16,24},{20,28},{24,32},{28,36},{32,40... | collective-permute-start | bytes 491528 | tf_op jit(solution)/shard_map/ppermute | solution.py:14
  412.3 17.7 %collective-permute-start.2 = (bf16[128,640]{0,1:T(8,128)(2,1)S(1)}, bf16[128,640]{0,1:T(8,128)(2,1)}, u32[]{:S(2)}, u32[]{:S(2)}) collective-permute-start(bf16[128,640]{0,1:T(8,128)(2,1)S(1)} %bitcast.282), channel_id=1, source_target_pairs={{0,4},{4,8},{8,12},{12,16},{16,20},{20,24},{24,28},{28,32},{32,36}... | collective-permute-start | bytes 491528 | tf_op jit(solution)/shard_map/ppermute | solution.py:14
  415.8 35.1 %copy-start.24 = (bf16[8,128,80]{1,2,0:T(8,128)(2,1)}, bf16[8,128,80]{1,2,0:T(8,128)(2,1)S(1)}, u32[]{:S(2)}) copy-start(bf16[8,128,80]{1,2,0:T(8,128)(2,1)S(1)} %copy.122) | copy-start | bytes 491524
  415.8 31.0 %collective-permute-start.3 = (bf16[128,640]{0,1:T(8,128)(2,1)S(1)}, bf16[128,640]{0,1:T(8,128)(2,1)}, u32[]{:S(2)}, u32[]{:S(2)}) collective-permute-start(bf16[128,640]{0,1:T(8,128)(2,1)S(1)} %bitcast.285), channel_id=1, source_target_pairs={{0,12},{4,16},{8,20},{12,24},{16,28},{20,32},{24,36},{28,40},{32,4... | collective-permute-start | bytes 491528 | tf_op jit(solution)/shard_map/ppermute | solution.py:14
  417.7 32.5 %collective-permute-start.4 = (bf16[128,640]{0,1:T(8,128)(2,1)S(1)}, bf16[128,640]{0,1:T(8,128)(2,1)}, u32[]{:S(2)}, u32[]{:S(2)}) collective-permute-start(bf16[128,640]{0,1:T(8,128)(2,1)S(1)} %bitcast.286), channel_id=1, source_target_pairs={{0,8},{4,12},{8,16},{12,20},{16,24},{20,28},{24,32},{28,36},{32,40... | collective-permute-start | bytes 491528 | tf_op jit(solution)/shard_map/ppermute | solution.py:14
  420.8 9.2 copy-start.26
  422.0 9.6 copy-start.14
  422.2 10.8 copy-start.16
  422.5 7.4 copy-start.36
  422.5 27.7 %collective-permute-start.5 = (bf16[128,640]{0,1:T(8,128)(2,1)S(1)}, bf16[128,640]{0,1:T(8,128)(2,1)S(1)}, u32[]{:S(2)}, u32[]{:S(2)}) collective-permute-start(bf16[128,640]{0,1:T(8,128)(2,1)S(1)} %bitcast.287), channel_id=1, source_target_pairs={{0,4},{4,8},{8,12},{12,16},{16,20},{20,24},{24,28},{28,32},{32,36}... | collective-permute-start | bytes 491528 | tf_op jit(solution)/shard_map/ppermute | solution.py:14
  431.6 19.3 %copy-start.3 = (f32[8,128,512]{2,1,0:T(8,128)}, f32[8,128,512]{2,1,0:T(8,128)S(1)}, u32[]{:S(2)}) copy-start(f32[8,128,512]{2,1,0:T(8,128)S(1)} %get-tuple-element.41) | copy-start | bytes 6291460
  432.6 26.7 %copy-start.27 = (f32[512,8]{0,1:T(8,128)}, f32[512,8]{0,1:T(8,128)S(1)}, u32[]{:S(2)}) copy-start(f32[512,8]{0,1:T(8,128)S(1)} %add_select_fusion) | copy-start | bytes 49156
  434.8 64.8 %collective-permute-start.10 = (f32[128,640]{0,1:T(8,128)}, f32[128,640]{0,1:T(8,128)}, u32[]{:S(2)}, u32[]{:S(2)}) collective-permute-start(f32[128,640]{0,1:T(8,128)} %bitcast.83), channel_id=1, source_target_pairs={{8,0},{12,4},{16,8},{20,12},{24,16},{28,20},{32,24},{36,28},{40,32... | collective-permute-start | bytes 983048 | tf_op jit(solution)/shard_map/ppermute | solution.py:14
  439.7 71.7 %collective-permute-start.11 = (f32[128,640]{0,1:T(8,128)}, f32[128,640]{0,1:T(8,128)}, u32[]{:S(2)}, u32[]{:S(2)}) collective-permute-start(f32[128,640]{0,1:T(8,128)} %bitcast.84), channel_id=1, source_target_pairs={{12,0},{16,4},{20,8},{24,12},{28,16},{32,20},{36,24},{40,28},{44,3... | collective-permute-start | bytes 983048 | tf_op jit(solution)/shard_map/ppermute | solution.py:14
  446.8 64.7 %collective-permute-start.9 = (f32[128,640]{0,1:T(8,128)}, f32[128,640]{0,1:T(8,128)}, u32[]{:S(2)}, u32[]{:S(2)}) collective-permute-start(f32[128,640]{0,1:T(8,128)} %bitcast.82), channel_id=1, source_target_pairs={{4,0},{8,4},{12,8},{16,12},{20,16},{24,20},{28,24},{32,28},{36,32}... | collective-permute-start | bytes 983048 | tf_op jit(solution)/shard_map/ppermute | solution.py:14
  474.3 12.0 %copy-start.11 = (pred[512,512]{0,1:T(8,128)(4,1)S(1)}, pred[512,512]{0,1:T(8,128)(4,1)}, u32[]{:S(2)}) copy-start(pred[512,512]{0,1:T(8,128)(4,1)} %copy-done.10) | copy-start | bytes 786436
  474.3 12.0 %copy-start.17 = (bf16[512,640]{0,1:T(8,128)(2,1)S(1)}, bf16[512,640]{0,1:T(8,128)(2,1)}, u32[]{:S(2)}) copy-start(bf16[512,640]{0,1:T(8,128)(2,1)} %copy.65) | copy-start | bytes 1966084
  474.3 12.0 %copy-start.18 = (bf16[512,640]{0,1:T(8,128)(2,1)S(1)}, bf16[512,640]{0,1:T(8,128)(2,1)}, u32[]{:S(2)}) copy-start(bf16[512,640]{0,1:T(8,128)(2,1)} %copy.76) | copy-start | bytes 1966084
  474.3 12.0 %copy-start.28 = (f32[512,8]{0,1:T(8,128)S(1)}, f32[512,8]{0,1:T(8,128)}, u32[]{:S(2)}) copy-start(f32[512,8]{0,1:T(8,128)} %copy-done.27) | copy-start | bytes 49156
  474.3 12.0 %copy-start.32 = (f32[512,8]{0,1:T(8,128)S(1)}, f32[512,8]{0,1:T(8,128)}, u32[]{:S(2)}) copy-start(f32[512,8]{0,1:T(8,128)} %copy-done.31) | copy-start | bytes 49156
  475.8 39.0 %collective-permute-start.6 = (f32[128,640]{0,1:T(8,128)}, f32[128,640]{0,1:T(8,128)}, u32[]{:S(2)}, u32[]{:S(2)}) collective-permute-start(f32[128,640]{0,1:T(8,128)} %bitcast.70), channel_id=1, source_target_pairs={{4,0},{8,4},{12,8},{16,12},{20,16},{24,20},{28,24},{32,28},{36,32}... | collective-permute-start | bytes 983048 | tf_op jit(solution)/shard_map/ppermute | solution.py:14
  479.2 35.6 %collective-permute-start.7 = (f32[128,640]{0,1:T(8,128)}, f32[128,640]{0,1:T(8,128)}, u32[]{:S(2)}, u32[]{:S(2)}) collective-permute-start(f32[128,640]{0,1:T(8,128)} %bitcast.71), channel_id=1, source_target_pairs={{8,0},{12,4},{16,8},{20,12},{24,16},{28,20},{32,24},{36,28},{40,32... | collective-permute-start | bytes 983048 | tf_op jit(solution)/shard_map/ppermute | solution.py:14
  497.9 7.5 copy-start.5
  499.6 10.7 copy-start.19
  499.6 18.3 %collective-permute-start.8 = (f32[128,640]{0,1:T(8,128)}, f32[128,640]{0,1:T(8,128)}, u32[]{:S(2)}, u32[]{:S(2)}) collective-permute-start(f32[128,640]{0,1:T(8,128)} %bitcast.271), channel_id=1, source_target_pairs={{12,0},{16,4},{20,8},{24,12},{28,16},{32,20},{36,24},{40,28},{44,3... | collective-permute-start | bytes 983048 | tf_op jit(solution)/shard_map/ppermute | solution.py:14
  1101.4 7.7 copy-start.1
  (23 other events, 62.7 us)
Sparse Core Ops, SparseCore 0:
  9.8 34.6 all-gather.1
  473.6 613.9 all-reduce.4
where the time goes:
time: 1120 us
  waiting for transfers between devices  572 us (51%)
  blocking collectives  337 us (30%)
  local copies, waits for them, and re-layouts  76.1 us (7%)
  matrix products  55.6 us (5%)
  starting transfers between devices  47.8 us (4%)
  between operations  15.8 us (1%)
  other arithmetic  12.1 us (1%)
    unnamed x3, waiting for transfers between devices  567 us
    all_gather x1, blocking collectives, on_device(): lax.all_gather(far_own_keys.reshape(far_count, row_width), 'seq', axis=0,...  171 us
    all_gather x1, blocking collectives, on_device(): lax.all_gather(far_own_values.reshape(far_count, row_width), 'seq', axis=...  166 us
    ppermute x12, starting transfers between devices, passed_along(): return lax.ppermute(block, axis, route)  47.8 us
  transfers between devices with their start and end apart: 14, of which 3 were waited for; matrix products, arithmetic and copies ran while one was open for 9% of the time, Pallas kernels for 0%

commit v1 on v0

v1 whole, which is shorter than its diff:
```python
import functools
import math

import jax
import jax.numpy as jnp
from jax import lax
from jax.experimental import pallas as pl
from jax.experimental.pallas import tpu as pltpu
from jax.sharding import PartitionSpec as P

NEAR = 4
F32 = jnp.float32
BF16 = jnp.bfloat16
LOG2E = math.log2(math.e)
NEG = float("-inf")


def nn(a, b):
    return lax.dot_general(a, b, (((1,), (0,)), ((), ())), preferred_element_type=F32)


def nt(a, b):
    return lax.dot_general(a, b, (((1,), (1,)), ((), ())), preferred_element_type=F32)


def tn(a, b):
    return lax.dot_general(a, b, (((0,), (0,)), ((), ())), preferred_element_type=F32)


def iota(shape, dim):
    return lax.broadcasted_iota(jnp.int32, shape, dim)


def one_hot(mask):
    return jnp.where(mask, 1.0, 0.0).astype(BF16)


def pick_matrix(tokens, count, offset):
    rate = tokens // count
    return one_hot(iota((tokens, count), 0) == iota((tokens, count), 1) * rate + offset)


def place_matrix(tokens, count, offset, rows=None):
    rate = tokens // count
    rows = rows or count
    return one_hot(iota((rows, tokens), 1) == iota((rows, tokens), 0) * rate + offset)


def split3(x):
    high = x.astype(BF16).astype(F32)
    rest = x - high
    middle = rest.astype(BF16).astype(F32)
    return high, middle, rest - middle


def log2_add(a, b):
    top = jnp.maximum(a, b)
    return top + jnp.log(jnp.exp2(a - top) + jnp.exp2(b - top)) * LOG2E


def causal_mask(size):
    return iota((size, size), 0) <= iota((size, size), 1)


def halves(tokens):
    half = tokens // 2
    return half, ((0, slice(0, half)), (1, slice(half, tokens)))


def forward(qt, kt, vt, factor, diag):
    tokens = qt.shape[1]
    half, blocks = halves(tokens)
    outs, norms = [], []
    for index, cols in blocks:
        keys = (index + 1) * half
        scores = tn(kt[:, :keys], qt[:, cols])
        last = jnp.where(diag, scores[keys - half :], NEG)
        parts = [last] if index == 0 else [scores[:half], last]
        top = functools.reduce(
            jnp.maximum, [jnp.max(part, axis=0, keepdims=True) for part in parts]
        )
        top = top * factor
        probs = [jnp.exp2(part * factor - top) for part in parts]
        total = sum(jnp.sum(part, axis=0, keepdims=True) for part in probs)
        packed = [part.astype(BF16) for part in probs]
        packed = packed[0] if index == 0 else jnp.concatenate(packed, axis=0)
        outs.append(nn(vt[:, :keys], packed) / total)
        norms.append(top + jnp.log(total) * LOG2E)
    return jnp.concatenate(outs, axis=1), jnp.concatenate(norms, axis=1)


def backward(qt, kt, vt, gt, norm, delta, factor, scale, diag):
    tokens = qt.shape[1]
    half, blocks = halves(tokens)
    dq = []
    for index, cols in blocks:
        keys = (index + 1) * half
        scores = tn(kt[:, :keys], qt[:, cols]) * factor - norm[:, cols]
        last = jnp.where(diag, jnp.exp2(scores[keys - half :]), 0.0)
        if index == 0:
            probs = last
        else:
            probs = jnp.concatenate([jnp.exp2(scores[:half]), last], axis=0)
        dprobs = tn(vt[:, :keys], gt[:, cols])
        dscores = (probs * (dprobs - delta[:, cols])).astype(BF16)
        dq.append(nn(kt[:, :keys], dscores) * scale)
        dk_part = nt(qt[:, cols], dscores) * scale
        dv_part = nt(gt[:, cols], probs.astype(BF16))
        if index == 0:
            dk, dv = dk_part, dv_part
        else:
            dk = jnp.concatenate([dk + dk_part[:, :half], dk_part[:, half:]], axis=1)
            dv = jnp.concatenate([dv + dv_part[:, :half], dv_part[:, half:]], axis=1)
    return jnp.concatenate(dq, axis=1), dk, dv


def prep_kernel(heads, sc, q, k, v, qkvt, near_q, near_kv, far_msg):
    tokens, width = q.shape
    d = width // heads
    for slot, ref in enumerate((q, k, v)):
        turned = ref[...].T
        for h in range(heads):
            qkvt[h, slot * d : (slot + 1) * d, :] = turned[h * d : (h + 1) * d]
    fill = qkvt.shape[1] - 3 * d
    near_count = tokens // NEAR
    for h in range(heads):
        qkvt[h, 3 * d :, :] = jnp.zeros((fill, tokens), BF16)
        block = qkvt[h]
        near = nn(block[: 3 * d], pick_matrix(tokens, near_count, sc[h])).astype(BF16)
        near_q[h] = near[:d]
        near_kv[h] = near[d:]
        rows = nt(place_matrix(tokens, 8, sc[heads + h], 16), block)
        message = jnp.concatenate([rows[:8, :128], rows[:8, 128:]], axis=0).astype(BF16)
        for copy in range(far_msg.shape[0]):
            far_msg[copy, h] = message


def local_kernel(heads, d, factor, qkvt, out, norm):
    tokens = qkvt.shape[2]
    diag = causal_mask(tokens // 2)
    for h in range(heads):
        o, n = forward(
            qkvt[h, :d], qkvt[h, d : 2 * d], qkvt[h, 2 * d : 3 * d], factor, diag
        )
        out[h] = o
        norm[h : h + 1, :] = n


def far_forward_kernel(d, factor, sc, got, qkvt, out, norm, msg, turned):
    rows = got[...].astype(F32)
    tokens = rows.shape[0] * 8
    wide = jnp.concatenate(
        [rows[:, :8].reshape(tokens, 128), rows[:, 8:].reshape(tokens, 128)], axis=1
    )
    block = wide.T.astype(BF16)
    qkvt[...] = block
    diag = causal_mask(tokens // 2)
    o, n = forward(block[:d], block[d : 2 * d], block[2 * d : 3 * d], factor, diag)
    out[...] = o
    norm[...] = jnp.broadcast_to(n, norm.shape)
    stack = jnp.concatenate(
        [o, jnp.broadcast_to(n, (8, tokens)), jnp.zeros((120 - d, tokens), F32)], axis=0
    )
    turned[...] = stack.T
    msg[...] = turned[pl.ds(pl.multiple_of(sc[17] * 64, 64), 64), :]


def near_bias(sc, slot):
    return jnp.where(sc[16] >= slot, 0.0, NEG).astype(F32)


def near_scores(sc, kt, qt, diag):
    count = qt.shape[1]
    scores = tn(kt, qt)
    parts = [jnp.where(diag, scores[:count], NEG)]
    for slot in range(1, NEAR):
        parts.append(scores[slot * count : (slot + 1) * count] + near_bias(sc, slot))
    return parts


def near_forward_kernel(heads, d, factor, sc, q, kv0, kv1, kv2, kv3, out, norm):
    count = q.shape[2]
    diag = causal_mask(count)
    for h in range(heads):
        kv = jnp.concatenate([kv0[h], kv1[h], kv2[h], kv3[h]], axis=1)
        parts = near_scores(sc, kv[:d], q[h], diag)
        top = functools.reduce(
            jnp.maximum, [jnp.max(part, axis=0, keepdims=True) for part in parts]
        )
        top = top * factor
        probs = [jnp.exp2(part * factor - top) for part in parts]
        total = sum(jnp.sum(part, axis=0, keepdims=True) for part in probs)
        packed = jnp.concatenate([part.astype(BF16) for part in probs], axis=0)
        out[h] = (nn(kv[d:], packed) / total).astype(BF16)
        norm[h : h + 1, :] = top + jnp.log(total) * LOG2E


def mix_kernel(
    heads, d, sc, w, c0, c1, c2, c3, l_out, l_norm, n_out, n_norm, gt, out, norm, msg
):
    tokens = c0.shape[0]
    width = heads * d
    grads = jnp.zeros((width, tokens), F32)
    for flip, ref in enumerate((c0, c1, c2, c3)):
        first = pl.multiple_of(jnp.bitwise_xor(sc[18], flip) * width, 128)
        grads = grads + nt(w[:, pl.ds(first, width)], ref[...])
    grads = grads.astype(BF16)
    gt[...] = grads
    count = tokens // NEAR
    lane = iota((1, tokens), 1)
    for h in range(heads):
        place = place_matrix(tokens, count, sc[h])
        terms = jnp.concatenate(split3(n_norm[h : h + 1, :]), axis=0)
        spread = jnp.sum(nn(terms.astype(BF16), place), axis=0, keepdims=True)
        near = jnp.where(lane % NEAR == sc[h], spread, NEG)
        mine = l_norm[h : h + 1, :]
        both = log2_add(mine, near)
        mixed = jnp.exp2(mine - both) * l_out[h] + jnp.exp2(near - both) * nn(
            n_out[h], place
        )
        out[h] = mixed
        norm[h : h + 1, :] = both
        g = grads[h * d : (h + 1) * d]
        product = jnp.sum(g.astype(F32) * mixed, axis=0, keepdims=True)
        stack = jnp.concatenate(
            [
                g.astype(F32),
                *split3(both),
                *split3(product),
                jnp.zeros((122 - d, tokens), F32),
            ],
            axis=0,
        ).astype(BF16)
        rows = nt(place_matrix(tokens, 8, sc[heads + h], 16), stack)[:8]
        for copy in range(msg.shape[0]):
            msg[copy, h] = rows


def total_kernel(
    heads, d, factor, scale, sc, gt, out, norm, far, nq, kv0, kv1, kv2, kv3,
    attended, all_norm, all_delta, own, back1, back2, back3, turned,
):
    tokens = gt.shape[1]
    count = tokens // NEAR
    diag = causal_mask(count)
    for h in range(heads):
        place = iota((8, tokens), 1) == iota((8, tokens), 0) * 64 + sc[heads + h]
        rows = far[h]
        spread = jnp.sum(jnp.where(place, rows[:, d : d + 1], 0.0), axis=0, keepdims=True)
        hit = iota((1, tokens), 1) % 64 == sc[heads + h]
        far_norm = jnp.where(hit, spread, NEG)
        mine = norm[h : h + 1, :]
        both = log2_add(mine, far_norm)
        far_out = tn(rows[:, :d].astype(BF16), one_hot(place))
        mixed = jnp.exp2(mine - both) * out[h] + jnp.exp2(far_norm - both) * far_out
        mixed = mixed.astype(BF16)
        turned[h * d : (h + 1) * d, :] = mixed
        g = gt[h * d : (h + 1) * d, :]
        delta = jnp.sum(g.astype(F32) * mixed.astype(F32), axis=0, keepdims=True)
        all_norm[h : h + 1, :] = both
        all_delta[h : h + 1, :] = delta
        stack = jnp.concatenate(
            [g.astype(F32), *split3(both), *split3(delta), jnp.zeros((10, tokens), F32)], axis=0
        ).astype(BF16)
        picked = nn(stack, pick_matrix(tokens, count, sc[h]))
        near_g = picked[:d].astype(BF16)
        near_norm = picked[d : d + 1] + picked[d + 1 : d + 2] + picked[d + 2 : d + 3]
        near_delta = picked[d + 3 : d + 4] + picked[d + 4 : d + 5] + picked[d + 5 : d + 6]
        kv = jnp.concatenate([kv0[h], kv1[h], kv2[h], kv3[h]], axis=1)
        q = nq[h]
        parts = near_scores(sc, kv[:d], q, diag)
        probs = jnp.concatenate(
            [jnp.exp2(part * factor - near_norm) for part in parts], axis=0
        )
        dprobs = tn(kv[d:], near_g)
        dscores = (probs * (dprobs - near_delta)).astype(BF16)
        own[h, :d] = (nn(kv[:d], dscores) * scale).astype(BF16)
        dk = (nt(q, dscores) * scale).astype(BF16)
        dv = nt(near_g, probs.astype(BF16)).astype(BF16)
        own[h, d : 2 * d] = dk[:, :count]
        own[h, 2 * d :] = dv[:, :count]
        for slot, ref in ((1, back1), (2, back2), (3, back3)):
            ref[h, :d] = dk[:, slot * count : (slot + 1) * count]
            ref[h, d:] = dv[:, slot * count : (slot + 1) * count]
    attended[...] = turned[...].T


def far_backward_kernel(d, factor, scale, sc, qkvt, out, norm, got, msg, turned):
    tokens = qkvt.shape[1]
    rows = got[...].reshape(tokens, 128).T
    gt = rows[:d].astype(BF16)
    rest_norm = rows[d : d + 1] + rows[d + 1 : d + 2] + rows[d + 2 : d + 3]
    rest_delta = rows[d + 3 : d + 4] + rows[d + 4 : d + 5] + rows[d + 5 : d + 6]
    mine = norm[:1, :]
    both = log2_add(mine, rest_norm)
    mine_delta = jnp.sum(rows[:d] * out[...], axis=0, keepdims=True)
    delta = jnp.exp2(mine - both) * mine_delta + jnp.exp2(rest_norm - both) * rest_delta
    dq, dk, dv = backward(
        qkvt[:d], qkvt[d : 2 * d], qkvt[2 * d : 3 * d], gt, both, delta, factor, scale,
        causal_mask(tokens // 2),
    )
    stack = jnp.concatenate([dq, dk, dv, jnp.zeros((256 - 3 * d, tokens), F32)], axis=0)
    turned[...] = stack.T
    msg[...] = turned[pl.ds(pl.multiple_of(sc[17] * 64, 64), 64), :]


def local_backward_kernel(heads, d, factor, scale, qkvt, gt, norm, delta, grads):
    tokens = gt.shape[1]
    diag = causal_mask(tokens // 2)
    for h in range(heads):
        dq, dk, dv = backward(
            qkvt[h, :d],
            qkvt[h, d : 2 * d],
            qkvt[h, 2 * d : 3 * d],
            gt[h * d : (h + 1) * d, :],
            norm[h : h + 1, :],
            delta[h : h + 1, :],
            factor,
            scale,
            diag,
        )
        grads[h, :d] = dq
        grads[h, d : 2 * d] = dk
        grads[h, 2 * d :] = dv


def final_kernel(heads, d, sc, grads, own, back1, back2, back3, far, dq, dk, dv, turned):
    tokens = grads.shape[2]
    count = tokens // NEAR
    for h in range(heads):
        near = own[h].astype(F32)
        came = back1[h].astype(F32) + back2[h].astype(F32) + back3[h].astype(F32)
        near = jnp.concatenate([near[:d], near[d:] + came], axis=0).astype(BF16)
        total = grads[h] + nn(near, place_matrix(tokens, count, sc[h]))
        place = one_hot(iota((8, tokens), 1) == iota((8, tokens), 0) * 64 + sc[heads + h])
        total = total + tn(far[h].astype(BF16), place)[: 3 * d]
        total = total.astype(BF16)
        for slot in range(3):
            turned[slot, h * d : (h + 1) * d, :] = total[slot * d : (slot + 1) * d]
    for slot, ref in enumerate((dq, dk, dv)):
        ref[...] = turned[slot].T


def call(kernel, name, operands, outs, scratch=(), scalars=None, flops=0):
    specs = [pl.BlockSpec(memory_space=pltpu.VMEM)] * len(operands)
    if scalars is not None:
        specs = [pl.BlockSpec(memory_space=pltpu.SMEM)] + specs
        operands = [scalars, *operands]
    size = sum(math.prod(x.shape) * x.dtype.itemsize for x in [*operands, *outs])
    return pl.pallas_call(
        kernel,
        name=name,
        out_shape=outs,
        in_specs=specs,
        out_specs=[pl.BlockSpec(memory_space=pltpu.VMEM)] * len(outs),
        scratch_shapes=list(scratch),
        compiler_params=pltpu.CompilerParams(vmem_limit_bytes=40 * 1024 * 1024),
        cost_estimate=pl.CostEstimate(flops=flops, bytes_accessed=size, transcendentals=0),
    )(*operands)


def on_device(query_rows, key_rows, value_rows, out_weight, cotangent, offsets):
    tokens, width = query_rows.shape
    heads = offsets.shape[1]
    d = width // heads
    scale = 1.0 / math.sqrt(d)
    factor = scale * LOG2E
    seq_size = lax.axis_size("seq")
    seq = lax.axis_index("seq")
    head = lax.axis_index("head")
    count = tokens // NEAR
    groups = seq_size // heads
    columns = [[a * heads + z for z in range(heads)] for a in range(groups)]

    def struct(shape, dtype):
        return jax.ShapeDtypeStruct(shape, dtype)

    extras = jnp.stack([seq % NEAR, seq // heads, head]).astype(jnp.int32)
    sc = jnp.concatenate([offsets.reshape(2 * heads), extras])

    c2 = lax.ppermute(cotangent, "head", [(i, i ^ 2) for i in range(4)])
    c1 = lax.ppermute(cotangent, "head", [(i, i ^ 1) for i in range(4)])
    c3 = lax.ppermute(c2, "head", [(i, i ^ 1) for i in range(4)])

    qkvt, near_q, near_kv, far_msg = call(
        functools.partial(prep_kernel, heads),
        "prep",
        [query_rows, key_rows, value_rows],
        [
            struct((heads, 256, tokens), BF16),
            struct((heads, d, count), BF16),
            struct((heads, 2 * d, count), BF16),
            struct((groups, heads, 16, 128), BF16),
        ],
        scalars=sc,
        flops=3_000_000_000,
    )
    far_got = lax.all_to_all(
        far_msg.reshape(seq_size, 16, 128), "seq", 0, 0, tiled=True
    )

    def shifted(x, distance):
        if distance > 0:
            route = [(i - distance, i) for i in range(seq_size) if i % NEAR >= distance]
        else:
            route = [(i, i + distance) for i in range(seq_size) if i % NEAR >= -distance]
        return lax.ppermute(x, "seq", route)

    kvs = [near_kv] + [shifted(near_kv, distance) for distance in (1, 2, 3)]
    l_out, l_norm = call(
        functools.partial(local_kernel, heads, d, factor),
        "local_forward",
        [qkvt],
        [struct((heads, d, tokens), F32), struct((heads, tokens), F32)],
        flops=5_000_000_000,
    )
    n_out, n_norm = call(
        functools.partial(near_forward_kernel, heads, d, factor),
        "near_forward",
        [near_q, *kvs],
        [struct((heads, d, count), BF16), struct((heads, count), F32)],
        scalars=sc,
        flops=2_000_000_000,
    )
    gt, out, norm, stat_msg = call(
        functools.partial(mix_kernel, heads, d),
        "mix",
        [out_weight, cotangent, c1, c2, c3, l_out, l_norm, n_out, n_norm],
        [
            struct((width, tokens), BF16),
            struct((heads, d, tokens), F32),
            struct((heads, tokens), F32),
            struct((groups, heads, 8, 128), F32),
        ],
        scalars=sc,
        flops=4_000_000_000,
    )
    stat_got = lax.all_to_all(stat_msg.reshape(seq_size, 8, 128), "seq", 0, 0, tiled=True)
    far_qkvt, far_out, far_norm, out_msg = call(
        functools.partial(far_forward_kernel, d, factor),
        "far_forward",
        [far_got],
        [
            struct((256, tokens), BF16),
            struct((d, tokens), F32),
            struct((8, tokens), F32),
            struct((64, 128), F32),
        ],
        scratch=[pltpu.VMEM((tokens, 128), F32)],
        scalars=sc,
        flops=2_000_000_000,
    )
    out_got = lax.all_to_all(
        out_msg.reshape(heads, 8, 128), "seq", 0, 0, tiled=True, axis_index_groups=columns
    )
    attended, all_norm, all_delta, own, back1, back2, back3 = call(
        functools.partial(total_kernel, heads, d, factor, scale),
        "total",
        [gt, out, norm, out_got, near_q, *kvs],
        [
            struct((tokens, width), BF16),
            struct((heads, tokens), F32),
            struct((heads, tokens), F32),
            struct((heads, 3 * d, count), BF16),
            struct((heads, 2 * d, count), BF16),
            struct((heads, 2 * d, count), BF16),
            struct((heads, 2 * d, count), BF16),
        ],
        scratch=[pltpu.VMEM((width, tokens), BF16)],
        scalars=sc,
        flops=5_000_000_000,
    )
    backs = [shifted(x, -distance) for distance, x in ((1, back1), (2, back2), (3, back3))]
    (grad_msg,) = call(
        functools.partial(far_backward_kernel, d, factor, scale),
        "far_backward",
        [far_qkvt, far_out, far_norm, stat_got],
        [struct((64, 256), F32)],
        scratch=[pltpu.VMEM((tokens, 256), F32)],
        scalars=sc,
        flops=2_000_000_000,
    )
    grad_got = lax.all_to_all(
        grad_msg.reshape(heads, 8, 256), "seq", 0, 0, tiled=True, axis_index_groups=columns
    )
    (grads,) = call(
        functools.partial(local_backward_kernel, heads, d, factor, scale),
        "local_backward",
        [qkvt, gt, all_norm, all_delta],
        [struct((heads, 3 * d, tokens), F32)],
        flops=8_000_000_000,
    )
    grad_query, grad_key, grad_value = call(
        functools.partial(final_kernel, heads, d),
        "final",
        [grads, own, *backs, grad_got],
        [struct((tokens, width), BF16)] * 3,
        scratch=[pltpu.VMEM((3, width, tokens), BF16)],
        scalars=sc,
        flops=2_000_000_000,
    )
    return (attended, grad_query, grad_key, grad_value)


def solution(mesh):
    return jax.shard_map(
        on_device,
        mesh=mesh,
        in_specs=(
            P("seq", "head"),
            P("seq", "head"),
            P("seq", "head"),
            P("head", None),
            P("seq", "head"),
            P(None, "head"),
        ),
        out_specs=(P("seq", "head"), P("seq", "head"), P("seq", "head"), P("seq", "head")),
        check_vma=False,
    )
```

time: 1120 us -> 132 us (0.12)
  waiting for transfers between devices: 572 us -> 18.9 us
  blocking collectives: 337 us -> 0 us
  matrix products: 55.6 us -> 0 us
  local copies, waits for them, and re-layouts: 76.1 us -> 25.9 us
  Pallas kernels: 0 us -> 33.8 us
  between operations: 15.8 us -> 0.84 us
  other arithmetic: 12.1 us -> 0.08 us
    unnamed x3 -> x0, waiting for transfers between devices: 567 us -> none
    all_gather x2 -> x0, blocking collectives: 337 us -> none  [the longest x1 171 us: on_device(): lax.all_gather(far_own_keys.reshape(far_count, row_width), 'seq', axis=0,...]
    dot_general x23 -> x0, matrix products: 55.6 us -> none  [the longest x3 8.84 us: level_grads(): jnp.einsum('ahd,bhd->hab', grads_out, values, preferred_element_type=jnp....]
    pallas_call x0 -> x9, Pallas kernels: none -> 33.8 us  [call(): pl.pallas_call(kernel, name=name, out_shape=outs, in_specs=specs, out_spe...]
    all_to_all x0 -> x4, starting transfers between devices: none -> 33.8 us  [the longest x1 11 us: on_device(): lax.all_to_all(stat_msg.reshape(seq_size, 8, 128), 'seq', 0, 0, tiled=True)]
    ppermute x12 -> x9, starting transfers between devices: 47.8 us -> 18.1 us  [the longest x6 15.6 us: shifted(): return lax.ppermute(x, 'seq', route)]
    another operation x8 -> x0, local copies, waits for them, and re-layouts: 21.1 us -> none  [choose_rows(): matrix.reshape(row_count // dilation, dilation, head_count, head_width)]
    broadcast_in_dim x26 -> x0, local copies, waits for them, and re-layouts: 20.3 us -> none  [the longest x18 18.5 us: spread_rows(): widened = jnp.where(pick_mask[None, :, :, None], level_out[:, None], 0.0)]
  transfers between devices with their start and end apart: 14 -> 13, of which waited for: 3 -> 3; matrix products, arithmetic and copies ran while one was open for 9% -> 1% of each run, Pallas kernels for 0% -> 23%
where the time goes in v1:
time: 132 us; the launch traced here: 131 us
  starting transfers between devices  51.9 us (39%)
  Pallas kernels  33.8 us (26%)
  local copies, waits for them, and re-layouts  25.9 us (20%)
  waiting for transfers between devices  18.9 us (14%)
    pallas_call x9, Pallas kernels, call(): pl.pallas_call(kernel, name=name, out_shape=outs, in_specs=specs, out_spe...  33.8 us
    unnamed x46, local copies, waits for them, and re-layouts  25.2 us
    ppermute x6, starting transfers between devices, shifted(): return lax.ppermute(x, 'seq', route)  15.6 us
    all_to_all x1, waiting for transfers between devices, on_device(): lax.all_to_all(far_msg.reshape(seq_size, 16, 128), 'seq', 0, 0, tiled=True)  13.2 us
    all_to_all x1, starting transfers between devices, on_device(): lax.all_to_all(stat_msg.reshape(seq_size, 8, 128), 'seq', 0, 0, tiled=True)  11 us
    all_to_all x1, starting transfers between devices, on_device(): lax.all_to_all(far_msg.reshape(seq_size, 16, 128), 'seq', 0, 0, tiled=True)  10.3 us
    all_to_all x1, starting transfers between devices, on_device(): lax.all_to_all(grad_msg.reshape(heads, 8, 256), 'seq', 0, 0, tiled=True,...  9.07 us
    ppermute x6, waiting for transfers between devices, shifted(): return lax.ppermute(x, 'seq', route)  5.48 us
  transfers between devices with their start and end apart: 13, of which 3 were waited for; matrix products, arithmetic and copies ran while one was open for 1% of the time, Pallas kernels for 23%

profile of v1, /device:TPU:8, one launch (start us, length us, event | category | flops | bytes accessed | tf_op | source)
XLA Modules:
  0.0 131.4 jit_solution(4055244331362004544)
XLA Ops:
  0.6 2.4 %collective-permute-start.1 = (bf16[512,640]{1,0:T(8,128)(2,1)}, bf16[512,640]{1,0:T(8,128)(2,1)S(1)}, u32[]{:S(2)}, u32[]{:S(2)}) collective-permute-start(bf16[512,640]{1,0:T(8,128)(2,1)} %c0.1), channel_id=1, source_target_pairs={{0,2},{1,3},{2,0},{3,1},{4,6},{5,7},{6,4},{7,5},{8,10},{9,11},{10,... | collective-permute-start | bytes 1966088 | tf_op jit(solution)/shard_map/ppermute | solution.py:381
  3.9 1.1 copy-done.1
  4.9 1.1 copy-done.2
  7.1 2.5 %prep.1 = (bf16[8,256,512]{2,1,0:T(8,128)(2,1)S(1)}, bf16[8,80,128]{2,1,0:T(8,128)(2,1)S(1)}, bf16[8,160,128]{2,1,0:T(8,128)(2,1)S(1)}, bf16[8,8,16,128]{3,2,1,0:T(8,128)(2,1)}) custom-call(s32[19]{0:T(128)S(1)} %pad_add_fusion.sc, bf16[512,640]{1,0:T(8,128)(2,1)S(1)} %copy-done.1, bf16[512,640]{1,0:T(8,128)(2,1)S(1)} %copy-done.2, ...), custom_call_target="tpu_custom_call" | custom-call | flops 3000000000 | bytes 4816972 | tf_op jit(solution)/shard_map/prep/pallas_call | solution.py:350
  9.6 1.3 %copy-done.7 = bf16[8,256,512]{2,1,0:T(8,128)(2,1)} copy-done((bf16[8,256,512]{2,1,0:T(8,128)(2,1)}, bf16[8,256,512]{2,1,0:T(8,128)(2,1)S(1)}, u32[]{:S(2)}) %copy-start.7) | copy-done | bytes 2097176
  10.9 4.5 %collective-permute-start.3 = (bf16[8,160,128]{2,1,0:T(8,128)(2,1)S(1)}, bf16[8,160,128]{2,1,0:T(8,128)(2,1)}, u32[]{:S(2)}, u32[]{:S(2)}) collective-permute-start(bf16[8,160,128]{2,1,0:T(8,128)(2,1)S(1)} %get-tuple-element.34.kv0), channel_id=1, source_target_pairs={{0,4},{4,8},{8,12},{16,20},{20,24},{24,28},{32,36},{36,40},{40,44}... | collective-permute-start | bytes 983048 | tf_op jit(solution)/shard_map/ppermute | solution.py:407
  15.5 5.2 %collective-permute-start.4 = (bf16[8,160,128]{2,1,0:T(8,128)(2,1)S(1)}, bf16[8,160,128]{2,1,0:T(8,128)(2,1)}, u32[]{:S(2)}, u32[]{:S(2)}) collective-permute-start(bf16[8,160,128]{2,1,0:T(8,128)(2,1)S(1)} %get-tuple-element.34.kv0), channel_id=1, source_target_pairs={{0,8},{4,12},{16,24},{20,28},{32,40},{36,44},{48,56},{52,60},{64,7... | collective-permute-start | bytes 983048 | tf_op jit(solution)/shard_map/ppermute | solution.py:407
  20.7 2.0 %collective-permute-start.5 = (bf16[8,160,128]{2,1,0:T(8,128)(2,1)S(1)}, bf16[8,160,128]{2,1,0:T(8,128)(2,1)}, u32[]{:S(2)}, u32[]{:S(2)}) collective-permute-start(bf16[8,160,128]{2,1,0:T(8,128)(2,1)S(1)} %get-tuple-element.34.kv0), channel_id=1, source_target_pairs={{0,12},{16,28},{32,44},{48,60},{64,76},{80,92},{96,108},{112,124},... | collective-permute-start | bytes 983048 | tf_op jit(solution)/shard_map/ppermute | solution.py:407
  22.7 10.3 %all-to-all-start = ((bf16[64,16,128]{2,1,0:T(8,128)(2,1)}), bf16[64,16,128]{2,1,0:T(8,128)(2,1)S(1)}, u32[]{:S(2)}, u32[]{:S(2)}) async-start(bf16[64,16,128]{2,1,0:T(8,128)(2,1)} %bitcast.3), calls=%async_computation | async-start | bytes 524288 | tf_op jit(solution)/shard_map/all_to_all | solution.py:398
  33.2 1.6 %copy-done.8 = bf16[8,256,512]{2,1,0:T(8,128)(2,1)S(1)} copy-done((bf16[8,256,512]{2,1,0:T(8,128)(2,1)S(1)}, bf16[8,256,512]{2,1,0:T(8,128)(2,1)}, u32[]{:S(2)}) %copy-start.8) | copy-done | bytes 2097176
  34.8 3.9 %local_forward.1 = (f32[8,80,512]{2,1,0:T(8,128)S(1)}, f32[8,512]{1,0:T(8,128)S(1)}) custom-call(bf16[8,256,512]{2,1,0:T(8,128)(2,1)S(1)} %copy-done.8), custom_call_target="tpu_custom_call" | custom-call | flops 5000000000 | bytes 3424256 | tf_op jit(solution)/shard_map/local_forward/pallas_call | solution.py:350
  39.7 3.5 %near_forward.1 = (bf16[8,80,128]{2,1,0:T(8,128)(2,1)S(1)}, f32[8,128]{1,0:T(8,128)S(1)}) custom-call(s32[19]{0:T(128)S(1)} %pad_add_fusion.sc, bf16[8,80,128]{2,1,0:T(8,128)(2,1)S(1)} %get-tuple-element.33.q.nq, bf16[8,160,128]{2,1,0:T(8,128)(2,1)S(1)} %get-tuple-element.34.kv0, bf16[8,160,128]{2,1,0:T(8,128)(2,1)} %collective-permute-done.3.kv1, ...), custom_call_target="tpu_custom_call" | custom-call | flops 2000000000 | bytes 1642572 | tf_op jit(solution)/shard_map/near_forward/pallas_call | solution.py:350
  43.9 13.2 %all-to-all-done.got = bf16[64,16,128]{2,1,0:T(8,128)(2,1)S(1)} async-done(((bf16[64,16,128]{2,1,0:T(8,128)(2,1)}), bf16[64,16,128]{2,1,0:T(8,128)(2,1)S(1)}, u32[]{:S(2)}, u32[]{:S(2)}) %all-to-all-start) | async-done | bytes 262176 | tf_op jit(solution)/shard_map/all_to_all | solution.py:398
  57.1 1.9 %far_forward.1 = (bf16[256,512]{1,0:T(8,128)(2,1)S(1)}, f32[80,512]{1,0:T(8,128)S(1)}, f32[8,512]{1,0:T(8,128)S(1)}, f32[64,128]{1,0:T(8,128)}) custom-call(s32[19]{0:T(128)S(1)} %pad_add_fusion.sc, bf16[64,16,128]{2,1,0:T(8,128)(2,1)S(1)} %all-to-all-done.got), custom_call_target="tpu_custom_call" | custom-call | flops 2000000000 | bytes 737356 | tf_op jit(solution)/shard_map/far_forward/pallas_call | solution.py:350
  60.4 3.3 %all-to-all-start.1 = ((f32[8,8,128]{2,1,0:T(8,128)}), f32[8,8,128]{2,1,0:T(8,128)S(1)}, u32[]{:S(2)}, u32[]{:S(2)}) async-start(f32[8,8,128]{2,1,0:T(8,128)} %bitcast.4), calls=%async_computation.1 | async-start | bytes 65536 | tf_op jit(solution)/shard_map/all_to_all | solution.py:453
  63.8 1.9 %copy-done = bf16[640,2560]{1,0:T(8,128)(2,1)S(1)} copy-done((bf16[640,2560]{1,0:T(8,128)(2,1)S(1)}, bf16[640,2560]{1,0:T(8,128)(2,1)}, u32[]{:S(2)}) %copy-start) | copy-done | bytes 3276824
  65.7 1.3 %copy-done.11 = f32[8,80,512]{2,1,0:T(8,128)S(1)} copy-done((f32[8,80,512]{2,1,0:T(8,128)S(1)}, f32[8,80,512]{2,1,0:T(8,128)}, u32[]{:S(2)}) %copy-start.11) | copy-done | bytes 1310744
  68.0 5.0 %mix.1 = (bf16[640,512]{1,0:T(8,128)(2,1)S(1)}, f32[8,80,512]{2,1,0:T(8,128)S(1)}, f32[8,512]{1,0:T(8,128)S(1)}, f32[8,8,8,128]{3,2,1,0:T(8,128)}) custom-call(s32[19]{0:T(128)S(1)} %pad_add_fusion.sc, bf16[640,2560]{1,0:T(8,128)(2,1)S(1)} %copy-done, bf16[512,640]{1,0:T(8,128)(2,1)S(1)} %copy-done.4, bf16[512,640]{1,0:T(8,128)(2,1)S(1)} %collective-permute-done.c1, ...), custom_call_target="tpu_custom_call" | custom-call | flops 4000000000 | bytes 9637964 | tf_op jit(solution)/shard_map/mix/pallas_call | solution.py:350
  74.9 11.0 %all-to-all-start.2 = ((f32[64,8,128]{2,1,0:T(8,128)}), f32[64,8,128]{2,1,0:T(8,128)S(1)}, u32[]{:S(2)}, u32[]{:S(2)}) async-start(f32[64,8,128]{2,1,0:T(8,128)} %bitcast.5), calls=%async_computation.2 | async-start | bytes 524288 | tf_op jit(solution)/shard_map/all_to_all | solution.py:438
  85.9 1.3 copy-done.13
  88.3 6.1 %total.1 = (bf16[512,640]{1,0:T(8,128)(2,1)}, f32[8,512]{1,0:T(8,128)S(1)}, f32[8,512]{1,0:T(8,128)S(1)}, bf16[8,240,128]{2,1,0:T(8,128)(2,1)S(1)}, bf16[8,160,1...) custom-call(s32[19]{0:T(128)S(1)} %pad_add_fusion.sc, ...), custom_call_target="tpu_custom_call" | custom-call | flops 5000000000 | bytes 5652556 | tf_op jit(solution)/shard_map/total/pallas_call | solution.py:350
  94.4 1.3 collective-permute-start.6
  95.6 1.3 collective-permute-start.7
  96.9 1.3 collective-permute-start.8
  100.1 2.2 %far_backward.1 = f32[64,256]{1,0:T(8,128)} custom-call(s32[19]{0:T(128)S(1)} %pad_add_fusion.sc, bf16[256,512]{1,0:T(8,128)(2,1)S(1)} %copy-done.18, f32[80,512]{1,0:T(8,128)S(1)} %copy-done.22, f32[8,512]{1,0:T(8,128)S(1)} %get-tuple-element.51.norm, f32[64,8,128]{2,1,0:T(8,128)S(1)} %all-to-all-done.2.got), custom_call_target="tpu_custom_call" | custom-call | flops 2000000000 | bytes 770124 | tf_op jit(solution)/shard_map/far_backward/pallas_call | solution.py:350
  102.3 9.1 %all-to-all-start.3 = ((f32[8,8,256]{2,1,0:T(8,128)}), f32[8,8,256]{2,1,0:T(8,128)S(1)}, u32[]{:S(2)}, u32[]{:S(2)}) async-start(f32[8,8,256]{2,1,0:T(8,128)} %bitcast.6), calls=%async_computation.3 | async-start | bytes 131072 | tf_op jit(solution)/shard_map/all_to_all | solution.py:483
  111.4 1.6 %copy-done.9 = bf16[8,256,512]{2,1,0:T(8,128)(2,1)S(1)} copy-done((bf16[8,256,512]{2,1,0:T(8,128)(2,1)S(1)}, bf16[8,256,512]{2,1,0:T(8,128)(2,1)}, u32[]{:S(2)}) %copy-start.9) | copy-done | bytes 2097176
  113.0 5.6 %local_backward.1.grads = f32[8,240,512]{2,1,0:T(8,128)S(1)} custom-call(bf16[8,256,512]{2,1,0:T(8,128)(2,1)S(1)} %copy-done.9, bf16[640,512]{1,0:T(8,128)(2,1)S(1)} %copy-done.16, f32[8,512]{1,0:T(8,128)S(1)} %get-tuple-element.43.norm, f32[8,512]{1,0:T(8,128)S(1)} %get-tuple-element.44.delta), custom_call_target="tpu_custom_call" | custom-call | flops 8000000000 | bytes 6717440 | tf_op jit(solution)/shard_map/local_backward/pallas_call | solution.py:350
  118.7 1.9 %copy-done.5 = f32[8,240,512]{2,1,0:T(8,128)} copy-done((f32[8,240,512]{2,1,0:T(8,128)}, f32[8,240,512]{2,1,0:T(8,128)S(1)}, u32[]{:S(2)}) %copy-start.5) | copy-done | bytes 3932184
  120.5 5.5 %collective-permute-done.7.back2 = bf16[8,160,128]{2,1,0:T(8,128)(2,1)S(1)} collective-permute-done((bf16[8,160,128]{2,1,0:T(8,128)(2,1)S(1)}, bf16[8,160,128]{2,1,0:T(8,128)(2,1)S(1)}, u32[]{:S(2)}, u32[]{:S(2)}) %collective-permute-start.7) | collective-permute-done | bytes 327712 | tf_op jit(solution)/shard_map/ppermute | solution.py:407
  126.2 2.1 %copy-done.6 = f32[8,240,512]{2,1,0:T(8,128)S(1)} copy-done((f32[8,240,512]{2,1,0:T(8,128)S(1)}, f32[8,240,512]{2,1,0:T(8,128)}, u32[]{:S(2)}) %copy-start.6) | copy-done | bytes 3932184
  128.3 3.1 %final.1 = (bf16[512,640]{1,0:T(8,128)(2,1)}, bf16[512,640]{1,0:T(8,128)(2,1)}, bf16[512,640]{1,0:T(8,128)(2,1)}) custom-call(s32[19]{0:T(128)S(1)} %pad_add_fusion.sc, f32[8,240,512]{2,1,0:T(8,128)S(1)} %copy-done.6, bf16[8,240,128]{2,1,0:T(8,128)(2,1)S(1)} %get-tuple-element.45.own, bf16[8,160,128]{2,1,0:T(8,128)(2,1)S(1)} %collective-permute-done.6.back1, ...), custom_call_target="tpu_custom_call" | custom-call | flops 2000000000 | bytes 7438412 | tf_op jit(solution)/shard_map/final/pallas_call | solution.py:350
  (51 shorter events, 11.1 us)
Async XLA Ops:
  0.6 32.4 %collective-permute-start.1 = (bf16[512,640]{1,0:T(8,128)(2,1)}, bf16[512,640]{1,0:T(8,128)(2,1)S(1)}, u32[]{:S(2)}, u32[]{:S(2)}) collective-permute-start(bf16[512,640]{1,0:T(8,128)(2,1)} %c0.1), channel_id=1, source_target_pairs={{0,2},{1,3},{2,0},{3,1},{4,6},{5,7},{6,4},{7,5},{8,10},{9,11},{10,... | collective-permute-start | bytes 1966088 | tf_op jit(solution)/shard_map/ppermute | solution.py:381
  3.9 1.1 copy-start.1
  4.9 1.1 copy-start.2
  6.0 1.1 copy-start.3
  7.1 15.6 %copy-start.4 = (bf16[512,640]{1,0:T(8,128)(2,1)S(1)}, bf16[512,640]{1,0:T(8,128)(2,1)}, u32[]{:S(2)}) copy-start(bf16[512,640]{1,0:T(8,128)(2,1)} %c0.1) | copy-start | bytes 1966084
  9.6 1.3 %copy-start.7 = (bf16[8,256,512]{2,1,0:T(8,128)(2,1)}, bf16[8,256,512]{2,1,0:T(8,128)(2,1)S(1)}, u32[]{:S(2)}) copy-start(bf16[8,256,512]{2,1,0:T(8,128)(2,1)S(1)} %get-tuple-element.30.qkvt) | copy-start | bytes 6291460
  10.9 28.8 %collective-permute-start.3 = (bf16[8,160,128]{2,1,0:T(8,128)(2,1)S(1)}, bf16[8,160,128]{2,1,0:T(8,128)(2,1)}, u32[]{:S(2)}, u32[]{:S(2)}) collective-permute-start(bf16[8,160,128]{2,1,0:T(8,128)(2,1)S(1)} %get-tuple-element.34.kv0), channel_id=1, source_target_pairs={{0,4},{4,8},{8,12},{16,20},{20,24},{24,28},{32,36},{36,40},{40,44}... | collective-permute-start | bytes 983048 | tf_op jit(solution)/shard_map/ppermute | solution.py:407
  15.5 24.2 %collective-permute-start.4 = (bf16[8,160,128]{2,1,0:T(8,128)(2,1)S(1)}, bf16[8,160,128]{2,1,0:T(8,128)(2,1)}, u32[]{:S(2)}, u32[]{:S(2)}) collective-permute-start(bf16[8,160,128]{2,1,0:T(8,128)(2,1)S(1)} %get-tuple-element.34.kv0), channel_id=1, source_target_pairs={{0,8},{4,12},{16,24},{20,28},{32,40},{36,44},{48,56},{52,60},{64,7... | collective-permute-start | bytes 983048 | tf_op jit(solution)/shard_map/ppermute | solution.py:407
  20.7 19.0 %collective-permute-start.5 = (bf16[8,160,128]{2,1,0:T(8,128)(2,1)S(1)}, bf16[8,160,128]{2,1,0:T(8,128)(2,1)}, u32[]{:S(2)}, u32[]{:S(2)}) collective-permute-start(bf16[8,160,128]{2,1,0:T(8,128)(2,1)S(1)} %get-tuple-element.34.kv0), channel_id=1, source_target_pairs={{0,12},{16,28},{32,44},{48,60},{64,76},{80,92},{96,108},{112,124},... | collective-permute-start | bytes 983048 | tf_op jit(solution)/shard_map/ppermute | solution.py:407
  22.7 41.1 %collective-permute-start = (bf16[512,640]{1,0:T(8,128)(2,1)S(1)}, bf16[512,640]{1,0:T(8,128)(2,1)S(1)}, u32[]{:S(2)}, u32[]{:S(2)}) collective-permute-start(bf16[512,640]{1,0:T(8,128)(2,1)S(1)} %copy-done.4), channel_id=1, source_target_pairs={{0,1},{1,0},{2,3},{3,2},{4,5},{5,4},{6,7},{7,6},{8,9},{9,8},{10,11... | collective-permute-start | bytes 1966088 | tf_op jit(solution)/shard_map/ppermute | solution.py:382
  22.7 34.4 %all-to-all-start = ((bf16[64,16,128]{2,1,0:T(8,128)(2,1)}), bf16[64,16,128]{2,1,0:T(8,128)(2,1)S(1)}, u32[]{:S(2)}, u32[]{:S(2)}) async-start(bf16[64,16,128]{2,1,0:T(8,128)(2,1)} %bitcast.3), calls=%async_computation | async-start | bytes 524288 | tf_op jit(solution)/shard_map/all_to_all | solution.py:398
  33.1 30.7 %collective-permute-start.2 = (bf16[512,640]{1,0:T(8,128)(2,1)S(1)}, bf16[512,640]{1,0:T(8,128)(2,1)S(1)}, u32[]{:S(2)}, u32[]{:S(2)}) collective-permute-start(bf16[512,640]{1,0:T(8,128)(2,1)S(1)} %collective-permute-done.1.c2), channel_id=1, source_target_pairs={{0,1},{1,0},{2,3},{3,2},{4,5},{5,4},{6,7},{7,6},{8,9},{9,8},{10,11... | collective-permute-start | bytes 1966088 | tf_op jit(solution)/shard_map/ppermute | solution.py:383
  33.2 1.6 %copy-start.8 = (bf16[8,256,512]{2,1,0:T(8,128)(2,1)S(1)}, bf16[8,256,512]{2,1,0:T(8,128)(2,1)}, u32[]{:S(2)}) copy-start(bf16[8,256,512]{2,1,0:T(8,128)(2,1)} %copy-done.7) | copy-start | bytes 6291460
  38.6 1.1 copy-start.10
  60.4 14.4 %all-to-all-start.1 = ((f32[8,8,128]{2,1,0:T(8,128)}), f32[8,8,128]{2,1,0:T(8,128)S(1)}, u32[]{:S(2)}, u32[]{:S(2)}) async-start(f32[8,8,128]{2,1,0:T(8,128)} %bitcast.4), calls=%async_computation.1 | async-start | bytes 65536 | tf_op jit(solution)/shard_map/all_to_all | solution.py:453
  63.8 1.9 %copy-start = (bf16[640,2560]{1,0:T(8,128)(2,1)S(1)}, bf16[640,2560]{1,0:T(8,128)(2,1)}, u32[]{:S(2)}) copy-start(bf16[640,2560]{1,0:T(8,128)(2,1)} %w.1) | copy-start | bytes 9830404
  65.7 1.3 %copy-start.11 = (f32[8,80,512]{2,1,0:T(8,128)S(1)}, f32[8,80,512]{2,1,0:T(8,128)}, u32[]{:S(2)}) copy-start(f32[8,80,512]{2,1,0:T(8,128)} %copy-done.10) | copy-start | bytes 3932164
  67.1 0.9 copy-start.20
  73.0 1.1 copy-start.12
  74.9 23.4 %all-to-all-start.2 = ((f32[64,8,128]{2,1,0:T(8,128)}), f32[64,8,128]{2,1,0:T(8,128)S(1)}, u32[]{:S(2)}, u32[]{:S(2)}) async-start(f32[64,8,128]{2,1,0:T(8,128)} %bitcast.5), calls=%async_computation.2 | async-start | bytes 524288 | tf_op jit(solution)/shard_map/all_to_all | solution.py:438
  85.9 1.3 %copy-start.13 = (f32[8,80,512]{2,1,0:T(8,128)S(1)}, f32[8,80,512]{2,1,0:T(8,128)}, u32[]{:S(2)}) copy-start(f32[8,80,512]{2,1,0:T(8,128)} %copy-done.12) | copy-start | bytes 3932164
  87.2 1.1 copy-start.15
  94.4 26.2 %collective-permute-start.6 = (bf16[8,160,128]{2,1,0:T(8,128)(2,1)S(1)}, bf16[8,160,128]{2,1,0:T(8,128)(2,1)S(1)}, u32[]{:S(2)}, u32[]{:S(2)}) collective-permute-start(bf16[8,160,128]{2,1,0:T(8,128)(2,1)S(1)} %get-tuple-element.46), channel_id=1, source_target_pairs={{4,0},{8,4},{12,8},{20,16},{24,20},{28,24},{36,32},{40,36},{44,40}... | collective-permute-start | bytes 983048 | tf_op jit(solution)/shard_map/ppermute | solution.py:407
  95.6 30.3 %collective-permute-start.7 = (bf16[8,160,128]{2,1,0:T(8,128)(2,1)S(1)}, bf16[8,160,128]{2,1,0:T(8,128)(2,1)S(1)}, u32[]{:S(2)}, u32[]{:S(2)}) collective-permute-start(bf16[8,160,128]{2,1,0:T(8,128)(2,1)S(1)} %get-tuple-element.47), channel_id=1, source_target_pairs={{8,0},{12,4},{24,16},{28,20},{40,32},{44,36},{56,48},{60,52},{72,6... | collective-permute-start | bytes 983048 | tf_op jit(solution)/shard_map/ppermute | solution.py:407
  96.9 29.0 %collective-permute-start.8 = (bf16[8,160,128]{2,1,0:T(8,128)(2,1)S(1)}, bf16[8,160,128]{2,1,0:T(8,128)(2,1)S(1)}, u32[]{:S(2)}, u32[]{:S(2)}) collective-permute-start(bf16[8,160,128]{2,1,0:T(8,128)(2,1)S(1)} %get-tuple-element.48), channel_id=1, source_target_pairs={{12,0},{28,16},{44,32},{60,48},{76,64},{92,80},{108,96},{124,112},... | collective-permute-start | bytes 983048 | tf_op jit(solution)/shard_map/ppermute | solution.py:407
  98.3 1.0 copy-start.18
  99.2 0.9 copy-start.22
  100.1 11.3 %copy-start.16 = (bf16[640,512]{1,0:T(8,128)(2,1)S(1)}, bf16[640,512]{1,0:T(8,128)(2,1)}, u32[]{:S(2)}) copy-start(bf16[640,512]{1,0:T(8,128)(2,1)} %copy-done.14) | copy-start | bytes 1966084
  102.3 23.8 %all-to-all-start.3 = ((f32[8,8,256]{2,1,0:T(8,128)}), f32[8,8,256]{2,1,0:T(8,128)S(1)}, u32[]{:S(2)}, u32[]{:S(2)}) async-start(f32[8,8,256]{2,1,0:T(8,128)} %bitcast.6), calls=%async_computation.3 | async-start | bytes 131072 | tf_op jit(solution)/shard_map/all_to_all | solution.py:483
  111.4 1.6 %copy-start.9 = (bf16[8,256,512]{2,1,0:T(8,128)(2,1)S(1)}, bf16[8,256,512]{2,1,0:T(8,128)(2,1)}, u32[]{:S(2)}) copy-start(bf16[8,256,512]{2,1,0:T(8,128)(2,1)} %copy-done.7) | copy-start | bytes 6291460
  118.6 1.9 %copy-start.5 = (f32[8,240,512]{2,1,0:T(8,128)}, f32[8,240,512]{2,1,0:T(8,128)S(1)}, u32[]{:S(2)}) copy-start(f32[8,240,512]{2,1,0:T(8,128)S(1)} %local_backward.1.grads) | copy-start | bytes 11796484
  126.2 2.1 %copy-start.6 = (f32[8,240,512]{2,1,0:T(8,128)S(1)}, f32[8,240,512]{2,1,0:T(8,128)}, u32[]{:S(2)}) copy-start(f32[8,240,512]{2,1,0:T(8,128)} %copy-done.5) | copy-start | bytes 11796484
  (4 other events, 2.9 us)

commit v2 on v1

v2 whole, which is shorter than its diff:
```python
import functools
import math

import jax
import jax.numpy as jnp
from jax import lax
from jax.experimental import pallas as pl
from jax.experimental.pallas import tpu as pltpu
from jax.sharding import PartitionSpec as P

NEAR = 4
F32 = jnp.float32
BF16 = jnp.bfloat16
LOG2E = math.log2(math.e)
NEG = float("-inf")


def nn(a, b):
    return lax.dot_general(a, b, (((1,), (0,)), ((), ())), preferred_element_type=F32)


def nt(a, b):
    return lax.dot_general(a, b, (((1,), (1,)), ((), ())), preferred_element_type=F32)


def tn(a, b):
    return lax.dot_general(a, b, (((0,), (0,)), ((), ())), preferred_element_type=F32)


def iota(shape, dim):
    return lax.broadcasted_iota(jnp.int32, shape, dim)


def one_hot(mask):
    return jnp.where(mask, 1.0, 0.0).astype(BF16)


def pick_matrix(tokens, count, offset):
    rate = tokens // count
    return one_hot(iota((tokens, count), 0) == iota((tokens, count), 1) * rate + offset)


def place_matrix(tokens, count, offset, rows=None):
    rate = tokens // count
    rows = rows or count
    return one_hot(iota((rows, tokens), 1) == iota((rows, tokens), 0) * rate + offset)


def split3(x):
    high = x.astype(BF16).astype(F32)
    rest = x - high
    middle = rest.astype(BF16).astype(F32)
    return high, middle, rest - middle


def log2_add(a, b):
    top = jnp.maximum(a, b)
    return top + jnp.log(jnp.exp2(a - top) + jnp.exp2(b - top)) * LOG2E


def causal_mask(size):
    return iota((size, size), 0) <= iota((size, size), 1)


def halves(tokens):
    half = tokens // 2
    return half, ((0, slice(0, half)), (1, slice(half, tokens)))


def forward(qt, kt, vt, factor, diag):
    tokens = qt.shape[1]
    half, blocks = halves(tokens)
    outs, norms = [], []
    for index, cols in blocks:
        keys = (index + 1) * half
        scores = tn(kt[:, :keys], qt[:, cols])
        last = jnp.where(diag, scores[keys - half :], NEG)
        parts = [last] if index == 0 else [scores[:half], last]
        top = functools.reduce(
            jnp.maximum, [jnp.max(part, axis=0, keepdims=True) for part in parts]
        )
        top = top * factor
        probs = [jnp.exp2(part * factor - top) for part in parts]
        total = sum(jnp.sum(part, axis=0, keepdims=True) for part in probs)
        packed = [part.astype(BF16) for part in probs]
        packed = packed[0] if index == 0 else jnp.concatenate(packed, axis=0)
        outs.append(nn(vt[:, :keys], packed) / total)
        norms.append(top + jnp.log(total) * LOG2E)
    return jnp.concatenate(outs, axis=1), jnp.concatenate(norms, axis=1)


def backward(qt, kt, vt, gt, norm, delta, factor, scale, diag):
    tokens = qt.shape[1]
    half, blocks = halves(tokens)
    dq = []
    for index, cols in blocks:
        keys = (index + 1) * half
        scores = tn(kt[:, :keys], qt[:, cols]) * factor - norm[:, cols]
        last = jnp.where(diag, jnp.exp2(scores[keys - half :]), 0.0)
        if index == 0:
            probs = last
        else:
            probs = jnp.concatenate([jnp.exp2(scores[:half]), last], axis=0)
        dprobs = tn(vt[:, :keys], gt[:, cols])
        dscores = (probs * (dprobs - delta[:, cols])).astype(BF16)
        dq.append(nn(kt[:, :keys], dscores) * scale)
        dk_part = nt(qt[:, cols], dscores) * scale
        dv_part = nt(gt[:, cols], probs.astype(BF16))
        if index == 0:
            dk, dv = dk_part, dv_part
        else:
            dk = jnp.concatenate([dk + dk_part[:, :half], dk_part[:, half:]], axis=1)
            dv = jnp.concatenate([dv + dv_part[:, :half], dv_part[:, half:]], axis=1)
    return jnp.concatenate(dq, axis=1), dk, dv


def fetch(src, dst, sem):
    copy = pltpu.make_async_copy(src, dst, sem)
    copy.start()
    return copy


def both_halves(pairs, sems, size):
    return [
        [
            fetch(src.at[pl.ds(i * size, size)], dst.at[pl.ds(i * size, size)], sems.at[i, j])
            for j, (src, dst) in enumerate(pairs)
        ]
        for i in range(2)
    ]


def wait_all(copies):
    for copy in copies:
        copy.wait()


def my_offsets(offsets, heads):
    mine = lax.axis_index("seq") % heads
    return offsets[0, mine], offsets[1, mine]


def sum3(x, first, axis):
    if axis == 0:
        return x[first : first + 1] + x[first + 1 : first + 2] + x[first + 2 : first + 3]
    return x[:, first : first + 1] + x[:, first + 1 : first + 2] + x[:, first + 2 : first + 3]


def local_kernel(
    heads, factor, offsets, q, k, v, qkvt, msg, out, norm, raw, turned, res, sems, out_sems
):
    tokens, width = q.shape
    d = width // heads
    loads = [fetch(ref, raw.at[i], sems.at[i]) for i, ref in enumerate((q, k, v))]
    stores = []
    for slot in range(3):
        loads[slot].wait()
        turned[slot] = raw[slot].T
        stores.append(fetch(turned.at[slot], qkvt.at[slot], out_sems.at[slot]))
    diag = causal_mask(tokens // 2)
    for h in range(heads):
        rows = slice(h * d, (h + 1) * d)
        block = jnp.concatenate([turned[0, rows], turned[1, rows], turned[2, rows]], axis=0)
        near = nn(block, pick_matrix(tokens, tokens // NEAR, offsets[0, h]))
        msg[h, : 3 * d] = near.astype(BF16)
        picked = nt(place_matrix(tokens, 8, offsets[1, h], 16), block)[:8]
        tail = jnp.concatenate([picked[:, 128:], jnp.zeros((8, 256 - 3 * d), F32)], axis=1)
        msg[h, 3 * d :] = jnp.concatenate([picked[:, :128], tail], axis=0).astype(BF16)
        o, n = forward(block[:d], block[d : 2 * d], block[2 * d :], factor, diag)
        res[rows] = o.astype(BF16)
        norm[h : h + 1, :] = n
    stores.append(fetch(res, out, out_sems.at[3]))
    wait_all(stores)


def stats_kernel(
    heads, d, offsets, w, c0, c1, c2, c3, l_out, l_norm, gt, msg,
    w_buf, c_buf, l_buf, g_buf, sems, out_sems,
):
    tokens, width = c0.shape
    count = tokens // NEAR
    head = lax.axis_index("head")
    loads = []
    for flip, ref in enumerate((c0, c1, c2, c3)):
        first = pl.multiple_of(jnp.bitwise_xor(head, flip) * width, 128)
        loads.append(fetch(w.at[:, pl.ds(first, width)], w_buf.at[flip], sems.at[flip]))
        loads.append(fetch(ref, c_buf.at[flip], sems.at[4 + flip]))
    loads.append(fetch(l_out, l_buf, sems.at[8]))
    wait_all(loads[:4])
    grads = nt(w_buf[0], c_buf[0]) + nt(w_buf[1], c_buf[1])
    wait_all(loads[4:])
    grads = grads + nt(w_buf[2], c_buf[2]) + nt(w_buf[3], c_buf[3])
    grads = grads.astype(BF16)
    g_buf[...] = grads
    store = fetch(g_buf, gt, out_sems.at[0])
    for h in range(heads):
        rows = slice(h * d, (h + 1) * d)
        g = grads[rows].astype(F32)
        product = jnp.sum(g * l_buf[rows].astype(F32), axis=0, keepdims=True)
        stack = jnp.concatenate(
            [
                g,
                *split3(l_norm[h : h + 1, :]),
                *split3(product),
                jnp.zeros((122 - d, tokens), F32),
            ],
            axis=0,
        ).astype(BF16)
        near = nn(stack[:96], pick_matrix(tokens, count, offsets[0, h]))
        far = nt(place_matrix(tokens, 8, offsets[1, h], 16), stack)
        msg[h] = jnp.concatenate([near, far], axis=0).astype(BF16)
    store.wait()


def segment(got, first, size, part):
    pieces = [got[4 * part + z, first : first + size, :] for z in range(NEAR)]
    return jnp.concatenate(pieces, axis=1)


def near_forward_kernel(d, factor, got, msg, norm):
    tokens = NEAR * got.shape[2]
    diag = causal_mask(tokens // 2)
    for part in range(2):
        qt, kt, vt = [segment(got, i * d, d, part) for i in range(3)]
        o, n = forward(qt, kt, vt, factor, diag)
        norm[part : part + 1, :] = n
        gap = jnp.zeros((6, tokens), F32)
        rest = jnp.zeros((87 - d, tokens), F32)
        stack = jnp.concatenate([o, gap, *split3(n), rest], axis=0).astype(BF16)
        for z in range(NEAR):
            msg[4 * part + z] = stack[:, z * 128 : (z + 1) * 128]


def far_block(got):
    rows = got[...].astype(F32)
    tokens = rows.shape[0] * 8
    wide = jnp.concatenate(
        [rows[:, :8].reshape(tokens, 128), rows[:, 8:].reshape(tokens, 128)], axis=1
    )
    return wide.T.astype(BF16)


def column_rows():
    return pl.ds(pl.multiple_of(lax.axis_index("seq") // 8 * 64, 64), 64)


def far_forward_kernel(d, factor, got, stats, near, norm, msg, turned):
    block = far_block(got)
    tokens = block.shape[1]
    diag = causal_mask(tokens // 2)
    o, n = forward(block[:d], block[d : 2 * d], block[2 * d : 3 * d], factor, diag)
    norm[...] = jnp.broadcast_to(n, norm.shape)
    stack = jnp.concatenate([o, *split3(n), jnp.zeros((125 - d, tokens), F32)], axis=0)
    turned[...] = stack.T
    mine = turned[column_rows(), :].reshape(8, 8, 128)
    msg[:, :d] = stats[:, :d]
    msg[:, d : 2 * d] = near[:, :d]
    both = stats[:, d : d + 16].astype(F32) + near[:, d:].astype(F32)
    msg[:, 2 * d : 2 * d + 16] = both.astype(BF16)
    far = stats[:, d + 16 :].astype(F32)[:, :8]
    msg[:, 2 * d + 16 :] = jnp.concatenate([far, mine], axis=1).astype(BF16)


def overlap(near_offset, far_offset):
    shift = far_offset - near_offset
    spot = iota((8, 128), 0) * 16 + lax.shift_right_arithmetic(shift, 2)
    return (iota((8, 128), 1) == spot) & (lax.bitwise_and(shift, 3) == 0)


def near_stats(d, stats, outs, part):
    g = segment(stats, 0, d, part).astype(F32)
    rest = segment(stats, 2 * d, 16, part).astype(F32)
    o = segment(outs, d, d, part).astype(F32)
    product = jnp.sum(g * o, axis=0, keepdims=True)
    return g, sum3(rest, 0, 0), sum3(rest, 3, 0), product


def owner_stats_kernel(heads, d, offsets, stats, outs, near_norm, msg):
    near_offset, far_offset = my_offsets(offsets, heads)
    same = overlap(near_offset, far_offset)
    hit = jnp.max(jnp.where(same, 1.0, 0.0), axis=1, keepdims=True) > 0.5
    lane = iota((8, 128), 1)
    for part in range(2):
        _, _, _, product = near_stats(d, stats, outs, part)
        for z in range(NEAR):
            cols = slice(z * 128, (z + 1) * 128)
            near_log = near_norm[part : part + 1, cols]
            near_log = jnp.sum(jnp.where(same, near_log, 0.0), axis=1, keepdims=True)
            near_log = jnp.where(hit, near_log, NEG)
            near_dot = jnp.sum(jnp.where(same, product[:, cols], 0.0), axis=1, keepdims=True)
            rows = stats[4 * part + z, 2 * d + 16 :, :].astype(F32)[:8]
            mine = sum3(rows, d, 1)
            both = log2_add(mine, near_log)
            dot = jnp.exp2(mine - both) * sum3(rows, d + 3, 1)
            dot = dot + jnp.exp2(near_log - both) * near_dot
            for i, term in enumerate([*split3(both), *split3(dot)]):
                rows = jnp.where(lane == d + i, term, rows)
            rows = jnp.concatenate([rows, jnp.zeros_like(rows)], axis=0).astype(BF16)
            for copy in range(msg.shape[0]):
                msg[copy, 4 * part + z] = rows


def near_backward_kernel(heads, d, factor, scale, offsets, got, stats, outs, near_norm, msg):
    near_offset, far_offset = my_offsets(offsets, heads)
    same = overlap(near_offset, far_offset)
    hit = jnp.max(jnp.where(same, 1.0, 0.0), axis=0, keepdims=True) > 0.5
    tokens = near_norm.shape[1]
    diag = causal_mask(tokens // 2)
    for part in range(2):
        g, local_norm, local_dot, near_dot = near_stats(d, stats, outs, part)
        far_norms, far_dots = [], []
        for z in range(NEAR):
            rows = outs[4 * part + z, 2 * d + 16 :, :].astype(F32)[8:]
            grads = stats[4 * part + z, 2 * d + 16 :, :].astype(F32)[:8]
            dot = jnp.sum(jnp.where(iota((8, 128), 1) < d, rows * grads, 0.0), axis=1, keepdims=True)
            log = jnp.sum(jnp.where(same, sum3(rows, d, 1), 0.0), axis=0, keepdims=True)
            far_norms.append(jnp.where(hit, log, NEG))
            far_dots.append(jnp.sum(jnp.where(same, dot, 0.0), axis=0, keepdims=True))
        far_norm = jnp.concatenate(far_norms, axis=1)
        far_dot = jnp.concatenate(far_dots, axis=1)
        mine = near_norm[part : part + 1, :]
        norm = log2_add(log2_add(mine, local_norm), far_norm)
        delta = jnp.exp2(mine - norm) * near_dot + jnp.exp2(local_norm - norm) * local_dot
        delta = delta + jnp.exp2(far_norm - norm) * far_dot
        qt, kt, vt = [segment(got, i * d, d, part) for i in range(3)]
        grads = backward(qt, kt, vt, g.astype(BF16), norm, delta, factor, scale, diag)
        for slot in range(3):
            packed = grads[slot].astype(BF16)
            for z in range(NEAR):
                msg[4 * part + z, slot * d : (slot + 1) * d] = packed[:, z * 128 : (z + 1) * 128]


def far_backward_kernel(d, factor, scale, got, norm, stats, near, msg, turned):
    block = far_block(got)
    qt, kt, vt = block[:d], block[d : 2 * d], block[2 * d : 3 * d]
    tokens = block.shape[1]
    rows = stats[...].astype(F32)[:, :8].reshape(tokens, 128).T
    gt = rows[:d].astype(BF16)
    rest_norm = sum3(rows, d, 0)
    rest_dot = sum3(rows, d + 3, 0)
    mine = norm[:1, :]
    both = log2_add(mine, rest_norm)
    share = jnp.exp2(mine - both)
    rest = jnp.exp2(rest_norm - both) * rest_dot
    scores = tn(kt, qt) * factor - mine
    causal = iota((tokens, tokens), 0) <= iota((tokens, tokens), 1)
    probs = jnp.where(causal, jnp.exp2(scores), 0.0)
    dprobs = tn(vt, gt)
    delta = share * jnp.sum(probs * dprobs, axis=0, keepdims=True) + rest
    probs = probs * share
    dscores = (probs * (dprobs - delta)).astype(BF16)
    dq = nn(kt, dscores) * scale
    dk = nt(qt, dscores) * scale
    dv = nt(gt, probs.astype(BF16))
    stack = jnp.concatenate([dq, dk, dv, jnp.zeros((256 - 3 * d, tokens), F32)], axis=0)
    turned[...] = stack.T
    picked = turned[column_rows(), :]
    msg[:, : 3 * d] = near[...]
    msg[:, 3 * d :] = jnp.concatenate(
        [picked[:, :128].reshape(8, 8, 128), picked[:, 128:].reshape(8, 8, 128)], axis=1
    ).astype(BF16)


def local_backward_kernel(
    heads, d, factor, scale, offsets, qkvt, gt, l_out, l_norm, got, attended, grads,
    buf, o_buf, turned, rows_buf, sems, load_sems, out_sems,
):
    tokens = gt.shape[1]
    count = tokens // NEAR
    first = [fetch(l_out, o_buf, sems.at[0]), fetch(gt, buf.at[3], sems.at[1])]
    loads = [fetch(qkvt.at[i], buf.at[i], load_sems.at[i]) for i in range(3)]
    lane = iota((1, tokens), 1)
    diag = causal_mask(tokens // 2)
    wait_all(first)
    norms, deltas = [], []
    for h in range(heads):
        rows = slice(h * d, (h + 1) * d)
        near = nn(got[h, d : 2 * d + 16, :], place_matrix(tokens, count, offsets[0, h]))
        near_norm = jnp.where(lane % NEAR == offsets[0, h], sum3(near, d + 6, 0), NEG)
        place = iota((8, tokens), 1) == iota((8, tokens), 0) * 64 + offsets[1, h]
        came = got[h, 2 * d + 16 :, :].astype(F32)[8:]
        spread = jnp.sum(jnp.where(place, sum3(came, d, 1), 0.0), axis=0, keepdims=True)
        far_norm = jnp.where(lane % 64 == offsets[1, h], spread, NEG)
        far_out = tn(came[:, :d].astype(BF16), one_hot(place))
        mine = l_norm[h : h + 1, :]
        both = log2_add(log2_add(mine, near_norm), far_norm)
        mixed = jnp.exp2(mine - both) * o_buf[rows].astype(F32)
        mixed = mixed + jnp.exp2(near_norm - both) * near[:d]
        mixed = (mixed + jnp.exp2(far_norm - both) * far_out).astype(BF16)
        turned[rows, :] = mixed
        delta = buf[3, rows].astype(F32) * mixed.astype(F32)
        norms.append(both)
        deltas.append(jnp.sum(delta, axis=0, keepdims=True))
    rows_buf[...] = turned[...].T
    store = fetch(rows_buf, attended, out_sems.at[0])
    wait_all(loads)
    for h in range(heads):
        rows = slice(h * d, (h + 1) * d)
        parts = backward(
            buf[0, rows], buf[1, rows], buf[2, rows], buf[3, rows],
            norms[h], deltas[h], factor, scale, diag,
        )
        for slot in range(3):
            grads[slot, rows] = parts[slot].astype(grads.dtype)
    store.wait()


def final_kernel(heads, d, offsets, grads, got, dq, dk, dv, turned, rows_buf, out_sems):
    tokens = grads.shape[2]
    count = tokens // NEAR
    for h in range(heads):
        rows = slice(h * d, (h + 1) * d)
        total = nn(got[h, : 3 * d], place_matrix(tokens, count, offsets[0, h]))
        place = one_hot(iota((8, tokens), 1) == iota((8, tokens), 0) * 64 + offsets[1, h])
        far = got[h, 3 * d :].astype(F32)
        far = jnp.concatenate([far[:8], far[8:]], axis=1).astype(BF16)
        total = total + tn(far, place)[: 3 * d]
        for slot in range(3):
            mine = total[slot * d : (slot + 1) * d] + grads[slot, rows].astype(F32)
            turned[slot, rows, :] = mine.astype(BF16)
    stores = []
    for slot, ref in enumerate((dq, dk, dv)):
        rows_buf[slot] = turned[slot].T
        stores.append(fetch(rows_buf.at[slot], ref, out_sems.at[slot]))
    wait_all(stores)


def call(kernel, name, operands, outs, scratch=(), limit=63_000_000):
    spaces = {"s": pltpu.SMEM, "v": pltpu.VMEM, "h": pltpu.HBM}
    arrays = [x for x, _ in operands]
    shapes = [x for x, _ in outs]
    return pl.pallas_call(
        kernel,
        name=name,
        out_shape=shapes,
        in_specs=[pl.BlockSpec(memory_space=spaces[where]) for _, where in operands],
        out_specs=[pl.BlockSpec(memory_space=spaces[where]) for _, where in outs],
        scratch_shapes=list(scratch),
        compiler_params=pltpu.CompilerParams(vmem_limit_bytes=limit),
        cost_estimate=pl.CostEstimate(flops=1000, bytes_accessed=1000, transcendentals=0),
    )(*arrays)


def after(x, y):
    return lax.optimization_barrier((x, y))[0]


def on_device(query_rows, key_rows, value_rows, out_weight, cotangent, offsets):
    tokens, width = query_rows.shape
    heads = offsets.shape[1]
    d = width // heads
    scale = 1.0 / math.sqrt(d)
    factor = scale * LOG2E
    seq_size = lax.axis_size("seq")
    count = tokens // NEAR
    groups = seq_size // heads
    columns = [[a * heads + z for z in range(heads)] for a in range(groups)]
    planes = [[a * heads + z for a in range(groups)] for z in range(heads)]
    struct = jax.ShapeDtypeStruct
    dma = pltpu.SemaphoreType.DMA

    def vmem(*shape, dtype=BF16):
        return pltpu.VMEM(shape, dtype)

    def along_column(x):
        return lax.all_to_all(x, "seq", 0, 0, tiled=True, axis_index_groups=columns)

    def over_plane(copies):
        got = lax.all_to_all(copies, "seq", 0, 0, tiled=True, axis_index_groups=planes)
        return got.reshape(seq_size, *copies.shape[2:])

    def flipped(x, bit):
        return lax.ppermute(x, "head", [(i, i ^ bit) for i in range(4)])

    c2 = flipped(cotangent, 2)
    qkvt, rows_msg, l_out, l_norm = call(
        functools.partial(local_kernel, heads, factor),
        "local_forward",
        [(offsets, "s"), (query_rows, "h"), (key_rows, "h"), (value_rows, "h")],
        [
            (struct((3, width, tokens), BF16), "h"),
            (struct((heads, 256, count), BF16), "v"),
            (struct((width, tokens), BF16), "h"),
            (struct((heads, tokens), F32), "v"),
        ],
        scratch=[
            vmem(3, tokens, width),
            vmem(3, width, tokens),
            vmem(width, tokens),
            dma((3,)),
            dma((4,)),
        ],
    )
    rows_got = along_column(rows_msg)
    c2 = after(c2, l_norm)
    c3 = flipped(c2, 1)
    c1 = flipped(after(cotangent, l_norm), 1)
    gt, stats_msg = call(
        functools.partial(stats_kernel, heads, d),
        "stats",
        [(offsets, "s"), (out_weight, "h")]
        + [(x, "h") for x in (cotangent, c1, c2, c3)]
        + [(l_out, "h"), (l_norm, "v")],
        [
            (struct((width, tokens), BF16), "h"),
            (struct((heads, 112, 128), BF16), "v"),
        ],
        scratch=[
            vmem(4, width, width),
            vmem(4, tokens, width),
            vmem(width, tokens),
            vmem(width, tokens),
            dma((9,)),
            dma((1,)),
        ],
    )
    rows_got = after(rows_got, stats_msg)
    far_rows = rows_got[:, 3 * d :]
    far_got = over_plane(jnp.broadcast_to(far_rows[None], (groups, *far_rows.shape)))
    near_out, near_norm = call(
        functools.partial(near_forward_kernel, d, factor),
        "near_forward",
        [(rows_got, "v")],
        [(struct((heads, 96, count), BF16), "v"), (struct((2, tokens), F32), "v")],
        limit=16_000_000,
    )
    far_norm, swap_msg = call(
        functools.partial(far_forward_kernel, d, factor),
        "far_forward",
        [(far_got, "v"), (stats_msg, "v"), (near_out, "v")],
        [(struct((8, tokens), F32), "v"), (struct((heads, 192, 128), BF16), "v")],
        scratch=[vmem(tokens, 128, dtype=F32)],
        limit=16_000_000,
    )
    swap_got = along_column(swap_msg)
    (far_msg,) = call(
        functools.partial(owner_stats_kernel, heads, d),
        "owner_stats",
        [(offsets, "s"), (swap_got, "v"), (swap_msg, "v"), (near_norm, "v")],
        [(struct((groups, heads, 16, 128), BF16), "v")],
        limit=16_000_000,
    )
    far_stats = over_plane(far_msg)
    (near_msg,) = call(
        functools.partial(near_backward_kernel, heads, d, factor, scale),
        "near_backward",
        [(offsets, "s"), (rows_got, "v"), (swap_got, "v"), (swap_msg, "v"), (near_norm, "v")],
        [(struct((heads, 3 * d, count), BF16), "v")],
        limit=16_000_000,
    )
    (grad_msg,) = call(
        functools.partial(far_backward_kernel, d, factor, scale),
        "far_backward",
        [(far_got, "v"), (far_norm, "v"), (far_stats, "v"), (near_msg, "v")],
        [(struct((heads, 256, 128), BF16), "v")],
        scratch=[vmem(tokens, 256, dtype=F32)],
        limit=16_000_000,
    )
    owner_grads = along_column(grad_msg)
    swap_got = after(swap_got, grad_msg)
    attended, grads = call(
        functools.partial(local_backward_kernel, heads, d, factor, scale),
        "local_backward",
        [(offsets, "s"), (qkvt, "h"), (gt, "h"), (l_out, "h"), (l_norm, "v"), (swap_got, "v")],
        [
            (struct((tokens, width), BF16), "h"),
            (struct((3, width, tokens), BF16), "v"),
        ],
        scratch=[
            vmem(4, width, tokens),
            vmem(width, tokens),
            vmem(width, tokens),
            vmem(tokens, width),
            dma((2,)),
            dma((3,)),
            dma((1,)),
        ],
    )
    grad_query, grad_key, grad_value = call(
        functools.partial(final_kernel, heads, d),
        "final",
        [(offsets, "s"), (grads, "v"), (owner_grads, "v")],
        [(struct((tokens, width), BF16), "h")] * 3,
        scratch=[
            vmem(3, width, tokens),
            vmem(3, tokens, width),
            dma((3,)),
        ],
        limit=16_000_000,
    )
    return (attended, grad_query, grad_key, grad_value)


def solution(mesh):
    return jax.shard_map(
        on_device,
        mesh=mesh,
        in_specs=(
            P("seq", "head"),
            P("seq", "head"),
            P("seq", "head"),
            P("head", None),
            P("seq", "head"),
            P(None, "head"),
        ),
        out_specs=(P("seq", "head"), P("seq", "head"), P("seq", "head"), P("seq", "head")),
        check_vma=False,
    )
```

time: 132 us -> 104 us (0.79)
  starting transfers between devices: 51.9 us -> 25.5 us
  local copies, waits for them, and re-layouts: 25.9 us -> 4.09 us
  blocking collectives: 0 us -> 15.3 us
  Pallas kernels: 33.8 us -> 37.5 us
    unnamed x46 -> x18, local copies, waits for them, and re-layouts: 25.2 us -> 3.35 us
    all_to_all x0 -> x1, blocking collectives: none -> 15.3 us  [along_column(): return lax.all_to_all(x, 'seq', 0, 0, tiled=True, axis_index_groups=columns)]
    ppermute x9 -> x3, starting transfers between devices: 18.1 us -> 2.95 us  [flipped(): return lax.ppermute(x, 'head', [(i, i ^ bit) for i in range(4)])]
    all_to_all x4, starting transfers between devices: 33.8 us -> 22.5 us  [the longest x2 12 us: along_column(): return lax.all_to_all(x, 'seq', 0, 0, tiled=True, axis_index_groups=columns)]
    all_to_all x4, waiting for transfers between devices: 13.4 us -> 17.6 us  [the longest x2 9.4 us: along_column(): return lax.all_to_all(x, 'seq', 0, 0, tiled=True, axis_index_groups=columns)]
    pallas_call x9, Pallas kernels: 33.8 us -> 37.5 us  [call(): pl.pallas_call(kernel, name=name, out_shape=shapes, in_specs=[pl.BlockSpe...]
    ppermute x9 -> x3, waiting for transfers between devices: 5.49 us -> 2.52 us  [flipped(): return lax.ppermute(x, 'head', [(i, i ^ bit) for i in range(4)])]
  transfers between devices with their start and end apart: 13 -> 7, of which waited for: 3 -> 6; matrix products, arithmetic and copies ran while one was open for 1% -> 0% of each run, Pallas kernels for 23% -> 29%
where the time goes in v2:
time: 104 us; the launch traced here: 103 us
  Pallas kernels  37.5 us (36%)
  starting transfers between devices  25.5 us (25%)
  waiting for transfers between devices  20.1 us (19%)
  blocking collectives  15.3 us (15%)
  local copies, waits for them, and re-layouts  4.09 us (4%)
    pallas_call x9, Pallas kernels, call(): pl.pallas_call(kernel, name=name, out_shape=shapes, in_specs=[pl.BlockSpe...  37.5 us
    all_to_all x1, blocking collectives, along_column(): return lax.all_to_all(x, 'seq', 0, 0, tiled=True, axis_index_groups=columns)  15.3 us
    all_to_all x2, starting transfers between devices, along_column(): return lax.all_to_all(x, 'seq', 0, 0, tiled=True, axis_index_groups=columns)  12 us
    all_to_all x2, starting transfers between devices, over_plane(): lax.all_to_all(copies, 'seq', 0, 0, tiled=True, axis_index_groups=planes)  10.6 us
    all_to_all x2, waiting for transfers between devices, along_column(): return lax.all_to_all(x, 'seq', 0, 0, tiled=True, axis_index_groups=columns)  9.4 us
    all_to_all x2, waiting for transfers between devices, over_plane(): lax.all_to_all(copies, 'seq', 0, 0, tiled=True, axis_index_groups=planes)  8.23 us
    unnamed x18, local copies, waits for them, and re-layouts  3.35 us
    ppermute x3, starting transfers between devices, flipped(): return lax.ppermute(x, 'head', [(i, i ^ bit) for i in range(4)])  2.95 us
  transfers between devices with their start and end apart: 7, of which 6 were waited for; matrix products, arithmetic and copies ran while one was open for 0% of the time, Pallas kernels for 29%

profile of v2, /device:TPU:8, one launch (start us, length us, event | category | flops | bytes accessed | tf_op | source)
XLA Modules:
  0.0 103.4 jit_solution(8109099939278963449)
XLA Ops:
  0.6 0.0 copy-start.5
  0.6 2.4 %collective-permute-start.1 = (bf16[512,640]{1,0:T(8,128)(2,1)}, bf16[512,640]{1,0:T(8,128)(2,1)S(1)}, u32[]{:S(2)}, u32[]{:S(2)}) collective-permute-start(bf16[512,640]{1,0:T(8,128)(2,1)} %c0.1), channel_id=1, source_target_pairs={{0,2},{1,3},{2,0},{3,1},{4,6},{5,7},{6,4},{7,5},{8,10},{9,11},{10,... | collective-permute-start | bytes 1966088 | tf_op jit(solution)/shard_map/ppermute | solution.py:473
  3.0 9.3 %local_forward.1 = (bf16[3,640,512]{2,1,0:T(8,128)(2,1)}, bf16[8,256,128]{2,1,0:T(8,128)(2,1)}, bf16[640,512]{1,0:T(8,128)(2,1)}, f32[8,512]{1,0:T(8,128)}) custom-call(s32[2,8]{1,0:T(2,128)} %offsets.11, bf16[512,640]{1,0:T(8,128)(2,1)} %q.1, bf16[512,640]{1,0:T(8,128)(2,1)} %k.1, bf16[512,640]{1,0:T(8,128)(2,1)} %v.1), custom_call_target="tpu_custom_call" | custom-call | flops 1000 | bytes 1000 | tf_op jit(solution)/shard_map/local_forward/pallas_call | solution.py:432
  12.3 8.5 %all-to-all-start = ((bf16[8,256,128]{2,1,0:T(8,128)(2,1)}), bf16[8,256,128]{2,1,0:T(8,128)(2,1)S(1)}, u32[]{:S(2)}, u32[]{:S(2)}) async-start(bf16[8,256,128]{2,1,0:T(8,128)(2,1)} %get-tuple-element.29), calls=%async_computation | async-start | bytes 1048576 | tf_op jit(solution)/shard_map/all_to_all | solution.py:466
  20.8 0.1 collective-permute-start
  20.9 0.0 collective-permute-done.1.c2
  20.9 0.0 copy-start.6
  20.9 0.5 collective-permute-start.2
  21.4 1.6 %collective-permute-done.c1 = bf16[512,640]{1,0:T(8,128)(2,1)S(1)} collective-permute-done((bf16[512,640]{1,0:T(8,128)(2,1)S(1)}, bf16[512,640]{1,0:T(8,128)(2,1)S(1)}, u32[]{:S(2)}, u32[]{:S(2)}) %collective-permute-start) | collective-permute-done | bytes 655392 | tf_op jit(solution)/shard_map/ppermute | solution.py:473
  23.0 0.9 collective-permute-done.2.c3
  23.9 0.8 copy-done.8
  24.8 6.6 %stats.1 = (bf16[640,512]{1,0:T(8,128)(2,1)}, bf16[8,112,128]{2,1,0:T(8,128)(2,1)}) custom-call(s32[2,8]{1,0:T(2,128)} %offsets.11, bf16[640,2560]{1,0:T(8,128)(2,1)} %w.1, bf16[512,640]{1,0:T(8,128)(2,1)} %c0.1, bf16[512,640]{1,0:T(8,128)(2,1)} %copy-done.7, bf16[512,640]{1,0:T(8,128)(2,1)} %copy-done.6, bf16[512,640]{1,0:T(8,128)(2,1)} %copy-done.8, ...), custom_call_target="tpu_custom_call" | custom-call | flops 1000 | bytes 1000 | tf_op jit(solution)/shard_map/stats/pallas_call | solution.py:432
  31.4 0.0 copy-start.3
  31.4 6.6 %all-to-all-done.got = bf16[8,256,128]{2,1,0:T(8,128)(2,1)S(1)} async-done(((bf16[8,256,128]{2,1,0:T(8,128)(2,1)}), bf16[8,256,128]{2,1,0:T(8,128)(2,1)S(1)}, u32[]{:S(2)}, u32[]{:S(2)}) %all-to-all-start) | async-done | bytes 524320 | tf_op jit(solution)/shard_map/all_to_all | solution.py:466
  38.0 0.7 broadcast_in_dim.2
  38.8 5.8 %all-to-all-start.1 = ((bf16[8,8,16,128]{3,2,1,0:T(8,128)(2,1)}), bf16[8,8,16,128]{3,2,1,0:T(8,128)(2,1)S(1)}, u32[]{:S(2)}, u32[]{:S(2)}) async-start(bf16[8,8,16,128]{3,2,1,0:T(8,128)(2,1)} %broadcast_in_dim.2), calls=%async_computation.1 | async-start | bytes 524288 | tf_op jit(solution)/shard_map/all_to_all | solution.py:469
  44.5 1.2 %near_forward.1 = (bf16[8,96,128]{2,1,0:T(8,128)(2,1)S(1)}, f32[2,512]{1,0:T(2,128)S(1)}) custom-call(bf16[8,256,128]{2,1,0:T(8,128)(2,1)S(1)} %all-to-all-done.got), custom_call_target="tpu_custom_call" | custom-call | flops 1000 | bytes 1000 | tf_op jit(solution)/shard_map/near_forward/pallas_call | solution.py:432
  45.7 4.6 %all-to-all-done.1 = bf16[8,8,16,128]{3,2,1,0:T(8,128)(2,1)S(1)} async-done(((bf16[8,8,16,128]{3,2,1,0:T(8,128)(2,1)}), bf16[8,8,16,128]{3,2,1,0:T(8,128)(2,1)S(1)}, u32[]{:S(2)}, u32[]{:S(2)}) %all-to-all-start.1) | async-done | bytes 262176 | tf_op jit(solution)/shard_map/all_to_all | solution.py:469
  50.3 0.9 copy-done.2
  51.3 0.8 far_forward.1
  52.1 15.3 %all_to_all.25.stats.got = bf16[8,192,128]{2,1,0:T(8,128)(2,1)S(1)} all-to-all(bf16[8,192,128]{2,1,0:T(8,128)(2,1)S(1)} %get-tuple-element.33.outs), channel_id=1, replica_groups={{0,4,8,12,16,20,24,28},{32,36,40,44,48,52,56,60},{64,68,72,76,80,84,88,..., dimensions={0} | all-to-all | bytes 786432 | tf_op jit(solution)/shard_map/all_to_all | solution.py:466
  67.4 1.7 %owner_stats.1 = bf16[8,8,16,128]{3,2,1,0:T(8,128)(2,1)} custom-call(s32[2,8]{1,0:T(2,128)S(1)} %copy-done.3, bf16[8,192,128]{2,1,0:T(8,128)(2,1)S(1)} %all_to_all.25.stats.got, bf16[8,192,128]{2,1,0:T(8,128)(2,1)S(1)} %get-tuple-element.33.outs, f32[2,512]{1,0:T(2,128)S(1)} %get-tuple-element.35.near_norm), custom_call_target="tpu_custom_call" | custom-call | flops 1000 | bytes 1000 | tf_op jit(solution)/shard_map/owner_stats/pallas_call | solution.py:432
  69.0 4.8 %all-to-all-start.3 = ((bf16[8,8,16,128]{3,2,1,0:T(8,128)(2,1)}), bf16[8,8,16,128]{3,2,1,0:T(8,128)(2,1)S(1)}, u32[]{:S(2)}, u32[]{:S(2)}) async-start(bf16[8,8,16,128]{3,2,1,0:T(8,128)(2,1)} %owner_stats.1), calls=%async_computation.3 | async-start | bytes 524288 | tf_op jit(solution)/shard_map/all_to_all | solution.py:469
  73.8 2.2 %near_backward.1.near = bf16[8,240,128]{2,1,0:T(8,128)(2,1)S(1)} custom-call(s32[2,8]{1,0:T(2,128)S(1)} %copy-done.3, bf16[8,256,128]{2,1,0:T(8,128)(2,1)S(1)} %all-to-all-done.got, bf16[8,192,128]{2,1,0:T(8,128)(2,1)S(1)} %all_to_all.25.stats.got, bf16[8,192,128]{2,1,0:T(8,128)(2,1)S(1)} %get-tuple-element.33.outs, f32[2,512]{1,0:T(2,128)S(1)} %get-tuple-element.35.near_norm), custom_call_target="tpu_custom_call" | custom-call | flops 1000 | bytes 1000 | tf_op jit(solution)/shard_map/near_backward/pallas_call | solution.py:432
  76.0 3.6 %all-to-all-done.3 = bf16[8,8,16,128]{3,2,1,0:T(8,128)(2,1)S(1)} async-done(((bf16[8,8,16,128]{3,2,1,0:T(8,128)(2,1)}), bf16[8,8,16,128]{3,2,1,0:T(8,128)(2,1)S(1)}, u32[]{:S(2)}, u32[]{:S(2)}) %all-to-all-start.3) | async-done | bytes 262176 | tf_op jit(solution)/shard_map/all_to_all | solution.py:469
  79.6 2.2 %far_backward.1 = bf16[8,256,128]{2,1,0:T(8,128)(2,1)} custom-call(bf16[64,16,128]{2,1,0:T(8,128)(2,1)S(1)} %bitcast.3, f32[8,512]{1,0:T(8,128)S(1)} %get-tuple-element.34.norm, bf16[64,16,128]{2,1,0:T(8,128)(2,1)S(1)} %bitcast.4, bf16[8,240,128]{2,1,0:T(8,128)(2,1)S(1)} %near_backward.1.near), custom_call_target="tpu_custom_call" | custom-call | flops 1000 | bytes 1000 | tf_op jit(solution)/shard_map/far_backward/pallas_call | solution.py:432
  81.8 3.5 %all-to-all-start.4 = ((bf16[8,256,128]{2,1,0:T(8,128)(2,1)}), bf16[8,256,128]{2,1,0:T(8,128)(2,1)S(1)}, u32[]{:S(2)}, u32[]{:S(2)}) async-start(bf16[8,256,128]{2,1,0:T(8,128)(2,1)} %far_backward.1), calls=%async_computation.4 | async-start | bytes 1048576 | tf_op jit(solution)/shard_map/all_to_all | solution.py:466
  85.3 0.0 copy-start.4
  85.4 10.4 %local_backward.1 = (bf16[512,640]{1,0:T(8,128)(2,1)}, bf16[3,640,512]{2,1,0:T(8,128)(2,1)}) custom-call(s32[2,8]{1,0:T(2,128)} %offsets.11, bf16[3,640,512]{2,1,0:T(8,128)(2,1)} %get-tuple-element.23.qkvt, bf16[640,512]{1,0:T(8,128)(2,1)} %get-tuple-element.28.gt, bf16[640,512]{1,0:T(8,128)(2,1)} %get-tuple-element.27.l_out, ...), custom_call_target="tpu_custom_call" | custom-call | flops 1000 | bytes 1000 | tf_op jit(solution)/shard_map/local_backward/pallas_call | solution.py:432
  95.8 2.8 %all-to-all-done.4.got = bf16[8,256,128]{2,1,0:T(8,128)(2,1)S(1)} async-done(((bf16[8,256,128]{2,1,0:T(8,128)(2,1)}), bf16[8,256,128]{2,1,0:T(8,128)(2,1)S(1)}, u32[]{:S(2)}, u32[]{:S(2)}) %all-to-all-start.4) | async-done | bytes 524320 | tf_op jit(solution)/shard_map/all_to_all | solution.py:466
  98.5 1.5 %copy-done.1 = bf16[3,640,512]{2,1,0:T(8,128)(2,1)S(1)} copy-done((bf16[3,640,512]{2,1,0:T(8,128)(2,1)S(1)}, bf16[3,640,512]{2,1,0:T(8,128)(2,1)}, u32[]{:S(2)}) %copy-start.1) | copy-done | bytes 1966104
  100.1 3.1 %final.1 = (bf16[512,640]{1,0:T(8,128)(2,1)}, bf16[512,640]{1,0:T(8,128)(2,1)}, bf16[512,640]{1,0:T(8,128)(2,1)}) custom-call(s32[2,8]{1,0:T(2,128)S(1)} %copy-done.4, bf16[3,640,512]{2,1,0:T(8,128)(2,1)S(1)} %copy-done.1, bf16[8,256,128]{2,1,0:T(8,128)(2,1)S(1)} %all-to-all-done.4.got), custom_call_target="tpu_custom_call" | custom-call | flops 1000 | bytes 1000 | tf_op jit(solution)/shard_map/final/pallas_call | solution.py:432
  (12 shorter events, 0.0 us)
Async XLA Ops:
  0.6 20.2 %copy-start.5 = (bf16[512,640]{1,0:T(8,128)(2,1)S(1)}, bf16[512,640]{1,0:T(8,128)(2,1)}, u32[]{:S(2)}) copy-start(bf16[512,640]{1,0:T(8,128)(2,1)} %c0.1) | copy-start | bytes 1966084
  0.6 20.3 %collective-permute-start.1 = (bf16[512,640]{1,0:T(8,128)(2,1)}, bf16[512,640]{1,0:T(8,128)(2,1)S(1)}, u32[]{:S(2)}, u32[]{:S(2)}) collective-permute-start(bf16[512,640]{1,0:T(8,128)(2,1)} %c0.1), channel_id=1, source_target_pairs={{0,2},{1,3},{2,0},{3,1},{4,6},{5,7},{6,4},{7,5},{8,10},{9,11},{10,... | collective-permute-start | bytes 1966088 | tf_op jit(solution)/shard_map/ppermute | solution.py:473
  12.3 25.7 %all-to-all-start = ((bf16[8,256,128]{2,1,0:T(8,128)(2,1)}), bf16[8,256,128]{2,1,0:T(8,128)(2,1)S(1)}, u32[]{:S(2)}, u32[]{:S(2)}) async-start(bf16[8,256,128]{2,1,0:T(8,128)(2,1)} %get-tuple-element.29), calls=%async_computation | async-start | bytes 1048576 | tf_op jit(solution)/shard_map/all_to_all | solution.py:466
  20.8 2.2 %collective-permute-start = (bf16[512,640]{1,0:T(8,128)(2,1)S(1)}, bf16[512,640]{1,0:T(8,128)(2,1)S(1)}, u32[]{:S(2)}, u32[]{:S(2)}) collective-permute-start(bf16[512,640]{1,0:T(8,128)(2,1)S(1)} %copy-done.5), channel_id=1, source_target_pairs={{0,1},{1,0},{2,3},{3,2},{4,5},{5,4},{6,7},{7,6},{8,9},{9,8},{10,11... | collective-permute-start | bytes 1966088 | tf_op jit(solution)/shard_map/ppermute | solution.py:473
  20.9 3.0 %copy-start.6 = (bf16[512,640]{1,0:T(8,128)(2,1)}, bf16[512,640]{1,0:T(8,128)(2,1)S(1)}, u32[]{:S(2)}) copy-start(bf16[512,640]{1,0:T(8,128)(2,1)S(1)} %collective-permute-done.1.c2) | copy-start | bytes 1966084
  20.9 3.0 %collective-permute-start.2 = (bf16[512,640]{1,0:T(8,128)(2,1)S(1)}, bf16[512,640]{1,0:T(8,128)(2,1)S(1)}, u32[]{:S(2)}, u32[]{:S(2)}) collective-permute-start(bf16[512,640]{1,0:T(8,128)(2,1)S(1)} %collective-permute-done.1.c2), channel_id=1, source_target_pairs={{0,1},{1,0},{2,3},{3,2},{4,5},{5,4},{6,7},{7,6},{8,9},{9,8},{10,11... | collective-permute-start | bytes 1966088 | tf_op jit(solution)/shard_map/ppermute | solution.py:473
  23.0 0.9 copy-start.7
  23.9 0.8 copy-start.8
  31.4 36.0 %copy-start.3 = (s32[2,8]{1,0:T(2,128)S(1)}, s32[2,8]{1,0:T(2,128)}, u32[]{:S(2)}) copy-start(s32[2,8]{1,0:T(2,128)} %offsets.11) | copy-start | bytes 196
  38.8 11.6 %all-to-all-start.1 = ((bf16[8,8,16,128]{3,2,1,0:T(8,128)(2,1)}), bf16[8,8,16,128]{3,2,1,0:T(8,128)(2,1)S(1)}, u32[]{:S(2)}, u32[]{:S(2)}) async-start(bf16[8,8,16,128]{3,2,1,0:T(8,128)(2,1)} %broadcast_in_dim.2), calls=%async_computation.1 | async-start | bytes 524288 | tf_op jit(solution)/shard_map/all_to_all | solution.py:469
  50.3 0.9 copy-start.2
  67.4 14.5 %copy-start = (bf16[8,192,128]{2,1,0:T(8,128)(2,1)}, bf16[8,192,128]{2,1,0:T(8,128)(2,1)S(1)}, u32[]{:S(2)}) copy-start(bf16[8,192,128]{2,1,0:T(8,128)(2,1)S(1)} %all_to_all.25.stats.got) | copy-start | bytes 1179652
  69.0 10.6 %all-to-all-start.3 = ((bf16[8,8,16,128]{3,2,1,0:T(8,128)(2,1)}), bf16[8,8,16,128]{3,2,1,0:T(8,128)(2,1)S(1)}, u32[]{:S(2)}, u32[]{:S(2)}) async-start(bf16[8,8,16,128]{3,2,1,0:T(8,128)(2,1)} %owner_stats.1), calls=%async_computation.3 | async-start | bytes 524288 | tf_op jit(solution)/shard_map/all_to_all | solution.py:469
  81.8 16.7 %all-to-all-start.4 = ((bf16[8,256,128]{2,1,0:T(8,128)(2,1)}), bf16[8,256,128]{2,1,0:T(8,128)(2,1)S(1)}, u32[]{:S(2)}, u32[]{:S(2)}) async-start(bf16[8,256,128]{2,1,0:T(8,128)(2,1)} %far_backward.1), calls=%async_computation.4 | async-start | bytes 1048576 | tf_op jit(solution)/shard_map/all_to_all | solution.py:466
  85.3 13.2 %copy-start.4 = (s32[2,8]{1,0:T(2,128)S(1)}, s32[2,8]{1,0:T(2,128)}, u32[]{:S(2)}) copy-start(s32[2,8]{1,0:T(2,128)} %offsets.11) | copy-start | bytes 196
  98.5 1.5 %copy-start.1 = (bf16[3,640,512]{2,1,0:T(8,128)(2,1)S(1)}, bf16[3,640,512]{2,1,0:T(8,128)(2,1)}, u32[]{:S(2)}) copy-start(bf16[3,640,512]{2,1,0:T(8,128)(2,1)} %get-tuple-element.38.grads) | copy-start | bytes 5898244

commit v3 on v2

--- a/solution.py
+++ b/solution.py
@@ -13,6 +13,7 @@
 BF16 = jnp.bfloat16
 LOG2E = math.log2(math.e)
 NEG = float("-inf")
+LOW = -1e30
 
 
 def nn(a, b):
@@ -147,7 +148,7 @@
 
 
 def local_kernel(
-    heads, factor, offsets, q, k, v, qkvt, msg, out, norm, raw, turned, res, sems, out_sems
+    heads, factor, offsets, q, k, v, qkvt, msg, out, norm, raw, turned, sent, res, sems, out_sems
 ):
     tokens, width = q.shape
     d = width // heads
@@ -162,14 +163,20 @@
         rows = slice(h * d, (h + 1) * d)
         block = jnp.concatenate([turned[0, rows], turned[1, rows], turned[2, rows]], axis=0)
         near = nn(block, pick_matrix(tokens, tokens // NEAR, offsets[0, h]))
-        msg[h, : 3 * d] = near.astype(BF16)
+        sent[h, : 3 * d] = near.astype(BF16)
         picked = nt(place_matrix(tokens, 8, offsets[1, h], 16), block)[:8]
         tail = jnp.concatenate([picked[:, 128:], jnp.zeros((8, 256 - 3 * d), F32)], axis=1)
-        msg[h, 3 * d :] = jnp.concatenate([picked[:, :128], tail], axis=0).astype(BF16)
-        o, n = forward(block[:d], block[d : 2 * d], block[2 * d :], factor, diag)
-        res[rows] = o.astype(BF16)
-        norm[h : h + 1, :] = n
-    stores.append(fetch(res, out, out_sems.at[3]))
+        sent[h, 3 * d :] = jnp.concatenate([picked[:, :128], tail], axis=0).astype(BF16)
+    stores.append(fetch(sent, msg, out_sems.at[3]))
+    size = heads // 2 * d
+    for part in range(2):
+        for h in range(part * heads // 2, (part + 1) * heads // 2):
+            rows = slice(h * d, (h + 1) * d)
+            o, n = forward(turned[0, rows], turned[1, rows], turned[2, rows], factor, diag)
+            res[rows] = o.astype(BF16)
+            norm[h : h + 1, :] = n
+        half = pl.ds(part * size, size)
+        stores.append(fetch(res.at[half], out.at[half], out_sems.at[4 + part]))
     wait_all(stores)
 
 
@@ -217,25 +224,52 @@
     return jnp.concatenate(pieces, axis=1)
 
 
-def near_forward_kernel(d, factor, got, msg, norm):
+def overlap(near_offset, far_offset):
+    shift = far_offset - near_offset
+    spot = iota((8, 128), 0) * 16 + lax.shift_right_arithmetic(shift, 2)
+    return (iota((8, 128), 1) == spot) & (lax.bitwise_and(shift, 3) == 0)
+
+
+def near_forward_kernel(heads, d, factor, offsets, got, stats, msg, norm, shared, buf, sems):
     tokens = NEAR * got.shape[2]
+    load = fetch(stats, buf, sems.at[0])
     diag = causal_mask(tokens // 2)
+    same = overlap(*my_offsets(offsets, heads))
+    hit = jnp.max(jnp.where(same, 1.0, 0.0), axis=1, keepdims=True) > 0.5
+    twice = one_hot(jnp.concatenate([same, same], axis=0))
+    lane = iota((8, 96), 1)
+    stacks = []
     for part in range(2):
         qt, kt, vt = [segment(got, i * d, d, part) for i in range(3)]
         o, n = forward(qt, kt, vt, factor, diag)
         norm[part : part + 1, :] = n
         gap = jnp.zeros((6, tokens), F32)
         rest = jnp.zeros((87 - d, tokens), F32)
-        stack = jnp.concatenate([o, gap, *split3(n), rest], axis=0).astype(BF16)
+        stacks.append(jnp.concatenate([o, gap, *split3(n), rest], axis=0))
+    load.wait()
+    for part in range(2):
         for z in range(NEAR):
-            msg[4 * part + z] = stack[:, z * 128 : (z + 1) * 128]
+            spot = 4 * part + z
+            piece = stacks[part][:, z * 128 : (z + 1) * 128]
+            packed = piece.astype(BF16)
+            msg[spot, :d] = buf[spot, :d]
+            msg[spot, d : 2 * d] = packed[:d]
+            both = buf[spot, d : d + 16].astype(F32) + piece[d:]
+            msg[spot, 2 * d :] = both.astype(BF16)
+            picked = nt(twice, packed)[:8]
+            picked = jnp.where((lane == d + 6) & ~hit, LOW, picked)
+            picked = jnp.concatenate([picked, jnp.zeros((8, 32), F32)], axis=1)
+            rows = buf[spot, d + 16 :].astype(F32)[:8]
+            rows = jnp.concatenate([picked, rows], axis=0).astype(BF16)
+            for copy in range(shared.shape[0]):
+                shared[copy, spot, :16] = got[spot, 3 * d :]
+                shared[copy, spot, 16:] = rows
 
 
 def far_block(got):
-    rows = got[...].astype(F32)
-    tokens = rows.shape[0] * 8
+    rows = got[:, :, :16, :].astype(F32).reshape(64, 16, 128)
     wide = jnp.concatenate(
-        [rows[:, :8].reshape(tokens, 128), rows[:, 8:].reshape(tokens, 128)], axis=1
+        [rows[:, :8].reshape(512, 128), rows[:, 8:].reshape(512, 128)], axis=1
     )
     return wide.T.astype(BF16)
 
@@ -244,7 +278,8 @@
     return pl.ds(pl.multiple_of(lax.axis_index("seq") // 8 * 64, 64), 64)
 
 
-def far_forward_kernel(d, factor, got, stats, near, norm, msg, turned):
+def far_forward_kernel(d, factor, got, near, norm, msg, keep, turned, sems):
+    copy = fetch(got, keep, sems.at[0])
     block = far_block(got)
     tokens = block.shape[1]
     diag = causal_mask(tokens // 2)
@@ -253,18 +288,13 @@
     stack = jnp.concatenate([o, *split3(n), jnp.zeros((125 - d, tokens), F32)], axis=0)
     turned[...] = stack.T
     mine = turned[column_rows(), :].reshape(8, 8, 128)
-    msg[:, :d] = stats[:, :d]
-    msg[:, d : 2 * d] = near[:, :d]
-    both = stats[:, d : d + 16].astype(F32) + near[:, d:].astype(F32)
-    msg[:, 2 * d : 2 * d + 16] = both.astype(BF16)
-    far = stats[:, d + 16 :].astype(F32)[:, :8]
-    msg[:, 2 * d + 16 :] = jnp.concatenate([far, mine], axis=1).astype(BF16)
-
-
-def overlap(near_offset, far_offset):
-    shift = far_offset - near_offset
-    spot = iota((8, 128), 0) * 16 + lax.shift_right_arithmetic(shift, 2)
-    return (iota((8, 128), 1) == spot) & (lax.bitwise_and(shift, 3) == 0)
+    msg[:, : 2 * d + 16] = near[...]
+    rows = got[:, :, 16:, :].astype(F32)
+    for h in range(msg.shape[0]):
+        far = rows[:, h, 8:, :].reshape(64, 128)
+        msg[h, 2 * d + 16 : 2 * d + 80] = far.astype(BF16)
+    msg[:, 2 * d + 80 :] = jnp.concatenate([mine, jnp.zeros_like(mine)], axis=1).astype(BF16)
+    copy.wait()
 
 
 def near_stats(d, stats, outs, part):
@@ -275,74 +305,56 @@
     return g, sum3(rest, 0, 0), sum3(rest, 3, 0), product
 
 
-def owner_stats_kernel(heads, d, offsets, stats, outs, near_norm, msg):
-    near_offset, far_offset = my_offsets(offsets, heads)
-    same = overlap(near_offset, far_offset)
-    hit = jnp.max(jnp.where(same, 1.0, 0.0), axis=1, keepdims=True) > 0.5
-    lane = iota((8, 128), 1)
-    for part in range(2):
-        _, _, _, product = near_stats(d, stats, outs, part)
-        for z in range(NEAR):
-            cols = slice(z * 128, (z + 1) * 128)
-            near_log = near_norm[part : part + 1, cols]
-            near_log = jnp.sum(jnp.where(same, near_log, 0.0), axis=1, keepdims=True)
-            near_log = jnp.where(hit, near_log, NEG)
-            near_dot = jnp.sum(jnp.where(same, product[:, cols], 0.0), axis=1, keepdims=True)
-            rows = stats[4 * part + z, 2 * d + 16 :, :].astype(F32)[:8]
-            mine = sum3(rows, d, 1)
-            both = log2_add(mine, near_log)
-            dot = jnp.exp2(mine - both) * sum3(rows, d + 3, 1)
-            dot = dot + jnp.exp2(near_log - both) * near_dot
-            for i, term in enumerate([*split3(both), *split3(dot)]):
-                rows = jnp.where(lane == d + i, term, rows)
-            rows = jnp.concatenate([rows, jnp.zeros_like(rows)], axis=0).astype(BF16)
-            for copy in range(msg.shape[0]):
-                msg[copy, 4 * part + z] = rows
-
-
-def near_backward_kernel(heads, d, factor, scale, offsets, got, stats, outs, near_norm, msg):
+def owner_backward_kernel(
+    heads, d, factor, scale, offsets, got, stats, mine, outs, near_norm, kept, far_norm,
+    msg, kept_buf, rows_buf, turned, sems,
+):
+    copy = fetch(kept, kept_buf, sems.at[0])
+    rows_buf[...] = stats[:, 2 * d + 16 : 2 * d + 80].astype(F32)
     near_offset, far_offset = my_offsets(offsets, heads)
     same = overlap(near_offset, far_offset)
     hit = jnp.max(jnp.where(same, 1.0, 0.0), axis=0, keepdims=True) > 0.5
     tokens = near_norm.shape[1]
     diag = causal_mask(tokens // 2)
+    plane = pl.ds(pl.multiple_of(lax.axis_index("seq") // 8 * 8, 8), 8)
+    lane = iota((8, 128), 1)
+    copy.wait()
     for part in range(2):
         g, local_norm, local_dot, near_dot = near_stats(d, stats, outs, part)
         far_norms, far_dots = [], []
         for z in range(NEAR):
-            rows = outs[4 * part + z, 2 * d + 16 :, :].astype(F32)[8:]
-            grads = stats[4 * part + z, 2 * d + 16 :, :].astype(F32)[:8]
-            dot = jnp.sum(jnp.where(iota((8, 128), 1) < d, rows * grads, 0.0), axis=1, keepdims=True)
+            rows = mine[4 * part + z, 2 * d + 80 :, :].astype(F32)[:8]
+            grads = rows_buf[4 * part + z, plane, :]
+            dot = jnp.sum(jnp.where(lane < d, rows * grads, 0.0), axis=1, keepdims=True)
             log = jnp.sum(jnp.where(same, sum3(rows, d, 1), 0.0), axis=0, keepdims=True)
             far_norms.append(jnp.where(hit, log, NEG))
             far_dots.append(jnp.sum(jnp.where(same, dot, 0.0), axis=0, keepdims=True))
-        far_norm = jnp.concatenate(far_norms, axis=1)
-        far_dot = jnp.concatenate(far_dots, axis=1)
-        mine = near_norm[part : part + 1, :]
-        norm = log2_add(log2_add(mine, local_norm), far_norm)
-        delta = jnp.exp2(mine - norm) * near_dot + jnp.exp2(local_norm - norm) * local_dot
-        delta = delta + jnp.exp2(far_norm - norm) * far_dot
+        extra = jnp.concatenate(far_norms, axis=1)
+        extra_dot = jnp.concatenate(far_dots, axis=1)
+        own = near_norm[part : part + 1, :]
+        norm = log2_add(log2_add(own, local_norm), extra)
+        delta = jnp.exp2(own - norm) * near_dot + jnp.exp2(local_norm - norm) * local_dot
+        delta = delta + jnp.exp2(extra - norm) * extra_dot
         qt, kt, vt = [segment(got, i * d, d, part) for i in range(3)]
         grads = backward(qt, kt, vt, g.astype(BF16), norm, delta, factor, scale, diag)
         for slot in range(3):
             packed = grads[slot].astype(BF16)
             for z in range(NEAR):
                 msg[4 * part + z, slot * d : (slot + 1) * d] = packed[:, z * 128 : (z + 1) * 128]
-
-
-def far_backward_kernel(d, factor, scale, got, norm, stats, near, msg, turned):
-    block = far_block(got)
+    block = far_block(kept_buf)
     qt, kt, vt = block[:d], block[d : 2 * d], block[2 * d : 3 * d]
-    tokens = block.shape[1]
-    rows = stats[...].astype(F32)[:, :8].reshape(tokens, 128).T
+    pieces = [rows_buf[z, 8 * a : 8 * a + 8, :] for a in range(8) for z in range(heads)]
+    rows = jnp.concatenate(pieces, axis=0).T
+    near = kept_buf[:, :, 16:, :].astype(F32)[:, :, :8, :].reshape(tokens, 128).T
     gt = rows[:d].astype(BF16)
-    rest_norm = sum3(rows, d, 0)
-    rest_dot = sum3(rows, d + 3, 0)
-    mine = norm[:1, :]
-    both = log2_add(mine, rest_norm)
-    share = jnp.exp2(mine - both)
-    rest = jnp.exp2(rest_norm - both) * rest_dot
-    scores = tn(kt, qt) * factor - mine
+    local_norm, other_norm = sum3(rows, d, 0), sum3(near, d + 6, 0)
+    own = far_norm[:1, :]
+    norm = log2_add(log2_add(own, local_norm), other_norm)
+    share = jnp.exp2(own - norm)
+    rest = jnp.exp2(local_norm - norm) * sum3(rows, d + 3, 0)
+    other = jnp.sum(rows[:d] * near[:d], axis=0, keepdims=True)
+    rest = rest + jnp.exp2(other_norm - norm) * other
+    scores = tn(kt, qt) * factor - own
     causal = iota((tokens, tokens), 0) <= iota((tokens, tokens), 1)
     probs = jnp.where(causal, jnp.exp2(scores), 0.0)
     dprobs = tn(vt, gt)
@@ -355,7 +367,6 @@
     stack = jnp.concatenate([dq, dk, dv, jnp.zeros((256 - 3 * d, tokens), F32)], axis=0)
     turned[...] = stack.T
     picked = turned[column_rows(), :]
-    msg[:, : 3 * d] = near[...]
     msg[:, 3 * d :] = jnp.concatenate(
         [picked[:, :128].reshape(8, 8, 128), picked[:, 128:].reshape(8, 8, 128)], axis=1
     ).astype(BF16)
@@ -363,7 +374,7 @@
 
 def local_backward_kernel(
     heads, d, factor, scale, offsets, qkvt, gt, l_out, l_norm, got, attended, grads,
-    buf, o_buf, turned, rows_buf, sems, load_sems, out_sems,
+    buf, o_buf, turned, rows_buf, res, sems, load_sems, out_sems,
 ):
     tokens = gt.shape[1]
     count = tokens // NEAR
@@ -378,7 +389,7 @@
         near = nn(got[h, d : 2 * d + 16, :], place_matrix(tokens, count, offsets[0, h]))
         near_norm = jnp.where(lane % NEAR == offsets[0, h], sum3(near, d + 6, 0), NEG)
         place = iota((8, tokens), 1) == iota((8, tokens), 0) * 64 + offsets[1, h]
-        came = got[h, 2 * d + 16 :, :].astype(F32)[8:]
+        came = got[h, 2 * d + 80 :, :].astype(F32)[:8]
         spread = jnp.sum(jnp.where(place, sum3(came, d, 1), 0.0), axis=0, keepdims=True)
         far_norm = jnp.where(lane % 64 == offsets[1, h], spread, NEG)
         far_out = tn(came[:, :d].astype(BF16), one_hot(place))
@@ -394,15 +405,23 @@
     rows_buf[...] = turned[...].T
     store = fetch(rows_buf, attended, out_sems.at[0])
     wait_all(loads)
-    for h in range(heads):
-        rows = slice(h * d, (h + 1) * d)
-        parts = backward(
-            buf[0, rows], buf[1, rows], buf[2, rows], buf[3, rows],
-            norms[h], deltas[h], factor, scale, diag,
-        )
+    size = heads // 2 * d
+    stores = [store]
+    for part in range(2):
+        for h in range(part * heads // 2, (part + 1) * heads // 2):
+            rows = slice(h * d, (h + 1) * d)
+            parts = backward(
+                buf[0, rows], buf[1, rows], buf[2, rows], buf[3, rows],
+                norms[h], deltas[h], factor, scale, diag,
+            )
+            for slot in range(3):
+                res[slot, rows] = parts[slot].astype(res.dtype)
+        half = pl.ds(part * size, size)
         for slot in range(3):
-            grads[slot, rows] = parts[slot].astype(grads.dtype)
-    store.wait()
+            stores.append(
+                fetch(res.at[slot, half], grads.at[slot, half], out_sems.at[1 + 3 * part + slot])
+            )
+    wait_all(stores)
 
 
 def final_kernel(heads, d, offsets, grads, got, dq, dk, dv, turned, rows_buf, out_sems):
@@ -466,35 +485,35 @@
         return lax.all_to_all(x, "seq", 0, 0, tiled=True, axis_index_groups=columns)
 
     def over_plane(copies):
-        got = lax.all_to_all(copies, "seq", 0, 0, tiled=True, axis_index_groups=planes)
-        return got.reshape(seq_size, *copies.shape[2:])
+        return lax.all_to_all(copies, "seq", 0, 0, tiled=True, axis_index_groups=planes)
 
     def flipped(x, bit):
         return lax.ppermute(x, "head", [(i, i ^ bit) for i in range(4)])
 
     c2 = flipped(cotangent, 2)
+    c1 = flipped(cotangent, 1)
     qkvt, rows_msg, l_out, l_norm = call(
         functools.partial(local_kernel, heads, factor),
         "local_forward",
         [(offsets, "s"), (query_rows, "h"), (key_rows, "h"), (value_rows, "h")],
         [
             (struct((3, width, tokens), BF16), "h"),
-            (struct((heads, 256, count), BF16), "v"),
+            (struct((heads, 256, count), BF16), "h"),
             (struct((width, tokens), BF16), "h"),
             (struct((heads, tokens), F32), "v"),
         ],
         scratch=[
             vmem(3, tokens, width),
             vmem(3, width, tokens),
+            vmem(heads, 256, count),
             vmem(width, tokens),
             dma((3,)),
-            dma((4,)),
+            dma((6,)),
         ],
     )
     rows_got = along_column(rows_msg)
     c2 = after(c2, l_norm)
     c3 = flipped(c2, 1)
-    c1 = flipped(after(cotangent, l_norm), 1)
     gt, stats_msg = call(
         functools.partial(stats_kernel, heads, d),
         "stats",
@@ -515,45 +534,44 @@
         ],
     )
     rows_got = after(rows_got, stats_msg)
-    far_rows = rows_got[:, 3 * d :]
-    far_got = over_plane(jnp.broadcast_to(far_rows[None], (groups, *far_rows.shape)))
-    near_out, near_norm = call(
-        functools.partial(near_forward_kernel, d, factor),
+    near_out, near_norm, shared = call(
+        functools.partial(near_forward_kernel, heads, d, factor),
         "near_forward",
-        [(rows_got, "v")],
-        [(struct((heads, 96, count), BF16), "v"), (struct((2, tokens), F32), "v")],
+        [(offsets, "s"), (rows_got, "v"), (stats_msg, "h")],
+        [
+            (struct((heads, 176, count), BF16), "v"),
+            (struct((2, tokens), F32), "v"),
+            (struct((groups, heads, 32, 128), BF16), "v"),
+        ],
+        scratch=[vmem(heads, 112, 128), dma((1,))],
         limit=16_000_000,
     )
-    far_norm, swap_msg = call(
+    far_got = over_plane(shared)
+    far_norm, swap_msg, far_kept = call(
         functools.partial(far_forward_kernel, d, factor),
         "far_forward",
-        [(far_got, "v"), (stats_msg, "v"), (near_out, "v")],
-        [(struct((8, tokens), F32), "v"), (struct((heads, 192, 128), BF16), "v")],
-        scratch=[vmem(tokens, 128, dtype=F32)],
+        [(far_got, "v"), (near_out, "v")],
+        [
+            (struct((8, tokens), F32), "v"),
+            (struct((heads, 256, 128), BF16), "v"),
+            (struct((groups, heads, 32, 128), BF16), "h"),
+        ],
+        scratch=[vmem(tokens, 128, dtype=F32), dma((1,))],
         limit=16_000_000,
     )
     swap_got = along_column(swap_msg)
-    (far_msg,) = call(
-        functools.partial(owner_stats_kernel, heads, d),
-        "owner_stats",
-        [(offsets, "s"), (swap_got, "v"), (swap_msg, "v"), (near_norm, "v")],
-        [(struct((groups, heads, 16, 128), BF16), "v")],
-        limit=16_000_000,
-    )
-    far_stats = over_plane(far_msg)
-    (near_msg,) = call(
-        functools.partial(near_backward_kernel, heads, d, factor, scale),
-        "near_backward",
-        [(offsets, "s"), (rows_got, "v"), (swap_got, "v"), (swap_msg, "v"), (near_norm, "v")],
-        [(struct((heads, 3 * d, count), BF16), "v")],
-        limit=16_000_000,
-    )
     (grad_msg,) = call(
-        functools.partial(far_backward_kernel, d, factor, scale),
-        "far_backward",
-        [(far_got, "v"), (far_norm, "v"), (far_stats, "v"), (near_msg, "v")],
+        functools.partial(owner_backward_kernel, heads, d, factor, scale),
+        "owner_backward",
+        [(offsets, "s"), (rows_got, "v"), (swap_got, "v"), (swap_msg, "v"), (near_out, "v")]
+        + [(near_norm, "v"), (far_kept, "h"), (far_norm, "v")],
         [(struct((heads, 256, 128), BF16), "v")],
-        scratch=[vmem(tokens, 256, dtype=F32)],
+        scratch=[
+            vmem(groups, heads, 32, 128),
+            vmem(heads, 64, 128, dtype=F32),
+            vmem(tokens, 256, dtype=F32),
+            dma((1,)),
+        ],
         limit=16_000_000,
     )
     owner_grads = along_column(grad_msg)
@@ -564,16 +582,17 @@
         [(offsets, "s"), (qkvt, "h"), (gt, "h"), (l_out, "h"), (l_norm, "v"), (swap_got, "v")],
         [
             (struct((tokens, width), BF16), "h"),
-            (struct((3, width, tokens), BF16), "v"),
+            (struct((3, width, tokens), BF16), "h"),
         ],
         scratch=[
             vmem(4, width, tokens),
             vmem(width, tokens),
             vmem(width, tokens),
             vmem(tokens, width),
+            vmem(3, width, tokens),
             dma((2,)),
             dma((3,)),
-            dma((1,)),
+            dma((7,)),
         ],
     )
     grad_query, grad_key, grad_value = call(

time: 104 us -> 101 us (0.971)
  blocking collectives: 15.3 us -> 32 us
  starting transfers between devices: 25.5 us -> 14.9 us
  waiting for transfers between devices: 20.1 us -> 13.6 us
  Pallas kernels: 37.5 us -> 35.6 us
    all_to_all x0 -> x1, blocking collectives: none -> 13.4 us  [over_plane(): lax.all_to_all(copies, 'seq', 0, 0, tiled=True, axis_index_groups=planes)]
    all_to_all x2 -> x0, starting transfers between devices: 10.6 us -> none  [over_plane(): lax.all_to_all(copies, 'seq', 0, 0, tiled=True, axis_index_groups=planes)]
    all_to_all x2 -> x0, waiting for transfers between devices: 8.23 us -> none  [over_plane(): lax.all_to_all(copies, 'seq', 0, 0, tiled=True, axis_index_groups=planes)]
    all_to_all x1, blocking collectives: 15.3 us -> 18.5 us  [along_column(): return lax.all_to_all(x, 'seq', 0, 0, tiled=True, axis_index_groups=columns)]
    pallas_call x9 -> x7, Pallas kernels: 37.5 us -> 35.6 us  [call(): pl.pallas_call(kernel, name=name, out_shape=shapes, in_specs=[pl.BlockSpe...]
    all_to_all x2, waiting for transfers between devices: 9.4 us -> 11.1 us  [along_column(): return lax.all_to_all(x, 'seq', 0, 0, tiled=True, axis_index_groups=columns)]
  transfers between devices with their start and end apart: 7 -> 5, of which waited for: 6 -> 4; matrix products, arithmetic and copies ran while one was open for 0% -> 0% of each run, Pallas kernels for 29% -> 25%
where the time goes in v3:
time: 101 us; the launch traced here: 100 us
  Pallas kernels  35.6 us (35%)
  blocking collectives  32 us (32%)
  starting transfers between devices  14.9 us (15%)
  waiting for transfers between devices  13.6 us (13%)
  local copies, waits for them, and re-layouts  3.35 us (3%)
    pallas_call x7, Pallas kernels, call(): pl.pallas_call(kernel, name=name, out_shape=shapes, in_specs=[pl.BlockSpe...  35.6 us
    all_to_all x1, blocking collectives, along_column(): return lax.all_to_all(x, 'seq', 0, 0, tiled=True, axis_index_groups=columns)  18.5 us
    all_to_all x1, blocking collectives, over_plane(): lax.all_to_all(copies, 'seq', 0, 0, tiled=True, axis_index_groups=planes)  13.4 us
    all_to_all x2, starting transfers between devices, along_column(): return lax.all_to_all(x, 'seq', 0, 0, tiled=True, axis_index_groups=columns)  12 us
    all_to_all x2, waiting for transfers between devices, along_column(): return lax.all_to_all(x, 'seq', 0, 0, tiled=True, axis_index_groups=columns)  11.1 us
    unnamed x18, local copies, waits for them, and re-layouts  3.35 us
    ppermute x3, starting transfers between devices, flipped(): return lax.ppermute(x, 'head', [(i, i ^ bit) for i in range(4)])  2.95 us
    ppermute x3, waiting for transfers between devices, flipped(): return lax.ppermute(x, 'head', [(i, i ^ bit) for i in range(4)])  2.52 us
  transfers between devices with their start and end apart: 5, of which 4 were waited for; matrix products, arithmetic and copies ran while one was open for 0% of the time, Pallas kernels for 25%

profile of v3, /device:TPU:8, one launch (start us, length us, event | category | flops | bytes accessed | tf_op | source)
XLA Modules:
  0.0 100.3 jit_solution(13394532140883324614)
XLA Ops:
  0.6 0.0 copy-start.5
  0.6 2.4 %collective-permute-start.1 = (bf16[512,640]{1,0:T(8,128)(2,1)}, bf16[512,640]{1,0:T(8,128)(2,1)S(1)}, u32[]{:S(2)}, u32[]{:S(2)}) collective-permute-start(bf16[512,640]{1,0:T(8,128)(2,1)} %c0.1), channel_id=1, source_target_pairs={{0,2},{1,3},{2,0},{3,1},{4,6},{5,7},{6,4},{7,5},{8,10},{9,11},{10,... | collective-permute-start | bytes 1966088 | tf_op jit(solution)/shard_map/ppermute | solution.py:491
  3.0 8.3 %local_forward.1 = (bf16[3,640,512]{2,1,0:T(8,128)(2,1)}, bf16[8,256,128]{2,1,0:T(8,128)(2,1)}, bf16[640,512]{1,0:T(8,128)(2,1)}, f32[8,512]{1,0:T(8,128)}) custom-call(s32[2,8]{1,0:T(2,128)} %offsets.11, bf16[512,640]{1,0:T(8,128)(2,1)} %q.1, bf16[512,640]{1,0:T(8,128)(2,1)} %k.1, bf16[512,640]{1,0:T(8,128)(2,1)} %v.1), custom_call_target="tpu_custom_call" | custom-call | flops 1000 | bytes 1000 | tf_op jit(solution)/shard_map/local_forward/pallas_call | solution.py:451
  11.3 8.5 %all-to-all-start = ((bf16[8,256,128]{2,1,0:T(8,128)(2,1)}), bf16[8,256,128]{2,1,0:T(8,128)(2,1)S(1)}, u32[]{:S(2)}, u32[]{:S(2)}) async-start(bf16[8,256,128]{2,1,0:T(8,128)(2,1)} %get-tuple-element.29), calls=%async_computation | async-start | bytes 1048576 | tf_op jit(solution)/shard_map/all_to_all | solution.py:485
  19.8 0.0 copy-done.5
  19.8 0.1 collective-permute-start
  19.9 0.0 collective-permute-done.1.c2
  19.9 0.0 copy-start.6
  19.9 0.5 collective-permute-start.2
  20.4 1.6 %collective-permute-done.c1 = bf16[512,640]{1,0:T(8,128)(2,1)S(1)} collective-permute-done((bf16[512,640]{1,0:T(8,128)(2,1)S(1)}, bf16[512,640]{1,0:T(8,128)(2,1)S(1)}, u32[]{:S(2)}, u32[]{:S(2)}) %collective-permute-start) | collective-permute-done | bytes 655392 | tf_op jit(solution)/shard_map/ppermute | solution.py:491
  22.0 0.0 copy-start.7
  22.0 0.9 collective-permute-done.2.c3
  22.9 0.8 copy-done.8
  23.8 0.0 copy-done.6
  23.8 0.0 copy-done.7
  23.8 6.7 %stats.1 = (bf16[640,512]{1,0:T(8,128)(2,1)}, bf16[8,112,128]{2,1,0:T(8,128)(2,1)}) custom-call(s32[2,8]{1,0:T(2,128)} %offsets.11, bf16[640,2560]{1,0:T(8,128)(2,1)} %w.1, bf16[512,640]{1,0:T(8,128)(2,1)} %c0.1, bf16[512,640]{1,0:T(8,128)(2,1)} %copy-done.7, bf16[512,640]{1,0:T(8,128)(2,1)} %copy-done.6, bf16[512,640]{1,0:T(8,128)(2,1)} %copy-done.8, ...), custom_call_target="tpu_custom_call" | custom-call | flops 1000 | bytes 1000 | tf_op jit(solution)/shard_map/stats/pallas_call | solution.py:451
  30.5 6.6 %all-to-all-done.got = bf16[8,256,128]{2,1,0:T(8,128)(2,1)S(1)} async-done(((bf16[8,256,128]{2,1,0:T(8,128)(2,1)}), bf16[8,256,128]{2,1,0:T(8,128)(2,1)S(1)}, u32[]{:S(2)}, u32[]{:S(2)}) %all-to-all-start) | async-done | bytes 524320 | tf_op jit(solution)/shard_map/all_to_all | solution.py:485
  37.0 0.0 copy-done.3
  37.0 0.9 copy-done.2
  38.0 2.3 %near_forward.1 = (bf16[8,176,128]{2,1,0:T(8,128)(2,1)S(1)}, f32[2,512]{1,0:T(2,128)S(1)}, bf16[8,8,32,128]{3,2,1,0:T(8,128)(2,1)S(1)}) custom-call(s32[2,8]{1,0:T(2,128)S(1)} %copy-done.3, bf16[8,256,128]{2,1,0:T(8,128)(2,1)S(1)} %all-to-all-done.got, bf16[8,112,128]{2,1,0:T(8,128)(2,1)S(1)} %copy-done.2), custom_call_target="tpu_custom_call" | custom-call | flops 1000 | bytes 1000 | tf_op jit(solution)/shard_map/near_forward/pallas_call | solution.py:451
  40.3 13.4 %all_to_all.20.got = bf16[8,8,32,128]{3,2,1,0:T(8,128)(2,1)S(1)} all-to-all(bf16[8,8,32,128]{3,2,1,0:T(8,128)(2,1)S(1)} %get-tuple-element.32), channel_id=1, replica_groups={{0,32,64,96,128,160,192,224},{4,36,68,100,132,164,196,228},{8,40,72,104..., dimensions={0} | all-to-all | bytes 1048576 | tf_op jit(solution)/shard_map/all_to_all | solution.py:488
  53.7 0.8 far_forward.1
  54.6 18.5 %all_to_all.21.stats.got = bf16[8,256,128]{2,1,0:T(8,128)(2,1)S(1)} all-to-all(bf16[8,256,128]{2,1,0:T(8,128)(2,1)S(1)} %get-tuple-element.34.mine), channel_id=1, replica_groups={{0,4,8,12,16,20,24,28},{32,36,40,44,48,52,56,60},{64,68,72,76,80,84,88,..., dimensions={0} | all-to-all | bytes 1048576 | tf_op jit(solution)/shard_map/all_to_all | solution.py:485
  73.1 4.2 %owner_backward.1 = bf16[8,256,128]{2,1,0:T(8,128)(2,1)} custom-call(s32[2,8]{1,0:T(2,128)S(1)} %copy-done.3, bf16[8,256,128]{2,1,0:T(8,128)(2,1)S(1)} %all-to-all-done.got, bf16[8,256,128]{2,1,0:T(8,128)(2,1)S(1)} %all_to_all.21.stats.got, bf16[8,256,128]{2,1,0:T(8,128)(2,1)S(1)} %get-tuple-element.34.mine, ...), custom_call_target="tpu_custom_call" | custom-call | flops 1000 | bytes 1000 | tf_op jit(solution)/shard_map/owner_backward/pallas_call | solution.py:451
  77.3 0.0 copy-done
  77.3 3.5 %all-to-all-start.3 = ((bf16[8,256,128]{2,1,0:T(8,128)(2,1)}), bf16[8,256,128]{2,1,0:T(8,128)(2,1)S(1)}, u32[]{:S(2)}, u32[]{:S(2)}) async-start(bf16[8,256,128]{2,1,0:T(8,128)(2,1)} %owner_backward.1), calls=%async_computation.3 | async-start | bytes 1048576 | tf_op jit(solution)/shard_map/all_to_all | solution.py:485
  80.8 0.0 copy-start.4
  80.8 10.1 %local_backward.1 = (bf16[512,640]{1,0:T(8,128)(2,1)}, bf16[3,640,512]{2,1,0:T(8,128)(2,1)}) custom-call(s32[2,8]{1,0:T(2,128)} %offsets.11, bf16[3,640,512]{2,1,0:T(8,128)(2,1)} %get-tuple-element.24.qkvt, bf16[640,512]{1,0:T(8,128)(2,1)} %get-tuple-element.28.gt, bf16[640,512]{1,0:T(8,128)(2,1)} %get-tuple-element.27.l_out, ...), custom_call_target="tpu_custom_call" | custom-call | flops 1000 | bytes 1000 | tf_op jit(solution)/shard_map/local_backward/pallas_call | solution.py:451
  91.0 4.5 %all-to-all-done.3.got = bf16[8,256,128]{2,1,0:T(8,128)(2,1)S(1)} async-done(((bf16[8,256,128]{2,1,0:T(8,128)(2,1)}), bf16[8,256,128]{2,1,0:T(8,128)(2,1)S(1)}, u32[]{:S(2)}, u32[]{:S(2)}) %all-to-all-start.3) | async-done | bytes 524320 | tf_op jit(solution)/shard_map/all_to_all | solution.py:485
  95.5 0.0 copy-done.4
  95.5 1.5 %copy-done.1 = bf16[3,640,512]{2,1,0:T(8,128)(2,1)S(1)} copy-done((bf16[3,640,512]{2,1,0:T(8,128)(2,1)S(1)}, bf16[3,640,512]{2,1,0:T(8,128)(2,1)}, u32[]{:S(2)}) %copy-start.1) | copy-done | bytes 1966104
  97.0 3.1 %final.1 = (bf16[512,640]{1,0:T(8,128)(2,1)}, bf16[512,640]{1,0:T(8,128)(2,1)}, bf16[512,640]{1,0:T(8,128)(2,1)}) custom-call(s32[2,8]{1,0:T(2,128)S(1)} %copy-done.4, bf16[3,640,512]{2,1,0:T(8,128)(2,1)S(1)} %copy-done.1, bf16[8,256,128]{2,1,0:T(8,128)(2,1)S(1)} %all-to-all-done.3.got), custom_call_target="tpu_custom_call" | custom-call | flops 1000 | bytes 1000 | tf_op jit(solution)/shard_map/final/pallas_call | solution.py:451
  (5 shorter events, 0.0 us)
Async XLA Ops:
  0.6 19.2 %copy-start.5 = (bf16[512,640]{1,0:T(8,128)(2,1)S(1)}, bf16[512,640]{1,0:T(8,128)(2,1)}, u32[]{:S(2)}) copy-start(bf16[512,640]{1,0:T(8,128)(2,1)} %c0.1) | copy-start | bytes 1966084
  0.6 19.3 %collective-permute-start.1 = (bf16[512,640]{1,0:T(8,128)(2,1)}, bf16[512,640]{1,0:T(8,128)(2,1)S(1)}, u32[]{:S(2)}, u32[]{:S(2)}) collective-permute-start(bf16[512,640]{1,0:T(8,128)(2,1)} %c0.1), channel_id=1, source_target_pairs={{0,2},{1,3},{2,0},{3,1},{4,6},{5,7},{6,4},{7,5},{8,10},{9,11},{10,... | collective-permute-start | bytes 1966088 | tf_op jit(solution)/shard_map/ppermute | solution.py:491
  11.3 25.7 %all-to-all-start = ((bf16[8,256,128]{2,1,0:T(8,128)(2,1)}), bf16[8,256,128]{2,1,0:T(8,128)(2,1)S(1)}, u32[]{:S(2)}, u32[]{:S(2)}) async-start(bf16[8,256,128]{2,1,0:T(8,128)(2,1)} %get-tuple-element.29), calls=%async_computation | async-start | bytes 1048576 | tf_op jit(solution)/shard_map/all_to_all | solution.py:485
  19.8 2.2 %collective-permute-start = (bf16[512,640]{1,0:T(8,128)(2,1)S(1)}, bf16[512,640]{1,0:T(8,128)(2,1)S(1)}, u32[]{:S(2)}, u32[]{:S(2)}) collective-permute-start(bf16[512,640]{1,0:T(8,128)(2,1)S(1)} %copy-done.5), channel_id=1, source_target_pairs={{0,1},{1,0},{2,3},{3,2},{4,5},{5,4},{6,7},{7,6},{8,9},{9,8},{10,11... | collective-permute-start | bytes 1966088 | tf_op jit(solution)/shard_map/ppermute | solution.py:491
  19.9 3.9 %copy-start.6 = (bf16[512,640]{1,0:T(8,128)(2,1)}, bf16[512,640]{1,0:T(8,128)(2,1)S(1)}, u32[]{:S(2)}) copy-start(bf16[512,640]{1,0:T(8,128)(2,1)S(1)} %collective-permute-done.1.c2) | copy-start | bytes 1966084
  19.9 3.0 %collective-permute-start.2 = (bf16[512,640]{1,0:T(8,128)(2,1)S(1)}, bf16[512,640]{1,0:T(8,128)(2,1)S(1)}, u32[]{:S(2)}, u32[]{:S(2)}) collective-permute-start(bf16[512,640]{1,0:T(8,128)(2,1)S(1)} %collective-permute-done.1.c2), channel_id=1, source_target_pairs={{0,1},{1,0},{2,3},{3,2},{4,5},{5,4},{6,7},{7,6},{8,9},{9,8},{10,11... | collective-permute-start | bytes 1966088 | tf_op jit(solution)/shard_map/ppermute | solution.py:491
  22.0 1.8 %copy-start.7 = (bf16[512,640]{1,0:T(8,128)(2,1)}, bf16[512,640]{1,0:T(8,128)(2,1)S(1)}, u32[]{:S(2)}) copy-start(bf16[512,640]{1,0:T(8,128)(2,1)S(1)} %collective-permute-done.c1) | copy-start | bytes 1966084
  22.9 0.8 copy-start.8
  23.8 13.2 %copy-start.3 = (s32[2,8]{1,0:T(2,128)S(1)}, s32[2,8]{1,0:T(2,128)}, u32[]{:S(2)}) copy-start(s32[2,8]{1,0:T(2,128)} %offsets.11) | copy-start | bytes 196
  37.0 0.9 copy-start.2
  73.1 4.2 %copy-start = (bf16[8,256,128]{2,1,0:T(8,128)(2,1)}, bf16[8,256,128]{2,1,0:T(8,128)(2,1)S(1)}, u32[]{:S(2)}) copy-start(bf16[8,256,128]{2,1,0:T(8,128)(2,1)S(1)} %all_to_all.21.stats.got) | copy-start | bytes 1572868
  77.3 18.2 %all-to-all-start.3 = ((bf16[8,256,128]{2,1,0:T(8,128)(2,1)}), bf16[8,256,128]{2,1,0:T(8,128)(2,1)S(1)}, u32[]{:S(2)}, u32[]{:S(2)}) async-start(bf16[8,256,128]{2,1,0:T(8,128)(2,1)} %owner_backward.1), calls=%async_computation.3 | async-start | bytes 1048576 | tf_op jit(solution)/shard_map/all_to_all | solution.py:485
  80.8 14.7 %copy-start.4 = (s32[2,8]{1,0:T(2,128)S(1)}, s32[2,8]{1,0:T(2,128)}, u32[]{:S(2)}) copy-start(s32[2,8]{1,0:T(2,128)} %offsets.11) | copy-start | bytes 196
  95.5 1.5 %copy-start.1 = (bf16[3,640,512]{2,1,0:T(8,128)(2,1)S(1)}, bf16[3,640,512]{2,1,0:T(8,128)(2,1)}, u32[]{:S(2)}) copy-start(bf16[3,640,512]{2,1,0:T(8,128)(2,1)} %get-tuple-element.40.grads) | copy-start | bytes 5898244

commit v4 on v3

--- a/solution.py
+++ b/solution.py
@@ -90,7 +90,7 @@
     return jnp.concatenate(outs, axis=1), jnp.concatenate(norms, axis=1)
 
 
-def backward(qt, kt, vt, gt, norm, delta, factor, scale, diag):
+def backward(qt, kt, vt, gt, norm, delta, factor, scale, diag, share=None):
     tokens = qt.shape[1]
     half, blocks = halves(tokens)
     dq = []
@@ -103,7 +103,12 @@
         else:
             probs = jnp.concatenate([jnp.exp2(scores[:half]), last], axis=0)
         dprobs = tn(vt[:, :keys], gt[:, cols])
-        dscores = (probs * (dprobs - delta[:, cols])).astype(BF16)
+        total = delta[:, cols]
+        if share is not None:
+            mine = jnp.sum(probs * dprobs, axis=0, keepdims=True)
+            total = total + share[:, cols] * mine
+            probs = probs * share[:, cols]
+        dscores = (probs * (dprobs - total)).astype(BF16)
         dq.append(nn(kt[:, :keys], dscores) * scale)
         dk_part = nt(qt[:, cols], dscores) * scale
         dv_part = nt(gt[:, cols], probs.astype(BF16))
@@ -278,8 +283,7 @@
     return pl.ds(pl.multiple_of(lax.axis_index("seq") // 8 * 64, 64), 64)
 
 
-def far_forward_kernel(d, factor, got, near, norm, msg, keep, turned, sems):
-    copy = fetch(got, keep, sems.at[0])
+def far_forward_kernel(d, factor, got, near, norm, msg, turned):
     block = far_block(got)
     tokens = block.shape[1]
     diag = causal_mask(tokens // 2)
@@ -294,7 +298,6 @@
         far = rows[:, h, 8:, :].reshape(64, 128)
         msg[h, 2 * d + 16 : 2 * d + 80] = far.astype(BF16)
     msg[:, 2 * d + 80 :] = jnp.concatenate([mine, jnp.zeros_like(mine)], axis=1).astype(BF16)
-    copy.wait()
 
 
 def near_stats(d, stats, outs, part):
@@ -306,10 +309,9 @@
 
 
 def owner_backward_kernel(
-    heads, d, factor, scale, offsets, got, stats, mine, outs, near_norm, kept, far_norm,
-    msg, kept_buf, rows_buf, turned, sems,
+    heads, d, factor, scale, offsets, got, stats, mine, outs, near_norm, plane_got,
+    far_norm, msg, rows_buf, turned,
 ):
-    copy = fetch(kept, kept_buf, sems.at[0])
     rows_buf[...] = stats[:, 2 * d + 16 : 2 * d + 80].astype(F32)
     near_offset, far_offset = my_offsets(offsets, heads)
     same = overlap(near_offset, far_offset)
@@ -318,7 +320,6 @@
     diag = causal_mask(tokens // 2)
     plane = pl.ds(pl.multiple_of(lax.axis_index("seq") // 8 * 8, 8), 8)
     lane = iota((8, 128), 1)
-    copy.wait()
     for part in range(2):
         g, local_norm, local_dot, near_dot = near_stats(d, stats, outs, part)
         far_norms, far_dots = [], []
@@ -341,11 +342,11 @@
             packed = grads[slot].astype(BF16)
             for z in range(NEAR):
                 msg[4 * part + z, slot * d : (slot + 1) * d] = packed[:, z * 128 : (z + 1) * 128]
-    block = far_block(kept_buf)
+    block = far_block(plane_got)
     qt, kt, vt = block[:d], block[d : 2 * d], block[2 * d : 3 * d]
     pieces = [rows_buf[z, 8 * a : 8 * a + 8, :] for a in range(8) for z in range(heads)]
     rows = jnp.concatenate(pieces, axis=0).T
-    near = kept_buf[:, :, 16:, :].astype(F32)[:, :, :8, :].reshape(tokens, 128).T
+    near = plane_got[:, :, 16:, :].astype(F32)[:, :, :8, :].reshape(tokens, 128).T
     gt = rows[:d].astype(BF16)
     local_norm, other_norm = sum3(rows, d, 0), sum3(near, d + 6, 0)
     own = far_norm[:1, :]
@@ -354,16 +355,7 @@
     rest = jnp.exp2(local_norm - norm) * sum3(rows, d + 3, 0)
     other = jnp.sum(rows[:d] * near[:d], axis=0, keepdims=True)
     rest = rest + jnp.exp2(other_norm - norm) * other
-    scores = tn(kt, qt) * factor - own
-    causal = iota((tokens, tokens), 0) <= iota((tokens, tokens), 1)
-    probs = jnp.where(causal, jnp.exp2(scores), 0.0)
-    dprobs = tn(vt, gt)
-    delta = share * jnp.sum(probs * dprobs, axis=0, keepdims=True) + rest
-    probs = probs * share
-    dscores = (probs * (dprobs - delta)).astype(BF16)
-    dq = nn(kt, dscores) * scale
-    dk = nt(qt, dscores) * scale
-    dv = nt(gt, probs.astype(BF16))
+    dq, dk, dv = backward(qt, kt, vt, gt, own, rest, factor, scale, diag, share)
     stack = jnp.concatenate([dq, dk, dv, jnp.zeros((256 - 3 * d, tokens), F32)], axis=0)
     turned[...] = stack.T
     picked = turned[column_rows(), :]
@@ -547,16 +539,15 @@
         limit=16_000_000,
     )
     far_got = over_plane(shared)
-    far_norm, swap_msg, far_kept = call(
+    far_norm, swap_msg = call(
         functools.partial(far_forward_kernel, d, factor),
         "far_forward",
         [(far_got, "v"), (near_out, "v")],
         [
             (struct((8, tokens), F32), "v"),
             (struct((heads, 256, 128), BF16), "v"),
-            (struct((groups, heads, 32, 128), BF16), "h"),
-        ],
-        scratch=[vmem(tokens, 128, dtype=F32), dma((1,))],
+        ],
+        scratch=[vmem(tokens, 128, dtype=F32)],
         limit=16_000_000,
     )
     swap_got = along_column(swap_msg)
@@ -564,13 +555,11 @@
         functools.partial(owner_backward_kernel, heads, d, factor, scale),
         "owner_backward",
         [(offsets, "s"), (rows_got, "v"), (swap_got, "v"), (swap_msg, "v"), (near_out, "v")]
-        + [(near_norm, "v"), (far_kept, "h"), (far_norm, "v")],
+        + [(near_norm, "v"), (far_got, "v"), (far_norm, "v")],
         [(struct((heads, 256, 128), BF16), "v")],
         scratch=[
-            vmem(groups, heads, 32, 128),
             vmem(heads, 64, 128, dtype=F32),
             vmem(tokens, 256, dtype=F32),
-            dma((1,)),
         ],
         limit=16_000_000,
     )

time: 101 us -> 101 us (level)
  no operation moved by 1% of the time
where the time goes in v4:
time: 101 us; the launch traced here: 100 us
  Pallas kernels  35.4 us (35%)
  blocking collectives  32 us (32%)
  starting transfers between devices  15.1 us (15%)
  waiting for transfers between devices  13.3 us (13%)
  local copies, waits for them, and re-layouts  3.35 us (3%)
    pallas_call x7, Pallas kernels, call(): pl.pallas_call(kernel, name=name, out_shape=shapes, in_specs=[pl.BlockSpe...  35.4 us
    all_to_all x1, blocking collectives, along_column(): return lax.all_to_all(x, 'seq', 0, 0, tiled=True, axis_index_groups=columns)  18.5 us
    all_to_all x1, blocking collectives, over_plane(): lax.all_to_all(copies, 'seq', 0, 0, tiled=True, axis_index_groups=planes)  13.4 us
    all_to_all x2, starting transfers between devices, along_column(): return lax.all_to_all(x, 'seq', 0, 0, tiled=True, axis_index_groups=columns)  12.2 us
    all_to_all x2, waiting for transfers between devices, along_column(): return lax.all_to_all(x, 'seq', 0, 0, tiled=True, axis_index_groups=columns)  10.8 us
    unnamed x18, local copies, waits for them, and re-layouts  3.35 us
    ppermute x3, starting transfers between devices, flipped(): return lax.ppermute(x, 'head', [(i, i ^ bit) for i in range(4)])  2.95 us
    ppermute x3, waiting for transfers between devices, flipped(): return lax.ppermute(x, 'head', [(i, i ^ bit) for i in range(4)])  2.52 us
  transfers between devices with their start and end apart: 5, of which 4 were waited for; matrix products, arithmetic and copies ran while one was open for 0% of the time, Pallas kernels for 25%

profile of v4, /device:TPU:8, one launch (start us, length us, event | category | flops | bytes accessed | tf_op | source)
XLA Modules:
  0.0 100.0 jit_solution(139571237918777281)
XLA Ops:
  0.6 0.0 copy-start.5
  0.6 2.4 %collective-permute-start.1 = (bf16[512,640]{1,0:T(8,128)(2,1)}, bf16[512,640]{1,0:T(8,128)(2,1)S(1)}, u32[]{:S(2)}, u32[]{:S(2)}) collective-permute-start(bf16[512,640]{1,0:T(8,128)(2,1)} %c0.1), channel_id=1, source_target_pairs={{0,2},{1,3},{2,0},{3,1},{4,6},{5,7},{6,4},{7,5},{8,10},{9,11},{10,... | collective-permute-start | bytes 1966088 | tf_op jit(solution)/shard_map/ppermute | solution.py:483
  3.0 8.3 %local_forward.1 = (bf16[3,640,512]{2,1,0:T(8,128)(2,1)}, bf16[8,256,128]{2,1,0:T(8,128)(2,1)}, bf16[640,512]{1,0:T(8,128)(2,1)}, f32[8,512]{1,0:T(8,128)}) custom-call(s32[2,8]{1,0:T(2,128)} %offsets.11, bf16[512,640]{1,0:T(8,128)(2,1)} %q.1, bf16[512,640]{1,0:T(8,128)(2,1)} %k.1, bf16[512,640]{1,0:T(8,128)(2,1)} %v.1), custom_call_target="tpu_custom_call" | custom-call | flops 1000 | bytes 1000 | tf_op jit(solution)/shard_map/local_forward/pallas_call | solution.py:443
  11.3 8.5 %all-to-all-start = ((bf16[8,256,128]{2,1,0:T(8,128)(2,1)}), bf16[8,256,128]{2,1,0:T(8,128)(2,1)S(1)}, u32[]{:S(2)}, u32[]{:S(2)}) async-start(bf16[8,256,128]{2,1,0:T(8,128)(2,1)} %get-tuple-element.28), calls=%async_computation | async-start | bytes 1048576 | tf_op jit(solution)/shard_map/all_to_all | solution.py:477
  19.8 0.0 copy-done.5
  19.8 0.1 collective-permute-start
  19.9 0.0 collective-permute-done.1.c2
  19.9 0.0 copy-start.6
  19.9 0.5 collective-permute-start.2
  20.4 1.6 %collective-permute-done.c1 = bf16[512,640]{1,0:T(8,128)(2,1)S(1)} collective-permute-done((bf16[512,640]{1,0:T(8,128)(2,1)S(1)}, bf16[512,640]{1,0:T(8,128)(2,1)S(1)}, u32[]{:S(2)}, u32[]{:S(2)}) %collective-permute-start) | collective-permute-done | bytes 655392 | tf_op jit(solution)/shard_map/ppermute | solution.py:483
  22.0 0.0 copy-start.7
  22.0 0.9 collective-permute-done.2.c3
  22.9 0.8 copy-done.8
  23.8 0.0 copy-done.6
  23.8 0.0 copy-done.7
  23.8 6.7 %stats.1 = (bf16[640,512]{1,0:T(8,128)(2,1)}, bf16[8,112,128]{2,1,0:T(8,128)(2,1)}) custom-call(s32[2,8]{1,0:T(2,128)} %offsets.11, bf16[640,2560]{1,0:T(8,128)(2,1)} %w.1, bf16[512,640]{1,0:T(8,128)(2,1)} %c0.1, bf16[512,640]{1,0:T(8,128)(2,1)} %copy-done.7, bf16[512,640]{1,0:T(8,128)(2,1)} %copy-done.6, bf16[512,640]{1,0:T(8,128)(2,1)} %copy-done.8, ...), custom_call_target="tpu_custom_call" | custom-call | flops 1000 | bytes 1000 | tf_op jit(solution)/shard_map/stats/pallas_call | solution.py:443
  30.5 6.6 %all-to-all-done.got = bf16[8,256,128]{2,1,0:T(8,128)(2,1)S(1)} async-done(((bf16[8,256,128]{2,1,0:T(8,128)(2,1)}), bf16[8,256,128]{2,1,0:T(8,128)(2,1)S(1)}, u32[]{:S(2)}, u32[]{:S(2)}) %all-to-all-start) | async-done | bytes 524320 | tf_op jit(solution)/shard_map/all_to_all | solution.py:477
  37.0 0.0 copy-done.3
  37.0 0.9 copy-done.2
  38.0 2.3 %near_forward.1 = (bf16[8,176,128]{2,1,0:T(8,128)(2,1)S(1)}, f32[2,512]{1,0:T(2,128)S(1)}, bf16[8,8,32,128]{3,2,1,0:T(8,128)(2,1)S(1)}) custom-call(s32[2,8]{1,0:T(2,128)S(1)} %copy-done.3, bf16[8,256,128]{2,1,0:T(8,128)(2,1)S(1)} %all-to-all-done.got, bf16[8,112,128]{2,1,0:T(8,128)(2,1)S(1)} %copy-done.2), custom_call_target="tpu_custom_call" | custom-call | flops 1000 | bytes 1000 | tf_op jit(solution)/shard_map/near_forward/pallas_call | solution.py:443
  40.3 13.4 %all_to_all.20.got.plane_got = bf16[8,8,32,128]{3,2,1,0:T(8,128)(2,1)S(1)} all-to-all(bf16[8,8,32,128]{3,2,1,0:T(8,128)(2,1)S(1)} %get-tuple-element.31), channel_id=1, replica_groups={{0,32,64,96,128,160,192,224},{4,36,68,100,132,164,196,228},{8,40,72,104..., dimensions={0} | all-to-all | bytes 1048576 | tf_op jit(solution)/shard_map/all_to_all | solution.py:480
  53.7 0.8 far_forward.1
  54.5 18.5 %all_to_all.21.stats.got = bf16[8,256,128]{2,1,0:T(8,128)(2,1)S(1)} all-to-all(bf16[8,256,128]{2,1,0:T(8,128)(2,1)S(1)} %get-tuple-element.33.mine), channel_id=1, replica_groups={{0,4,8,12,16,20,24,28},{32,36,40,44,48,52,56,60},{64,68,72,76,80,84,88,..., dimensions={0} | all-to-all | bytes 1048576 | tf_op jit(solution)/shard_map/all_to_all | solution.py:477
  73.1 4.0 %owner_backward.1 = bf16[8,256,128]{2,1,0:T(8,128)(2,1)} custom-call(s32[2,8]{1,0:T(2,128)S(1)} %copy-done.3, bf16[8,256,128]{2,1,0:T(8,128)(2,1)S(1)} %all-to-all-done.got, bf16[8,256,128]{2,1,0:T(8,128)(2,1)S(1)} %all_to_all.21.stats.got, bf16[8,256,128]{2,1,0:T(8,128)(2,1)S(1)} %get-tuple-element.33.mine, ...), custom_call_target="tpu_custom_call" | custom-call | flops 1000 | bytes 1000 | tf_op jit(solution)/shard_map/owner_backward/pallas_call | solution.py:443
  77.1 0.0 copy-done
  77.1 3.7 %all-to-all-start.3 = ((bf16[8,256,128]{2,1,0:T(8,128)(2,1)}), bf16[8,256,128]{2,1,0:T(8,128)(2,1)S(1)}, u32[]{:S(2)}, u32[]{:S(2)}) async-start(bf16[8,256,128]{2,1,0:T(8,128)(2,1)} %owner_backward.1), calls=%async_computation.3 | async-start | bytes 1048576 | tf_op jit(solution)/shard_map/all_to_all | solution.py:477
  80.8 0.0 copy-start.4
  80.8 10.2 %local_backward.1 = (bf16[512,640]{1,0:T(8,128)(2,1)}, bf16[3,640,512]{2,1,0:T(8,128)(2,1)}) custom-call(s32[2,8]{1,0:T(2,128)} %offsets.11, bf16[3,640,512]{2,1,0:T(8,128)(2,1)} %get-tuple-element.23.qkvt, bf16[640,512]{1,0:T(8,128)(2,1)} %get-tuple-element.27.gt, bf16[640,512]{1,0:T(8,128)(2,1)} %get-tuple-element.26.l_out, ...), custom_call_target="tpu_custom_call" | custom-call | flops 1000 | bytes 1000 | tf_op jit(solution)/shard_map/local_backward/pallas_call | solution.py:443
  90.9 4.2 %all-to-all-done.3.got = bf16[8,256,128]{2,1,0:T(8,128)(2,1)S(1)} async-done(((bf16[8,256,128]{2,1,0:T(8,128)(2,1)}), bf16[8,256,128]{2,1,0:T(8,128)(2,1)S(1)}, u32[]{:S(2)}, u32[]{:S(2)}) %all-to-all-start.3) | async-done | bytes 524320 | tf_op jit(solution)/shard_map/all_to_all | solution.py:477
  95.1 0.0 copy-done.4
  95.2 1.5 %copy-done.1 = bf16[3,640,512]{2,1,0:T(8,128)(2,1)S(1)} copy-done((bf16[3,640,512]{2,1,0:T(8,128)(2,1)S(1)}, bf16[3,640,512]{2,1,0:T(8,128)(2,1)}, u32[]{:S(2)}) %copy-start.1) | copy-done | bytes 1966104
  96.7 3.1 %final.1 = (bf16[512,640]{1,0:T(8,128)(2,1)}, bf16[512,640]{1,0:T(8,128)(2,1)}, bf16[512,640]{1,0:T(8,128)(2,1)}) custom-call(s32[2,8]{1,0:T(2,128)S(1)} %copy-done.4, bf16[3,640,512]{2,1,0:T(8,128)(2,1)S(1)} %copy-done.1, bf16[8,256,128]{2,1,0:T(8,128)(2,1)S(1)} %all-to-all-done.3.got), custom_call_target="tpu_custom_call" | custom-call | flops 1000 | bytes 1000 | tf_op jit(solution)/shard_map/final/pallas_call | solution.py:443
  (5 shorter events, 0.0 us)
Async XLA Ops:
  0.6 19.2 %copy-start.5 = (bf16[512,640]{1,0:T(8,128)(2,1)S(1)}, bf16[512,640]{1,0:T(8,128)(2,1)}, u32[]{:S(2)}) copy-start(bf16[512,640]{1,0:T(8,128)(2,1)} %c0.1) | copy-start | bytes 1966084
  0.6 19.3 %collective-permute-start.1 = (bf16[512,640]{1,0:T(8,128)(2,1)}, bf16[512,640]{1,0:T(8,128)(2,1)S(1)}, u32[]{:S(2)}, u32[]{:S(2)}) collective-permute-start(bf16[512,640]{1,0:T(8,128)(2,1)} %c0.1), channel_id=1, source_target_pairs={{0,2},{1,3},{2,0},{3,1},{4,6},{5,7},{6,4},{7,5},{8,10},{9,11},{10,... | collective-permute-start | bytes 1966088 | tf_op jit(solution)/shard_map/ppermute | solution.py:483
  11.3 25.7 %all-to-all-start = ((bf16[8,256,128]{2,1,0:T(8,128)(2,1)}), bf16[8,256,128]{2,1,0:T(8,128)(2,1)S(1)}, u32[]{:S(2)}, u32[]{:S(2)}) async-start(bf16[8,256,128]{2,1,0:T(8,128)(2,1)} %get-tuple-element.28), calls=%async_computation | async-start | bytes 1048576 | tf_op jit(solution)/shard_map/all_to_all | solution.py:477
  19.8 2.2 %collective-permute-start = (bf16[512,640]{1,0:T(8,128)(2,1)S(1)}, bf16[512,640]{1,0:T(8,128)(2,1)S(1)}, u32[]{:S(2)}, u32[]{:S(2)}) collective-permute-start(bf16[512,640]{1,0:T(8,128)(2,1)S(1)} %copy-done.5), channel_id=1, source_target_pairs={{0,1},{1,0},{2,3},{3,2},{4,5},{5,4},{6,7},{7,6},{8,9},{9,8},{10,11... | collective-permute-start | bytes 1966088 | tf_op jit(solution)/shard_map/ppermute | solution.py:483
  19.9 3.9 %copy-start.6 = (bf16[512,640]{1,0:T(8,128)(2,1)}, bf16[512,640]{1,0:T(8,128)(2,1)S(1)}, u32[]{:S(2)}) copy-start(bf16[512,640]{1,0:T(8,128)(2,1)S(1)} %collective-permute-done.1.c2) | copy-start | bytes 1966084
  19.9 3.0 %collective-permute-start.2 = (bf16[512,640]{1,0:T(8,128)(2,1)S(1)}, bf16[512,640]{1,0:T(8,128)(2,1)S(1)}, u32[]{:S(2)}, u32[]{:S(2)}) collective-permute-start(bf16[512,640]{1,0:T(8,128)(2,1)S(1)} %collective-permute-done.1.c2), channel_id=1, source_target_pairs={{0,1},{1,0},{2,3},{3,2},{4,5},{5,4},{6,7},{7,6},{8,9},{9,8},{10,11... | collective-permute-start | bytes 1966088 | tf_op jit(solution)/shard_map/ppermute | solution.py:483
  22.0 1.8 %copy-start.7 = (bf16[512,640]{1,0:T(8,128)(2,1)}, bf16[512,640]{1,0:T(8,128)(2,1)S(1)}, u32[]{:S(2)}) copy-start(bf16[512,640]{1,0:T(8,128)(2,1)S(1)} %collective-permute-done.c1) | copy-start | bytes 1966084
  22.9 0.8 copy-start.8
  23.8 13.2 %copy-start.3 = (s32[2,8]{1,0:T(2,128)S(1)}, s32[2,8]{1,0:T(2,128)}, u32[]{:S(2)}) copy-start(s32[2,8]{1,0:T(2,128)} %offsets.11) | copy-start | bytes 196
  37.0 0.9 copy-start.2
  73.1 4.0 %copy-start = (bf16[8,256,128]{2,1,0:T(8,128)(2,1)}, bf16[8,256,128]{2,1,0:T(8,128)(2,1)S(1)}, u32[]{:S(2)}) copy-start(bf16[8,256,128]{2,1,0:T(8,128)(2,1)S(1)} %all_to_all.21.stats.got) | copy-start | bytes 1572868
  77.1 18.1 %all-to-all-start.3 = ((bf16[8,256,128]{2,1,0:T(8,128)(2,1)}), bf16[8,256,128]{2,1,0:T(8,128)(2,1)S(1)}, u32[]{:S(2)}, u32[]{:S(2)}) async-start(bf16[8,256,128]{2,1,0:T(8,128)(2,1)} %owner_backward.1), calls=%async_computation.3 | async-start | bytes 1048576 | tf_op jit(solution)/shard_map/all_to_all | solution.py:477
  80.8 14.4 %copy-start.4 = (s32[2,8]{1,0:T(2,128)S(1)}, s32[2,8]{1,0:T(2,128)}, u32[]{:S(2)}) copy-start(s32[2,8]{1,0:T(2,128)} %offsets.11) | copy-start | bytes 196
  95.2 1.5 %copy-start.1 = (bf16[3,640,512]{2,1,0:T(8,128)(2,1)S(1)}, bf16[3,640,512]{2,1,0:T(8,128)(2,1)}, u32[]{:S(2)}) copy-start(bf16[3,640,512]{2,1,0:T(8,128)(2,1)} %get-tuple-element.38.grads) | copy-start | bytes 5898244

commit v5 on v4

--- a/solution.py
+++ b/solution.py
@@ -283,7 +283,7 @@
     return pl.ds(pl.multiple_of(lax.axis_index("seq") // 8 * 64, 64), 64)
 
 
-def far_forward_kernel(d, factor, got, near, norm, msg, turned):
+def far_forward_kernel(d, factor, got, near, norm, msg, own, turned):
     block = far_block(got)
     tokens = block.shape[1]
     diag = causal_mask(tokens // 2)
@@ -293,11 +293,16 @@
     turned[...] = stack.T
     mine = turned[column_rows(), :].reshape(8, 8, 128)
     msg[:, : 2 * d + 16] = near[...]
+    own[...] = mine
     rows = got[:, :, 16:, :].astype(F32)
+    used = d + 6
     for h in range(msg.shape[0]):
         far = rows[:, h, 8:, :].reshape(64, 128)
-        msg[h, 2 * d + 16 : 2 * d + 80] = far.astype(BF16)
-    msg[:, 2 * d + 80 :] = jnp.concatenate([mine, jnp.zeros_like(mine)], axis=1).astype(BF16)
+        first = jnp.concatenate([far[:8, :used], mine[h, :, : 128 - used]], axis=1)
+        tail = mine[h, :, 128 - used : 2 * (128 - used)]
+        second = jnp.concatenate([far[8:16, :used], tail], axis=1)
+        far = jnp.concatenate([first, second, far[16:]], axis=0)
+        msg[h, 2 * d + 16 :] = far.astype(BF16)
 
 
 def near_stats(d, stats, outs, part):
@@ -324,7 +329,7 @@
         g, local_norm, local_dot, near_dot = near_stats(d, stats, outs, part)
         far_norms, far_dots = [], []
         for z in range(NEAR):
-            rows = mine[4 * part + z, 2 * d + 80 :, :].astype(F32)[:8]
+            rows = mine[4 * part + z]
             grads = rows_buf[4 * part + z, plane, :]
             dot = jnp.sum(jnp.where(lane < d, rows * grads, 0.0), axis=1, keepdims=True)
             log = jnp.sum(jnp.where(same, sum3(rows, d, 1), 0.0), axis=0, keepdims=True)
@@ -381,7 +386,8 @@
         near = nn(got[h, d : 2 * d + 16, :], place_matrix(tokens, count, offsets[0, h]))
         near_norm = jnp.where(lane % NEAR == offsets[0, h], sum3(near, d + 6, 0), NEG)
         place = iota((8, tokens), 1) == iota((8, tokens), 0) * 64 + offsets[1, h]
-        came = got[h, 2 * d + 80 :, :].astype(F32)[:8]
+        came = got[h, 2 * d + 16 : 2 * d + 32, :].astype(F32)
+        came = jnp.concatenate([came[:8, d + 6 :], came[8:, d + 6 :]], axis=1)
         spread = jnp.sum(jnp.where(place, sum3(came, d, 1), 0.0), axis=0, keepdims=True)
         far_norm = jnp.where(lane % 64 == offsets[1, h], spread, NEG)
         far_out = tn(came[:, :d].astype(BF16), one_hot(place))
@@ -539,13 +545,14 @@
         limit=16_000_000,
     )
     far_got = over_plane(shared)
-    far_norm, swap_msg = call(
+    far_norm, swap_msg, own_far = call(
         functools.partial(far_forward_kernel, d, factor),
         "far_forward",
         [(far_got, "v"), (near_out, "v")],
         [
             (struct((8, tokens), F32), "v"),
-            (struct((heads, 256, 128), BF16), "v"),
+            (struct((heads, 240, 128), BF16), "v"),
+            (struct((heads, 8, 128), F32), "v"),
         ],
         scratch=[vmem(tokens, 128, dtype=F32)],
         limit=16_000_000,
@@ -554,7 +561,7 @@
     (grad_msg,) = call(
         functools.partial(owner_backward_kernel, heads, d, factor, scale),
         "owner_backward",
-        [(offsets, "s"), (rows_got, "v"), (swap_got, "v"), (swap_msg, "v"), (near_out, "v")]
+        [(offsets, "s"), (rows_got, "v"), (swap_got, "v"), (own_far, "v"), (near_out, "v")]
         + [(near_norm, "v"), (far_got, "v"), (far_norm, "v")],
         [(struct((heads, 256, 128), BF16), "v")],
         scratch=[

time: 101 us -> 100 us (0.990)
  no operation moved by 1% of the time
where the time goes in v5:
time: 100 us; the launch traced here: 99.5 us
  Pallas kernels  35.7 us (36%)
  blocking collectives  31.3 us (31%)
  starting transfers between devices  15.1 us (15%)
  waiting for transfers between devices  13.2 us (13%)
  local copies, waits for them, and re-layouts  3.35 us (3%)
    pallas_call x7, Pallas kernels, call(): pl.pallas_call(kernel, name=name, out_shape=shapes, in_specs=[pl.BlockSpe...  35.7 us
    all_to_all x1, blocking collectives, along_column(): return lax.all_to_all(x, 'seq', 0, 0, tiled=True, axis_index_groups=columns)  17.8 us
    all_to_all x1, blocking collectives, over_plane(): lax.all_to_all(copies, 'seq', 0, 0, tiled=True, axis_index_groups=planes)  13.4 us
    all_to_all x2, starting transfers between devices, along_column(): return lax.all_to_all(x, 'seq', 0, 0, tiled=True, axis_index_groups=columns)  12.2 us
    all_to_all x2, waiting for transfers between devices, along_column(): return lax.all_to_all(x, 'seq', 0, 0, tiled=True, axis_index_groups=columns)  10.7 us
    unnamed x18, local copies, waits for them, and re-layouts  3.35 us
    ppermute x3, starting transfers between devices, flipped(): return lax.ppermute(x, 'head', [(i, i ^ bit) for i in range(4)])  2.95 us
    ppermute x3, waiting for transfers between devices, flipped(): return lax.ppermute(x, 'head', [(i, i ^ bit) for i in range(4)])  2.52 us
  transfers between devices with their start and end apart: 5, of which 4 were waited for; matrix products, arithmetic and copies ran while one was open for 0% of the time, Pallas kernels for 25%

profile of v5, /device:TPU:8, one launch (start us, length us, event | category | flops | bytes accessed | tf_op | source)
XLA Modules:
  0.0 99.5 jit_solution(12425828774233447442)
XLA Ops:
  0.6 0.0 copy-start.5
  0.6 2.4 %collective-permute-start.1 = (bf16[512,640]{1,0:T(8,128)(2,1)}, bf16[512,640]{1,0:T(8,128)(2,1)S(1)}, u32[]{:S(2)}, u32[]{:S(2)}) collective-permute-start(bf16[512,640]{1,0:T(8,128)(2,1)} %c0.1), channel_id=1, source_target_pairs={{0,2},{1,3},{2,0},{3,1},{4,6},{5,7},{6,4},{7,5},{8,10},{9,11},{10,... | collective-permute-start | bytes 1966088 | tf_op jit(solution)/shard_map/ppermute | solution.py:489
  3.0 8.3 %local_forward.1 = (bf16[3,640,512]{2,1,0:T(8,128)(2,1)}, bf16[8,256,128]{2,1,0:T(8,128)(2,1)}, bf16[640,512]{1,0:T(8,128)(2,1)}, f32[8,512]{1,0:T(8,128)}) custom-call(s32[2,8]{1,0:T(2,128)} %offsets.11, bf16[512,640]{1,0:T(8,128)(2,1)} %q.1, bf16[512,640]{1,0:T(8,128)(2,1)} %k.1, bf16[512,640]{1,0:T(8,128)(2,1)} %v.1), custom_call_target="tpu_custom_call" | custom-call | flops 1000 | bytes 1000 | tf_op jit(solution)/shard_map/local_forward/pallas_call | solution.py:449
  11.3 8.5 %all-to-all-start = ((bf16[8,256,128]{2,1,0:T(8,128)(2,1)}), bf16[8,256,128]{2,1,0:T(8,128)(2,1)S(1)}, u32[]{:S(2)}, u32[]{:S(2)}) async-start(bf16[8,256,128]{2,1,0:T(8,128)(2,1)} %get-tuple-element.29), calls=%async_computation | async-start | bytes 1048576 | tf_op jit(solution)/shard_map/all_to_all | solution.py:483
  19.8 0.0 copy-done.5
  19.8 0.1 collective-permute-start
  19.9 0.0 collective-permute-done.1.c2
  19.9 0.0 copy-start.6
  19.9 0.5 collective-permute-start.2
  20.4 1.6 %collective-permute-done.c1 = bf16[512,640]{1,0:T(8,128)(2,1)S(1)} collective-permute-done((bf16[512,640]{1,0:T(8,128)(2,1)S(1)}, bf16[512,640]{1,0:T(8,128)(2,1)S(1)}, u32[]{:S(2)}, u32[]{:S(2)}) %collective-permute-start) | collective-permute-done | bytes 655392 | tf_op jit(solution)/shard_map/ppermute | solution.py:489
  22.0 0.0 copy-start.7
  22.0 0.9 collective-permute-done.2.c3
  22.9 0.8 copy-done.8
  23.8 0.0 copy-done.6
  23.8 0.0 copy-done.7
  23.8 6.7 %stats.1 = (bf16[640,512]{1,0:T(8,128)(2,1)}, bf16[8,112,128]{2,1,0:T(8,128)(2,1)}) custom-call(s32[2,8]{1,0:T(2,128)} %offsets.11, bf16[640,2560]{1,0:T(8,128)(2,1)} %w.1, bf16[512,640]{1,0:T(8,128)(2,1)} %c0.1, bf16[512,640]{1,0:T(8,128)(2,1)} %copy-done.7, bf16[512,640]{1,0:T(8,128)(2,1)} %copy-done.6, bf16[512,640]{1,0:T(8,128)(2,1)} %copy-done.8, ...), custom_call_target="tpu_custom_call" | custom-call | flops 1000 | bytes 1000 | tf_op jit(solution)/shard_map/stats/pallas_call | solution.py:449
  30.5 6.6 %all-to-all-done.got = bf16[8,256,128]{2,1,0:T(8,128)(2,1)S(1)} async-done(((bf16[8,256,128]{2,1,0:T(8,128)(2,1)}), bf16[8,256,128]{2,1,0:T(8,128)(2,1)S(1)}, u32[]{:S(2)}, u32[]{:S(2)}) %all-to-all-start) | async-done | bytes 524320 | tf_op jit(solution)/shard_map/all_to_all | solution.py:483
  37.0 0.0 copy-done.3
  37.0 0.9 copy-done.2
  38.0 2.3 %near_forward.1 = (bf16[8,176,128]{2,1,0:T(8,128)(2,1)S(1)}, f32[2,512]{1,0:T(2,128)S(1)}, bf16[8,8,32,128]{3,2,1,0:T(8,128)(2,1)S(1)}) custom-call(s32[2,8]{1,0:T(2,128)S(1)} %copy-done.3, bf16[8,256,128]{2,1,0:T(8,128)(2,1)S(1)} %all-to-all-done.got, bf16[8,112,128]{2,1,0:T(8,128)(2,1)S(1)} %copy-done.2), custom_call_target="tpu_custom_call" | custom-call | flops 1000 | bytes 1000 | tf_op jit(solution)/shard_map/near_forward/pallas_call | solution.py:449
  40.3 13.4 %all_to_all.20.got.plane_got = bf16[8,8,32,128]{3,2,1,0:T(8,128)(2,1)S(1)} all-to-all(bf16[8,8,32,128]{3,2,1,0:T(8,128)(2,1)S(1)} %get-tuple-element.32), channel_id=1, replica_groups={{0,32,64,96,128,160,192,224},{4,36,68,100,132,164,196,228},{8,40,72,104..., dimensions={0} | all-to-all | bytes 1048576 | tf_op jit(solution)/shard_map/all_to_all | solution.py:486
  53.7 0.9 far_forward.1
  54.6 17.8 %all_to_all.21.stats.got = bf16[8,240,128]{2,1,0:T(8,128)(2,1)S(1)} all-to-all(bf16[8,240,128]{2,1,0:T(8,128)(2,1)S(1)} %get-tuple-element.34), channel_id=1, replica_groups={{0,4,8,12,16,20,24,28},{32,36,40,44,48,52,56,60},{64,68,72,76,80,84,88,..., dimensions={0} | all-to-all | bytes 983040 | tf_op jit(solution)/shard_map/all_to_all | solution.py:483
  72.4 4.0 %owner_backward.1 = bf16[8,256,128]{2,1,0:T(8,128)(2,1)} custom-call(s32[2,8]{1,0:T(2,128)S(1)} %copy-done.3, bf16[8,256,128]{2,1,0:T(8,128)(2,1)S(1)} %all-to-all-done.got, bf16[8,240,128]{2,1,0:T(8,128)(2,1)S(1)} %all_to_all.21.stats.got, f32[8,8,128]{2,1,0:T(8,128)S(1)} %get-tuple-element.35.mine, bf16[8,176,128]{2,1,0:T(8,128)(2,1)S(1)} %get-tuple-element.33.near.outs, ...), custom_call_target="tpu_custom_call" | custom-call | flops 1000 | bytes 1000 | tf_op jit(solution)/shard_map/owner_backward/pallas_call | solution.py:449
  76.5 3.7 %all-to-all-start.3 = ((bf16[8,256,128]{2,1,0:T(8,128)(2,1)}), bf16[8,256,128]{2,1,0:T(8,128)(2,1)S(1)}, u32[]{:S(2)}, u32[]{:S(2)}) async-start(bf16[8,256,128]{2,1,0:T(8,128)(2,1)} %owner_backward.1), calls=%async_computation.3 | async-start | bytes 1048576 | tf_op jit(solution)/shard_map/all_to_all | solution.py:483
  80.2 0.0 copy-start.4
  80.2 0.0 copy-done
  80.2 10.3 %local_backward.1 = (bf16[512,640]{1,0:T(8,128)(2,1)}, bf16[3,640,512]{2,1,0:T(8,128)(2,1)}) custom-call(s32[2,8]{1,0:T(2,128)} %offsets.11, bf16[3,640,512]{2,1,0:T(8,128)(2,1)} %get-tuple-element.24.qkvt, bf16[640,512]{1,0:T(8,128)(2,1)} %get-tuple-element.28.gt, bf16[640,512]{1,0:T(8,128)(2,1)} %get-tuple-element.27.l_out, ...), custom_call_target="tpu_custom_call" | custom-call | flops 1000 | bytes 1000 | tf_op jit(solution)/shard_map/local_backward/pallas_call | solution.py:449
  90.5 4.1 %all-to-all-done.3.got = bf16[8,256,128]{2,1,0:T(8,128)(2,1)S(1)} async-done(((bf16[8,256,128]{2,1,0:T(8,128)(2,1)}), bf16[8,256,128]{2,1,0:T(8,128)(2,1)S(1)}, u32[]{:S(2)}, u32[]{:S(2)}) %all-to-all-start.3) | async-done | bytes 524320 | tf_op jit(solution)/shard_map/all_to_all | solution.py:483
  94.6 0.0 copy-done.4
  94.6 1.5 %copy-done.1 = bf16[3,640,512]{2,1,0:T(8,128)(2,1)S(1)} copy-done((bf16[3,640,512]{2,1,0:T(8,128)(2,1)S(1)}, bf16[3,640,512]{2,1,0:T(8,128)(2,1)}, u32[]{:S(2)}) %copy-start.1) | copy-done | bytes 1966104
  96.2 3.1 %final.1 = (bf16[512,640]{1,0:T(8,128)(2,1)}, bf16[512,640]{1,0:T(8,128)(2,1)}, bf16[512,640]{1,0:T(8,128)(2,1)}) custom-call(s32[2,8]{1,0:T(2,128)S(1)} %copy-done.4, bf16[3,640,512]{2,1,0:T(8,128)(2,1)S(1)} %copy-done.1, bf16[8,256,128]{2,1,0:T(8,128)(2,1)S(1)} %all-to-all-done.3.got), custom_call_target="tpu_custom_call" | custom-call | flops 1000 | bytes 1000 | tf_op jit(solution)/shard_map/final/pallas_call | solution.py:449
  (5 shorter events, 0.0 us)
Async XLA Ops:
  0.6 19.2 %copy-start.5 = (bf16[512,640]{1,0:T(8,128)(2,1)S(1)}, bf16[512,640]{1,0:T(8,128)(2,1)}, u32[]{:S(2)}) copy-start(bf16[512,640]{1,0:T(8,128)(2,1)} %c0.1) | copy-start | bytes 1966084
  0.6 19.3 %collective-permute-start.1 = (bf16[512,640]{1,0:T(8,128)(2,1)}, bf16[512,640]{1,0:T(8,128)(2,1)S(1)}, u32[]{:S(2)}, u32[]{:S(2)}) collective-permute-start(bf16[512,640]{1,0:T(8,128)(2,1)} %c0.1), channel_id=1, source_target_pairs={{0,2},{1,3},{2,0},{3,1},{4,6},{5,7},{6,4},{7,5},{8,10},{9,11},{10,... | collective-permute-start | bytes 1966088 | tf_op jit(solution)/shard_map/ppermute | solution.py:489
  11.3 25.7 %all-to-all-start = ((bf16[8,256,128]{2,1,0:T(8,128)(2,1)}), bf16[8,256,128]{2,1,0:T(8,128)(2,1)S(1)}, u32[]{:S(2)}, u32[]{:S(2)}) async-start(bf16[8,256,128]{2,1,0:T(8,128)(2,1)} %get-tuple-element.29), calls=%async_computation | async-start | bytes 1048576 | tf_op jit(solution)/shard_map/all_to_all | solution.py:483
  19.8 2.2 %collective-permute-start = (bf16[512,640]{1,0:T(8,128)(2,1)S(1)}, bf16[512,640]{1,0:T(8,128)(2,1)S(1)}, u32[]{:S(2)}, u32[]{:S(2)}) collective-permute-start(bf16[512,640]{1,0:T(8,128)(2,1)S(1)} %copy-done.5), channel_id=1, source_target_pairs={{0,1},{1,0},{2,3},{3,2},{4,5},{5,4},{6,7},{7,6},{8,9},{9,8},{10,11... | collective-permute-start | bytes 1966088 | tf_op jit(solution)/shard_map/ppermute | solution.py:489
  19.9 3.9 %copy-start.6 = (bf16[512,640]{1,0:T(8,128)(2,1)}, bf16[512,640]{1,0:T(8,128)(2,1)S(1)}, u32[]{:S(2)}) copy-start(bf16[512,640]{1,0:T(8,128)(2,1)S(1)} %collective-permute-done.1.c2) | copy-start | bytes 1966084
  19.9 3.0 %collective-permute-start.2 = (bf16[512,640]{1,0:T(8,128)(2,1)S(1)}, bf16[512,640]{1,0:T(8,128)(2,1)S(1)}, u32[]{:S(2)}, u32[]{:S(2)}) collective-permute-start(bf16[512,640]{1,0:T(8,128)(2,1)S(1)} %collective-permute-done.1.c2), channel_id=1, source_target_pairs={{0,1},{1,0},{2,3},{3,2},{4,5},{5,4},{6,7},{7,6},{8,9},{9,8},{10,11... | collective-permute-start | bytes 1966088 | tf_op jit(solution)/shard_map/ppermute | solution.py:489
  22.0 1.8 %copy-start.7 = (bf16[512,640]{1,0:T(8,128)(2,1)}, bf16[512,640]{1,0:T(8,128)(2,1)S(1)}, u32[]{:S(2)}) copy-start(bf16[512,640]{1,0:T(8,128)(2,1)S(1)} %collective-permute-done.c1) | copy-start | bytes 1966084
  22.9 0.8 copy-start.8
  23.8 13.2 %copy-start.3 = (s32[2,8]{1,0:T(2,128)S(1)}, s32[2,8]{1,0:T(2,128)}, u32[]{:S(2)}) copy-start(s32[2,8]{1,0:T(2,128)} %offsets.11) | copy-start | bytes 196
  37.0 0.9 copy-start.2
  72.4 7.7 %copy-start = (bf16[8,240,128]{2,1,0:T(8,128)(2,1)}, bf16[8,240,128]{2,1,0:T(8,128)(2,1)S(1)}, u32[]{:S(2)}) copy-start(bf16[8,240,128]{2,1,0:T(8,128)(2,1)S(1)} %all_to_all.21.stats.got) | copy-start | bytes 1474564
  76.5 18.1 %all-to-all-start.3 = ((bf16[8,256,128]{2,1,0:T(8,128)(2,1)}), bf16[8,256,128]{2,1,0:T(8,128)(2,1)S(1)}, u32[]{:S(2)}, u32[]{:S(2)}) async-start(bf16[8,256,128]{2,1,0:T(8,128)(2,1)} %owner_backward.1), calls=%async_computation.3 | async-start | bytes 1048576 | tf_op jit(solution)/shard_map/all_to_all | solution.py:483
  80.2 14.5 %copy-start.4 = (s32[2,8]{1,0:T(2,128)S(1)}, s32[2,8]{1,0:T(2,128)}, u32[]{:S(2)}) copy-start(s32[2,8]{1,0:T(2,128)} %offsets.11) | copy-start | bytes 196
  94.6 1.5 %copy-start.1 = (bf16[3,640,512]{2,1,0:T(8,128)(2,1)S(1)}, bf16[3,640,512]{2,1,0:T(8,128)(2,1)}, u32[]{:S(2)}) copy-start(bf16[3,640,512]{2,1,0:T(8,128)(2,1)} %get-tuple-element.40.grads) | copy-start | bytes 5898244

commit v6 on v5

--- a/solution.py
+++ b/solution.py
@@ -315,7 +315,7 @@
 
 def owner_backward_kernel(
     heads, d, factor, scale, offsets, got, stats, mine, outs, near_norm, plane_got,
-    far_norm, msg, rows_buf, turned,
+    far_norm, sent, rows_buf, turned, msg, sems,
 ):
     rows_buf[...] = stats[:, 2 * d + 16 : 2 * d + 80].astype(F32)
     near_offset, far_offset = my_offsets(offsets, heads)
@@ -347,6 +347,8 @@
             packed = grads[slot].astype(BF16)
             for z in range(NEAR):
                 msg[4 * part + z, slot * d : (slot + 1) * d] = packed[:, z * 128 : (z + 1) * 128]
+    near_part, far_part = pl.ds(0, 3 * d), pl.ds(3 * d, 16)
+    store = fetch(msg.at[:, near_part], sent.at[:, near_part], sems.at[0])
     block = far_block(plane_got)
     qt, kt, vt = block[:d], block[d : 2 * d], block[2 * d : 3 * d]
     pieces = [rows_buf[z, 8 * a : 8 * a + 8, :] for a in range(8) for z in range(heads)]
@@ -367,6 +369,7 @@
     msg[:, 3 * d :] = jnp.concatenate(
         [picked[:, :128].reshape(8, 8, 128), picked[:, 128:].reshape(8, 8, 128)], axis=1
     ).astype(BF16)
+    wait_all([store, fetch(msg.at[:, far_part], sent.at[:, far_part], sems.at[1])])
 
 
 def local_backward_kernel(
@@ -563,10 +566,12 @@
         "owner_backward",
         [(offsets, "s"), (rows_got, "v"), (swap_got, "v"), (own_far, "v"), (near_out, "v")]
         + [(near_norm, "v"), (far_got, "v"), (far_norm, "v")],
-        [(struct((heads, 256, 128), BF16), "v")],
+        [(struct((heads, 256, 128), BF16), "h")],
         scratch=[
             vmem(heads, 64, 128, dtype=F32),
             vmem(tokens, 256, dtype=F32),
+            vmem(heads, 256, 128),
+            dma((2,)),
         ],
         limit=16_000_000,
     )

time: 100 us -> 99.8 us (level)
  no operation moved by 1% of the time
where the time goes in v6:
time: 99.8 us; the launch traced here: 99.3 us
  Pallas kernels  35.5 us (36%)
  blocking collectives  31.3 us (31%)
  starting transfers between devices  15.1 us (15%)
  waiting for transfers between devices  13.2 us (13%)
  local copies, waits for them, and re-layouts  3.35 us (3%)
    pallas_call x7, Pallas kernels, call(): pl.pallas_call(kernel, name=name, out_shape=shapes, in_specs=[pl.BlockSpe...  35.5 us
    all_to_all x1, blocking collectives, along_column(): return lax.all_to_all(x, 'seq', 0, 0, tiled=True, axis_index_groups=columns)  17.8 us
    all_to_all x1, blocking collectives, over_plane(): lax.all_to_all(copies, 'seq', 0, 0, tiled=True, axis_index_groups=planes)  13.4 us
    all_to_all x2, starting transfers between devices, along_column(): return lax.all_to_all(x, 'seq', 0, 0, tiled=True, axis_index_groups=columns)  12.2 us
    all_to_all x2, waiting for transfers between devices, along_column(): return lax.all_to_all(x, 'seq', 0, 0, tiled=True, axis_index_groups=columns)  10.7 us
    unnamed x18, local copies, waits for them, and re-layouts  3.35 us
    ppermute x3, starting transfers between devices, flipped(): return lax.ppermute(x, 'head', [(i, i ^ bit) for i in range(4)])  2.95 us
    ppermute x3, waiting for transfers between devices, flipped(): return lax.ppermute(x, 'head', [(i, i ^ bit) for i in range(4)])  2.52 us
  transfers between devices with their start and end apart: 5, of which 4 were waited for; matrix products, arithmetic and copies ran while one was open for 0% of the time, Pallas kernels for 25%

profile of v6, /device:TPU:8, one launch (start us, length us, event | category | flops | bytes accessed | tf_op | source)
XLA Modules:
  0.0 99.3 jit_solution(14933294734088660128)
XLA Ops:
  0.6 0.0 copy-start.5
  0.6 2.4 %collective-permute-start.1 = (bf16[512,640]{1,0:T(8,128)(2,1)}, bf16[512,640]{1,0:T(8,128)(2,1)S(1)}, u32[]{:S(2)}, u32[]{:S(2)}) collective-permute-start(bf16[512,640]{1,0:T(8,128)(2,1)} %c0.1), channel_id=1, source_target_pairs={{0,2},{1,3},{2,0},{3,1},{4,6},{5,7},{6,4},{7,5},{8,10},{9,11},{10,... | collective-permute-start | bytes 1966088 | tf_op jit(solution)/shard_map/ppermute | solution.py:492
  3.0 8.3 %local_forward.1 = (bf16[3,640,512]{2,1,0:T(8,128)(2,1)}, bf16[8,256,128]{2,1,0:T(8,128)(2,1)}, bf16[640,512]{1,0:T(8,128)(2,1)}, f32[8,512]{1,0:T(8,128)}) custom-call(s32[2,8]{1,0:T(2,128)} %offsets.11, bf16[512,640]{1,0:T(8,128)(2,1)} %q.1, bf16[512,640]{1,0:T(8,128)(2,1)} %k.1, bf16[512,640]{1,0:T(8,128)(2,1)} %v.1), custom_call_target="tpu_custom_call" | custom-call | flops 1000 | bytes 1000 | tf_op jit(solution)/shard_map/local_forward/pallas_call | solution.py:452
  11.3 8.5 %all-to-all-start = ((bf16[8,256,128]{2,1,0:T(8,128)(2,1)}), bf16[8,256,128]{2,1,0:T(8,128)(2,1)S(1)}, u32[]{:S(2)}, u32[]{:S(2)}) async-start(bf16[8,256,128]{2,1,0:T(8,128)(2,1)} %get-tuple-element.29), calls=%async_computation | async-start | bytes 1048576 | tf_op jit(solution)/shard_map/all_to_all | solution.py:486
  19.8 0.0 copy-done.5
  19.8 0.1 collective-permute-start
  19.9 0.0 collective-permute-done.1.c2
  19.9 0.0 copy-start.6
  19.9 0.5 collective-permute-start.2
  20.4 1.6 %collective-permute-done.c1 = bf16[512,640]{1,0:T(8,128)(2,1)S(1)} collective-permute-done((bf16[512,640]{1,0:T(8,128)(2,1)S(1)}, bf16[512,640]{1,0:T(8,128)(2,1)S(1)}, u32[]{:S(2)}, u32[]{:S(2)}) %collective-permute-start) | collective-permute-done | bytes 655392 | tf_op jit(solution)/shard_map/ppermute | solution.py:492
  22.0 0.0 copy-start.7
  22.0 0.9 collective-permute-done.2.c3
  22.9 0.8 copy-done.8
  23.8 0.0 copy-done.6
  23.8 0.0 copy-done.7
  23.8 6.7 %stats.1 = (bf16[640,512]{1,0:T(8,128)(2,1)}, bf16[8,112,128]{2,1,0:T(8,128)(2,1)}) custom-call(s32[2,8]{1,0:T(2,128)} %offsets.11, bf16[640,2560]{1,0:T(8,128)(2,1)} %w.1, bf16[512,640]{1,0:T(8,128)(2,1)} %c0.1, bf16[512,640]{1,0:T(8,128)(2,1)} %copy-done.7, bf16[512,640]{1,0:T(8,128)(2,1)} %copy-done.6, bf16[512,640]{1,0:T(8,128)(2,1)} %copy-done.8, ...), custom_call_target="tpu_custom_call" | custom-call | flops 1000 | bytes 1000 | tf_op jit(solution)/shard_map/stats/pallas_call | solution.py:452
  30.5 6.6 %all-to-all-done.got = bf16[8,256,128]{2,1,0:T(8,128)(2,1)S(1)} async-done(((bf16[8,256,128]{2,1,0:T(8,128)(2,1)}), bf16[8,256,128]{2,1,0:T(8,128)(2,1)S(1)}, u32[]{:S(2)}, u32[]{:S(2)}) %all-to-all-start) | async-done | bytes 524320 | tf_op jit(solution)/shard_map/all_to_all | solution.py:486
  37.0 0.0 copy-done.3
  37.0 0.9 copy-done.2
  38.0 2.3 %near_forward.1 = (bf16[8,176,128]{2,1,0:T(8,128)(2,1)S(1)}, f32[2,512]{1,0:T(2,128)S(1)}, bf16[8,8,32,128]{3,2,1,0:T(8,128)(2,1)S(1)}) custom-call(s32[2,8]{1,0:T(2,128)S(1)} %copy-done.3, bf16[8,256,128]{2,1,0:T(8,128)(2,1)S(1)} %all-to-all-done.got, bf16[8,112,128]{2,1,0:T(8,128)(2,1)S(1)} %copy-done.2), custom_call_target="tpu_custom_call" | custom-call | flops 1000 | bytes 1000 | tf_op jit(solution)/shard_map/near_forward/pallas_call | solution.py:452
  40.3 13.4 %all_to_all.20.got.plane_got = bf16[8,8,32,128]{3,2,1,0:T(8,128)(2,1)S(1)} all-to-all(bf16[8,8,32,128]{3,2,1,0:T(8,128)(2,1)S(1)} %get-tuple-element.32), channel_id=1, replica_groups={{0,32,64,96,128,160,192,224},{4,36,68,100,132,164,196,228},{8,40,72,104..., dimensions={0} | all-to-all | bytes 1048576 | tf_op jit(solution)/shard_map/all_to_all | solution.py:489
  53.7 0.9 far_forward.1
  54.6 17.8 %all_to_all.21.stats.got = bf16[8,240,128]{2,1,0:T(8,128)(2,1)S(1)} all-to-all(bf16[8,240,128]{2,1,0:T(8,128)(2,1)S(1)} %get-tuple-element.34), channel_id=1, replica_groups={{0,4,8,12,16,20,24,28},{32,36,40,44,48,52,56,60},{64,68,72,76,80,84,88,..., dimensions={0} | all-to-all | bytes 983040 | tf_op jit(solution)/shard_map/all_to_all | solution.py:486
  72.4 3.9 %owner_backward.1 = bf16[8,256,128]{2,1,0:T(8,128)(2,1)} custom-call(s32[2,8]{1,0:T(2,128)S(1)} %copy-done.3, bf16[8,256,128]{2,1,0:T(8,128)(2,1)S(1)} %all-to-all-done.got, bf16[8,240,128]{2,1,0:T(8,128)(2,1)S(1)} %all_to_all.21.stats.got, f32[8,8,128]{2,1,0:T(8,128)S(1)} %get-tuple-element.35.mine, bf16[8,176,128]{2,1,0:T(8,128)(2,1)S(1)} %get-tuple-element.33.near.outs, ...), custom_call_target="tpu_custom_call" | custom-call | flops 1000 | bytes 1000 | tf_op jit(solution)/shard_map/owner_backward/pallas_call | solution.py:452
  76.3 3.7 %all-to-all-start.3 = ((bf16[8,256,128]{2,1,0:T(8,128)(2,1)}), bf16[8,256,128]{2,1,0:T(8,128)(2,1)S(1)}, u32[]{:S(2)}, u32[]{:S(2)}) async-start(bf16[8,256,128]{2,1,0:T(8,128)(2,1)} %owner_backward.1), calls=%async_computation.3 | async-start | bytes 1048576 | tf_op jit(solution)/shard_map/all_to_all | solution.py:486
  80.0 0.0 copy-start.4
  80.0 0.0 copy-done
  80.0 10.3 %local_backward.1 = (bf16[512,640]{1,0:T(8,128)(2,1)}, bf16[3,640,512]{2,1,0:T(8,128)(2,1)}) custom-call(s32[2,8]{1,0:T(2,128)} %offsets.11, bf16[3,640,512]{2,1,0:T(8,128)(2,1)} %get-tuple-element.24.qkvt, bf16[640,512]{1,0:T(8,128)(2,1)} %get-tuple-element.28.gt, bf16[640,512]{1,0:T(8,128)(2,1)} %get-tuple-element.27.l_out, ...), custom_call_target="tpu_custom_call" | custom-call | flops 1000 | bytes 1000 | tf_op jit(solution)/shard_map/local_backward/pallas_call | solution.py:452
  90.4 4.1 %all-to-all-done.3.got = bf16[8,256,128]{2,1,0:T(8,128)(2,1)S(1)} async-done(((bf16[8,256,128]{2,1,0:T(8,128)(2,1)}), bf16[8,256,128]{2,1,0:T(8,128)(2,1)S(1)}, u32[]{:S(2)}, u32[]{:S(2)}) %all-to-all-start.3) | async-done | bytes 524320 | tf_op jit(solution)/shard_map/all_to_all | solution.py:486
  94.5 0.0 copy-done.4
  94.5 1.5 %copy-done.1 = bf16[3,640,512]{2,1,0:T(8,128)(2,1)S(1)} copy-done((bf16[3,640,512]{2,1,0:T(8,128)(2,1)S(1)}, bf16[3,640,512]{2,1,0:T(8,128)(2,1)}, u32[]{:S(2)}) %copy-start.1) | copy-done | bytes 1966104
  96.0 3.1 %final.1 = (bf16[512,640]{1,0:T(8,128)(2,1)}, bf16[512,640]{1,0:T(8,128)(2,1)}, bf16[512,640]{1,0:T(8,128)(2,1)}) custom-call(s32[2,8]{1,0:T(2,128)S(1)} %copy-done.4, bf16[3,640,512]{2,1,0:T(8,128)(2,1)S(1)} %copy-done.1, bf16[8,256,128]{2,1,0:T(8,128)(2,1)S(1)} %all-to-all-done.3.got), custom_call_target="tpu_custom_call" | custom-call | flops 1000 | bytes 1000 | tf_op jit(solution)/shard_map/final/pallas_call | solution.py:452
  (5 shorter events, 0.0 us)
Async XLA Ops:
  0.6 19.2 %copy-start.5 = (bf16[512,640]{1,0:T(8,128)(2,1)S(1)}, bf16[512,640]{1,0:T(8,128)(2,1)}, u32[]{:S(2)}) copy-start(bf16[512,640]{1,0:T(8,128)(2,1)} %c0.1) | copy-start | bytes 1966084
  0.6 19.3 %collective-permute-start.1 = (bf16[512,640]{1,0:T(8,128)(2,1)}, bf16[512,640]{1,0:T(8,128)(2,1)S(1)}, u32[]{:S(2)}, u32[]{:S(2)}) collective-permute-start(bf16[512,640]{1,0:T(8,128)(2,1)} %c0.1), channel_id=1, source_target_pairs={{0,2},{1,3},{2,0},{3,1},{4,6},{5,7},{6,4},{7,5},{8,10},{9,11},{10,... | collective-permute-start | bytes 1966088 | tf_op jit(solution)/shard_map/ppermute | solution.py:492
  11.3 25.7 %all-to-all-start = ((bf16[8,256,128]{2,1,0:T(8,128)(2,1)}), bf16[8,256,128]{2,1,0:T(8,128)(2,1)S(1)}, u32[]{:S(2)}, u32[]{:S(2)}) async-start(bf16[8,256,128]{2,1,0:T(8,128)(2,1)} %get-tuple-element.29), calls=%async_computation | async-start | bytes 1048576 | tf_op jit(solution)/shard_map/all_to_all | solution.py:486
  19.8 2.2 %collective-permute-start = (bf16[512,640]{1,0:T(8,128)(2,1)S(1)}, bf16[512,640]{1,0:T(8,128)(2,1)S(1)}, u32[]{:S(2)}, u32[]{:S(2)}) collective-permute-start(bf16[512,640]{1,0:T(8,128)(2,1)S(1)} %copy-done.5), channel_id=1, source_target_pairs={{0,1},{1,0},{2,3},{3,2},{4,5},{5,4},{6,7},{7,6},{8,9},{9,8},{10,11... | collective-permute-start | bytes 1966088 | tf_op jit(solution)/shard_map/ppermute | solution.py:492
  19.9 3.9 %copy-start.6 = (bf16[512,640]{1,0:T(8,128)(2,1)}, bf16[512,640]{1,0:T(8,128)(2,1)S(1)}, u32[]{:S(2)}) copy-start(bf16[512,640]{1,0:T(8,128)(2,1)S(1)} %collective-permute-done.1.c2) | copy-start | bytes 1966084
  19.9 3.0 %collective-permute-start.2 = (bf16[512,640]{1,0:T(8,128)(2,1)S(1)}, bf16[512,640]{1,0:T(8,128)(2,1)S(1)}, u32[]{:S(2)}, u32[]{:S(2)}) collective-permute-start(bf16[512,640]{1,0:T(8,128)(2,1)S(1)} %collective-permute-done.1.c2), channel_id=1, source_target_pairs={{0,1},{1,0},{2,3},{3,2},{4,5},{5,4},{6,7},{7,6},{8,9},{9,8},{10,11... | collective-permute-start | bytes 1966088 | tf_op jit(solution)/shard_map/ppermute | solution.py:492
  22.0 1.8 %copy-start.7 = (bf16[512,640]{1,0:T(8,128)(2,1)}, bf16[512,640]{1,0:T(8,128)(2,1)S(1)}, u32[]{:S(2)}) copy-start(bf16[512,640]{1,0:T(8,128)(2,1)S(1)} %collective-permute-done.c1) | copy-start | bytes 1966084
  22.9 0.8 copy-start.8
  23.8 13.2 %copy-start.3 = (s32[2,8]{1,0:T(2,128)S(1)}, s32[2,8]{1,0:T(2,128)}, u32[]{:S(2)}) copy-start(s32[2,8]{1,0:T(2,128)} %offsets.11) | copy-start | bytes 196
  37.0 0.9 copy-start.2
  72.4 7.6 %copy-start = (bf16[8,240,128]{2,1,0:T(8,128)(2,1)}, bf16[8,240,128]{2,1,0:T(8,128)(2,1)S(1)}, u32[]{:S(2)}) copy-start(bf16[8,240,128]{2,1,0:T(8,128)(2,1)S(1)} %all_to_all.21.stats.got) | copy-start | bytes 1474564
  76.3 18.2 %all-to-all-start.3 = ((bf16[8,256,128]{2,1,0:T(8,128)(2,1)}), bf16[8,256,128]{2,1,0:T(8,128)(2,1)S(1)}, u32[]{:S(2)}, u32[]{:S(2)}) async-start(bf16[8,256,128]{2,1,0:T(8,128)(2,1)} %owner_backward.1), calls=%async_computation.3 | async-start | bytes 1048576 | tf_op jit(solution)/shard_map/all_to_all | solution.py:486
  80.0 14.5 %copy-start.4 = (s32[2,8]{1,0:T(2,128)S(1)}, s32[2,8]{1,0:T(2,128)}, u32[]{:S(2)}) copy-start(s32[2,8]{1,0:T(2,128)} %offsets.11) | copy-start | bytes 196
  94.5 1.5 %copy-start.1 = (bf16[3,640,512]{2,1,0:T(8,128)(2,1)S(1)}, bf16[3,640,512]{2,1,0:T(8,128)(2,1)}, u32[]{:S(2)}) copy-start(bf16[3,640,512]{2,1,0:T(8,128)(2,1)} %get-tuple-element.40.grads) | copy-start | bytes 5898244
